TPU v7x, 128 devices: a whole 4x4x4 slice. The times are simulated.
128 devices in a mesh: ctx: 32 (over z, y, x_lo), tp: 4 (over x_hi, core).
Axes of the slice: x: 4 (x_hi: 2, x_lo: 2; x = x_hi * 2 + x_lo), y: 4, z: 4, core: 2. Of those that a mesh axis runs over, the one named last changes fastest.
Arguments:
- tokens: bfloat16 [8192, 4096], P('ctx', 'tp'), may hold values from -7 to 7
- in_weight: bfloat16 [4096, 2, 4096], P(None, None, 'tp'), may hold values from -0.09375 to 0.09375
- short_kernel: float32 [3, 2, 4096], P(None, None, 'tp'), may hold values from -3 to 3
- long_filter: float32 [8192, 4096], P('ctx', 'tp'), may hold values from -3 to 3
- skip_gain: float32 [4096], P('tp'), may hold values from -4 to 4
Outputs:
- block_output: bfloat16 [8192, 4096], P('ctx', 'tp')
All inputs are finite; a program needn't handle non-finite values.
Results may differ from a plain program's by a relative error of at most 0.007.
Values may be sent and summed in bfloat16 or wider, within the bound.
No kernel may reach another device: no remote copies, remote signals or barrier semaphores. Data moves between devices by JAX's collectives and lax.ppermute only.
A program may use at most 128 MiB of HBM per device.

v0:
```python
import math

import jax
import jax.numpy as jnp
from jax import lax
from jax.sharding import PartitionSpec as P

HIGHEST_PRECISION = lax.Precision.HIGHEST


def from_partner(array, axis, stride):
    return lax.ppermute(array, axis, [(i, i ^ 1 << stride) for i in range(lax.axis_size(axis))])


def shifted(block, axis, distance):
    devices = range(lax.axis_size(axis))
    route = [(i - distance, i) for i in devices if i - distance in devices]
    return lax.ppermute(block, axis, route)


def causal_filter(values, rim, kernel):
    tap_count = kernel.shape[0]
    length = values.shape[0]
    extended = jnp.concatenate([rim, values], 0)
    summed = jnp.zeros_like(values)
    for tap_index in range(tap_count):
        offset = tap_count - 1 - tap_index
        summed = summed + kernel[tap_index] * extended[offset : offset + length]
    return summed


def column_convolve(columns, ctx_count, row_count, sign_row):
    seq_length = columns.shape[0]
    width_here = columns.shape[2]
    pad_count = 2 * ctx_count
    full_length = pad_count * row_count
    grid = columns.reshape(ctx_count, row_count, 3, width_here)
    freq_index = jnp.arange(pad_count, dtype=jnp.int32)
    block_index = jnp.arange(ctx_count, dtype=jnp.int32)
    row_index = jnp.arange(row_count, dtype=jnp.int32)
    outer_angle = (
        2.0
        * math.pi
        / pad_count
        * (freq_index[:, None] * block_index[None, :] % pad_count).astype(jnp.float32)
    )
    outer_cos = jnp.cos(outer_angle)
    outer_sin = jnp.sin(outer_angle)
    twist_angle = (
        2.0
        * math.pi
        / full_length
        * (freq_index[:, None] * row_index[None, :] % full_length).astype(jnp.float32)
    )
    twist_cos = jnp.cos(twist_angle)[:, :, None, None]
    twist_sin = jnp.sin(twist_angle)[:, :, None, None]
    inner_angle = (
        2.0
        * math.pi
        / row_count
        * (row_index[:, None] * row_index[None, :] % row_count).astype(jnp.float32)
    )
    inner_cos = jnp.cos(inner_angle)
    inner_sin = jnp.sin(inner_angle)
    first_real = jnp.einsum("kn,nqsc->kqsc", outer_cos, grid, precision=HIGHEST_PRECISION)
    first_imag = -jnp.einsum("kn,nqsc->kqsc", outer_sin, grid, precision=HIGHEST_PRECISION)
    turned_real = first_real * twist_cos + first_imag * twist_sin
    turned_imag = first_imag * twist_cos - first_real * twist_sin
    spec_real = jnp.einsum(
        "qm,kqsc->kmsc", inner_cos, turned_real, precision=HIGHEST_PRECISION
    ) + jnp.einsum("qm,kqsc->kmsc", inner_sin, turned_imag, precision=HIGHEST_PRECISION)
    spec_imag = jnp.einsum(
        "qm,kqsc->kmsc", inner_cos, turned_imag, precision=HIGHEST_PRECISION
    ) - jnp.einsum("qm,kqsc->kmsc", inner_sin, turned_real, precision=HIGHEST_PRECISION)
    filter_real = spec_real[:, :, 2:3]
    signed_imag = spec_imag[:, :, 2:3] * sign_row[:, None]
    data_real = spec_real[:, :, :2]
    data_imag = spec_imag[:, :, :2]
    prod_real = data_real * filter_real - data_imag * signed_imag
    prod_imag = data_real * signed_imag + data_imag * filter_real
    back_real = jnp.einsum(
        "mq,kmsc->kqsc", inner_cos, prod_real, precision=HIGHEST_PRECISION
    ) - jnp.einsum("mq,kmsc->kqsc", inner_sin, prod_imag, precision=HIGHEST_PRECISION)
    back_imag = jnp.einsum(
        "mq,kmsc->kqsc", inner_cos, prod_imag, precision=HIGHEST_PRECISION
    ) + jnp.einsum("mq,kmsc->kqsc", inner_sin, prod_real, precision=HIGHEST_PRECISION)
    untwist_real = back_real * twist_cos - back_imag * twist_sin
    untwist_imag = back_imag * twist_cos + back_real * twist_sin
    result = jnp.einsum(
        "kn,kqsc->nqsc", outer_cos, untwist_real, precision=HIGHEST_PRECISION
    ) - jnp.einsum("kn,kqsc->nqsc", outer_sin, untwist_imag, precision=HIGHEST_PRECISION)
    return (result / full_length).reshape(seq_length, 2, width_here)


def shards(tokens, in_weight, short_kernel, long_filter, skip_gain):
    ctx_count = lax.axis_size("ctx")
    bit_count = ctx_count.bit_length() - 1
    row_count = tokens.shape[0]
    local_width = tokens.shape[1]
    model_width = in_weight.shape[0]
    tap_count = short_kernel.shape[0]
    weights = in_weight.reshape(model_width, 2 * local_width)
    mirrored = tokens
    for bit_index in range(bit_count):
        mirrored = from_partner(mirrored, "ctx", bit_index)
    gathered, mirror_full = (
        lax.all_gather(tokens, "tp", axis=1, tiled=True),
        lax.all_gather(mirrored, "tp", axis=1, tiled=True),
    )
    both_rows = jnp.concatenate([gathered, jnp.flip(mirror_full, (0, 1))], 0)
    projected = jnp.dot(both_rows, weights, preferred_element_type=jnp.float32).astype(jnp.bfloat16)
    projected = projected.reshape(2, row_count, 2, local_width)
    forward_rows = projected[0].astype(jnp.float32)
    reverse_rows = projected[1].astype(jnp.float32)
    edge_rows = projected[:, row_count - tap_count + 1 :]
    rim_below = shifted(edge_rows, "ctx", 1).astype(jnp.float32)
    forward_mix = causal_filter(forward_rows, rim_below[0], short_kernel)
    reverse_mix = causal_filter(reverse_rows, rim_below[1], short_kernel)
    forward_gate = forward_mix[:, 0]
    forward_value = forward_mix[:, 1]
    reverse_gate = reverse_mix[:, 0]
    reverse_value = reverse_mix[:, 1]
    sign_pair = jnp.ones((2,), jnp.float32)
    stacked_rows = jnp.stack([forward_value, reverse_value, long_filter], 1)
    columns = lax.all_to_all(stacked_rows, "ctx", split_axis=2, concat_axis=0, tiled=True)
    column_result = column_convolve(columns, ctx_count, row_count, sign_pair)
    conv_pair = lax.all_to_all(column_result, "ctx", split_axis=0, concat_axis=2, tiled=True)
    forward_out = forward_gate * (conv_pair[:, 0] + skip_gain * forward_value)
    reverse_out = reverse_gate * (conv_pair[:, 1] + skip_gain * reverse_value)
    moved = reverse_out
    for bit_index in range(bit_count):
        moved = from_partner(moved, "ctx", bit_index)
    reverse_back = jnp.flip(moved, 0)
    return (forward_out + reverse_back).astype(jnp.bfloat16)


def solution(mesh):
    placed = (P("ctx", "tp"), P(None, None, "tp"), P(None, None, "tp"), P("ctx", "tp"), P("tp"))
    return jax.shard_map(
        shards, mesh=mesh, in_specs=placed, out_specs=P("ctx", "tp"), check_vma=False
    )
```

profile of v0, /device:TPU:10, one launch (start us, length us, event | category | flops | bytes accessed | tf_op | source)
XLA Modules:
  0.0 549.7 jit_solution(3617481231644144525)
XLA Ops:
  7.1 13.3 %collective-permute-done = bf16[256,1024]{1,0:T(8,128)(2,1)S(1)} collective-permute-done((bf16[256,1024]{1,0:T(8,128)(2,1)}, bf16[256,1024]{1,0:T(8,128)(2,1)S(1)}, u32[]{:S(2)}, u32[]{:S(2)}) %collective-permute-start) | collective-permute-done | bytes 524320 | tf_op jit(solution)/shard_map/ppermute | solution.py:12
  20.9 12.3 %collective-permute-done.1 = bf16[256,1024]{1,0:T(8,128)(2,1)S(1)} collective-permute-done((bf16[256,1024]{1,0:T(8,128)(2,1)S(1)}, bf16[256,1024]{1,0:T(8,128)(2,1)S(1)}, u32[]{:S(2)}, u32[]{:S(2)}) %collective-permute-start.1) | collective-permute-done | bytes 524320 | tf_op jit(solution)/shard_map/ppermute | solution.py:12
  35.7 10.8 %collective-permute-done.2 = bf16[256,1024]{1,0:T(8,128)(2,1)S(1)} collective-permute-done((bf16[256,1024]{1,0:T(8,128)(2,1)S(1)}, bf16[256,1024]{1,0:T(8,128)(2,1)S(1)}, u32[]{:S(2)}, u32[]{:S(2)}) %collective-permute-start.2) | collective-permute-done | bytes 524320 | tf_op jit(solution)/shard_map/ppermute | solution.py:12
  48.5 9.2 %collective-permute-done.3 = bf16[256,1024]{1,0:T(8,128)(2,1)S(1)} collective-permute-done((bf16[256,1024]{1,0:T(8,128)(2,1)S(1)}, bf16[256,1024]{1,0:T(8,128)(2,1)S(1)}, u32[]{:S(2)}, u32[]{:S(2)}) %collective-permute-start.3) | collective-permute-done | bytes 524320 | tf_op jit(solution)/shard_map/ppermute | solution.py:12
  63.0 9.2 %collective-permute-done.4 = bf16[256,1024]{1,0:T(8,128)(2,1)S(1)} collective-permute-done((bf16[256,1024]{1,0:T(8,128)(2,1)S(1)}, bf16[256,1024]{1,0:T(8,128)(2,1)S(1)}, u32[]{:S(2)}, u32[]{:S(2)}) %collective-permute-start.4) | collective-permute-done | bytes 524320 | tf_op jit(solution)/shard_map/ppermute | solution.py:12
  76.3 17.1 %copy.77 = bf16[512,8,2,1024]{3,1,2,0:T(8,128)(2,1)} copy(bf16[512,8,2,1024]{3,2,1,0:T(2,128)(2,1)} %bitcast.116) | data formatting | bytes 33554432
  93.5 6.1 %all-gather.5.cloned.1.call-done = bf16[256,4096]{1,0:T(8,128)(2,1)} async-done(((bf16[256,1024]{1,0:T(8,128)(2,1)}), bf16[256,4096]{1,0:T(8,128)(2,1)}) %all-gather.5.cloned.1.call-update) | async-done | bytes 2097168 | tf_op jit(solution)/shard_map/all_gather | solution.py:108
  99.6 32.1 %rev.8 = bf16[256,4096]{1,0:T(8,128)(2,1)} reverse(bf16[256,4096]{1,0:T(8,128)(2,1)} %all-gather.5.cloned.1.call-done), dimensions={0,1} | reverse | bytes 4194304 | tf_op jit(solution)/shard_map/jit(_flip)/rev | solution.py:110
  131.8 13.6 %fusion.20 = bf16[512,2048]{1,0:T(8,128)(2,1)S(1)} fusion(bf16[4096,2048]{1,0:T(8,128)(2,1)} %bitcast.117, bf16[256,4096]{1,0:T(8,128)(2,1)} %rev.8, bf16[256,4096]{1,0:T(8,128)(2,1)} %all-gather.3.cloned.1.call-done), kind=kOutput, calls=%fused_computation.33 | convolution fusion | flops 8599371776 | bytes 23068672 | tf_op jit(solution)/shard_map/dot_general | solution.py:111
  173.8 8.6 %all-to-all-start = ((f32[256,3,1024]{0,1,2:T(4,128)}), f32[256,3,1024]{0,1,2:T(4,128)}, u32[]{:S(2)}, u32[]{:S(2)}) async-start(f32[256,3,1024]{0,1,2:T(4,128)} %copy.53), calls=%async_computation | async-start | bytes 8388608 | tf_op jit(solution)/shard_map/all_to_all | solution.py:125
  182.7 58.1 %all-to-all-done = f32[256,3,1024]{0,1,2:T(4,128)} async-done(((f32[256,3,1024]{0,1,2:T(4,128)}), f32[256,3,1024]{0,1,2:T(4,128)}, u32[]{:S(2)}, u32[]{:S(2)}) %all-to-all-start) | async-done | bytes 3145760 | tf_op jit(solution)/shard_map/all_to_all | solution.py:125
  240.8 9.3 %fusion.16 = f32[64,256,3,32]{1,0,3,2:T(8,128)S(1)} fusion(f32[256,3,32,32]{0,1,3,2:T(4,128)} %bitcast.10), kind=kOutput, calls=%fused_computation.29 | convolution fusion | flops 604008448 | bytes 9437184 | tf_op jit(solution)/shard_map/kn,nqsc->kqsc/dot_general | solution.py:66
  250.1 10.9 %multiply_add_fusion = (f32[64,256,3,32]{1,0,3,2:T(8,128)S(1)}, f32[64,256,3,32]{1,0,3,2:T(8,128)S(1)}) fusion(f32[64,256,3,32]{1,0,3,2:T(8,128)S(1)} %fusion.16, f32[64,256]{1,0:T(8,128)S(1)} %get-tuple-element.18, f32[64,256]{1,0:T(8,128)S(1)} %get-tuple-element.19, f32[256,3,32,32]{0,1,3,2:T(4,128)} %bitcast.10), kind=kOutput, calls=%fused_computation.3 | convolution fusion | flops 615018496 | bytes 22151168 | tf_op jit(solution)/shard_map/kn,nqsc->kqsc/dot_general | solution.py:65
  261.1 9.7 %fusion = f32[64,3,32,256]{3,2,1,0:T(8,128)S(1)} fusion(f32[64,256,3,32]{1,0,3,2:T(8,128)S(1)} %get-tuple-element.6), kind=kOutput, calls=%fused_computation.4 | convolution fusion | flops 4832755712 | bytes 12582912 | tf_op jit(solution)/shard_map/qm,kqsc->kmsc/dot_general | solution.py:72
  270.8 11.3 %fusion.2 = f32[64,3,32,256]{3,2,1,0:T(8,128)} fusion(f32[64,256,3,32]{1,0,3,2:T(8,128)S(1)} %get-tuple-element.6), kind=kOutput, calls=%fused_computation.6 | convolution fusion | flops 4832755712 | bytes 12582912 | tf_op jit(solution)/shard_map/qm,kqsc->kmsc/dot_general | solution.py:71
  282.1 9.8 %subtract_bitcast_fusion = f32[64,256,3,32]{1,3,2,0:T(8,128)S(1)} fusion(f32[64,3,32,256]{3,2,1,0:T(8,128)S(1)} %fusion, f32[64,256,3,32]{1,0,3,2:T(8,128)S(1)} %get-tuple-element.5), kind=kOutput, calls=%fused_computation | convolution fusion | flops 4834328576 | bytes 18874368 | tf_op jit(solution)/shard_map/qm,kqsc->kmsc/dot_general | solution.py:74
  291.9 10.0 %add_bitcast_fusion = f32[64,256,3,32]{1,3,2,0:T(8,128)S(1)} fusion(f32[64,3,32,256]{3,2,1,0:T(8,128)S(1)} %copy-done, f32[64,256,3,32]{1,0,3,2:T(8,128)S(1)} %get-tuple-element.5), kind=kOutput, calls=%fused_computation.1 | convolution fusion | flops 4834328576 | bytes 18874368 | tf_op jit(solution)/shard_map/qm,kqsc->kmsc/dot_general | solution.py:69
  307.2 6.5 %fusion.56 = f32[64,2,32,256]{3,2,1,0:T(8,128)} fusion(f32[64,256,3,32]{1,3,2,0:T(8,128)S(1)} %subtract_bitcast_fusion, f32[64,256,3,32]{1,3,2,0:T(8,128)S(1)} %add_bitcast_fusion, f32[64,256,32]{1,2,0:T(8,128)S(1)} %slice_bitcast_fusion, f32[64,256,32]{1,2,0:T(8,128)S(1)} %slice_bitcast_fusion.1), kind=kOutput, calls=%fused_computation.81 | convolution fusion | flops 3225288704 | bytes 16777216 | tf_op jit(solution)/shard_map/mq,kmsc->kqsc/dot_general | solution.py:81
  313.6 6.6 %convolution_add_fusion = f32[64,2,32,256]{3,2,1,0:T(8,128)} fusion(f32[64,2,32,256]{3,2,1,0:T(8,128)S(1)} %fusion.54, f32[64,256,3,32]{1,3,2,0:T(8,128)S(1)} %subtract_bitcast_fusion, f32[64,256,3,32]{1,3,2,0:T(8,128)S(1)} %add_bitcast_fusion, f32[64,256,32]{1,2,0:T(8,128)S(1)} %slice_bitcast_fusion, f32[64,256,32]{1,2,0:T(8,128)S(1)} %slice_bitcast_fusion.1), kind=kOutput, calls=%fused_computation.36 | convolution fusion | flops 3226337280 | bytes 20971520 | tf_op jit(solution)/shard_map/mq,kmsc->kqsc/dot_general | solution.py:86
  320.2 10.9 %subtract_bitcast_fusion.1 = (f32[64,256,2,32]{1,3,2,0:T(8,128)}, f32[64,256,2,32]{1,3,2,0:T(8,128)}) fusion(f32[64,2,32,256]{3,2,1,0:T(8,128)} %convolution_add_fusion, f32[64,256]{1,0:T(8,128)S(1)} %get-tuple-element.18, f32[64,256]{1,0:T(8,128)S(1)} %get-tuple-element.19, f32[64,2,32,256]{3,2,1,0:T(8,128)} %fusion.56, ...), kind=kOutput, calls=%fused_computation.21 | convolution fusion | flops 3232628736 | bytes 29491200 | tf_op jit(solution)/shard_map/mq,kmsc->kqsc/dot_general | solution.py:83
  331.1 7.0 %fusion.12 = f32[32,256,2,32]{1,0,3,2:T(8,128)S(1)} fusion(f32[64,256,2,32]{1,3,2,0:T(8,128)} %get-tuple-element.8), kind=kOutput, calls=%fused_computation.16 | convolution fusion | flops 402681856 | bytes 6291456 | tf_op jit(solution)/shard_map/kn,kqsc->nqsc/dot_general | solution.py:91
  342.8 6.0 %copy.72 = f32[32,256,2,32]{3,2,1,0:T(2,128)} copy(f32[32,256,2,32]{1,0,3,2:T(8,128)S(1)} %subtract_multiply_fusion) | data formatting | bytes 4194304 | tf_op jit(solution)/shard_map/reshape | solution.py:92
  348.8 10.3 %reshape.65 = f32[32,1,16384]{2,1,0:T(1,128)S(1)} reshape(f32[8192,2,32]{2,1,0:T(2,128)} %bitcast.114) | data formatting | bytes 4194304
  359.1 31.9 %all_to_all.33 = f32[32,1,16384]{2,1,0:T(1,128)} all-to-all(f32[32,1,16384]{2,1,0:T(1,128)S(1)} %reshape.65), channel_id=1, replica_groups=mesh['ctx'=32,'tp'=4] {'ctx'}, dimensions={0} | all-to-all | bytes 4194304 | tf_op jit(solution)/shard_map/all_to_all | solution.py:127
  391.6 7.4 %reduce = f32[32,16384]{1,0:T(8,128)S(1)} reduce(f32[32,1,16384]{2,1,0:T(1,128)} %all_to_all.33, f32[]{:T(128)} %broadcast.132), dimensions={1}, to_apply=%all_to_all.27.reduce_sub_computation | reduce | bytes 4194308 | tf_op jit(solution)/shard_map/all_to_all | solution.py:127
  399.0 8.5 %reshape.66 = f32[8192,2,32]{2,1,0:T(2,128)} reshape(f32[32,16384]{1,0:T(8,128)S(1)} %reduce) | data formatting | bytes 4194304
  407.5 11.0 %copy.74 = f32[32,256,2,32]{1,3,0,2:T(8,128)} copy(f32[32,256,2,32]{3,2,1,0:T(2,128)} %bitcast.115) | data formatting | bytes 4194304 | tf_op jit(solution)/shard_map/all_to_all | solution.py:127
  421.9 20.0 %collective-permute-done.6 = f32[256,1024]{0,1:T(8,128)S(1)} collective-permute-done((f32[256,1024]{0,1:T(8,128)S(1)}, f32[256,1024]{0,1:T(8,128)S(1)}, u32[]{:S(2)}, u32[]{:S(2)}) %collective-permute-start.6) | collective-permute-done | bytes 1048608 | tf_op jit(solution)/shard_map/ppermute | solution.py:12
  443.2 19.8 %collective-permute-done.7 = f32[256,1024]{0,1:T(8,128)S(1)} collective-permute-done((f32[256,1024]{0,1:T(8,128)S(1)}, f32[256,1024]{0,1:T(8,128)S(1)}, u32[]{:S(2)}, u32[]{:S(2)}) %collective-permute-start.7) | collective-permute-done | bytes 1048608 | tf_op jit(solution)/shard_map/ppermute | solution.py:12
  468.8 22.2 %collective-permute-done.8 = f32[256,1024]{0,1:T(8,128)S(1)} collective-permute-done((f32[256,1024]{0,1:T(8,128)S(1)}, f32[256,1024]{0,1:T(8,128)S(1)}, u32[]{:S(2)}, u32[]{:S(2)}) %collective-permute-start.8) | collective-permute-done | bytes 1048608 | tf_op jit(solution)/shard_map/ppermute | solution.py:12
  491.0 24.5 %collective-permute-done.9 = f32[256,1024]{0,1:T(8,128)S(1)} collective-permute-done((f32[256,1024]{0,1:T(8,128)S(1)}, f32[256,1024]{0,1:T(8,128)S(1)}, u32[]{:S(2)}, u32[]{:S(2)}) %collective-permute-start.9) | collective-permute-done | bytes 1048608 | tf_op jit(solution)/shard_map/ppermute | solution.py:12
  515.5 22.6 %collective-permute-done.10 = f32[256,1024]{0,1:T(8,128)S(1)} collective-permute-done((f32[256,1024]{0,1:T(8,128)S(1)}, f32[256,1024]{0,1:T(8,128)S(1)}, u32[]{:S(2)}, u32[]{:S(2)}) %collective-permute-start.10) | collective-permute-done | bytes 1048608 | tf_op jit(solution)/shard_map/ppermute | solution.py:12
  (66 shorter events, 68.9 us)
Async XLA Ops:
  6.5 93.1 %all-gather.5.cloned.1.call-start = ((), (), s32[]{:S(2)}) async-start(), calls=%async_computation.3 | async-start | bytes 2621440 | tf_op jit(solution)/shard_map/all_gather | solution.py:108
  6.5 13.9 %collective-permute-start = (bf16[256,1024]{1,0:T(8,128)(2,1)}, bf16[256,1024]{1,0:T(8,128)(2,1)S(1)}, u32[]{:S(2)}, u32[]{:S(2)}) collective-permute-start(bf16[256,1024]{1,0:T(8,128)(2,1)} %param.5), channel_id=1, source_target_pairs={{0,4},{4,0},{8,12},{12,8},{16,20},{20,16},{24,28},{28,24},{32,36},... | collective-permute-start | bytes 1572872 | tf_op jit(solution)/shard_map/ppermute | solution.py:12
  20.4 12.8 %collective-permute-start.1 = (bf16[256,1024]{1,0:T(8,128)(2,1)S(1)}, bf16[256,1024]{1,0:T(8,128)(2,1)S(1)}, u32[]{:S(2)}, u32[]{:S(2)}) collective-permute-start(bf16[256,1024]{1,0:T(8,128)(2,1)S(1)} %collective-permute-done), channel_id=1, source_target_pairs={{0,8},{4,12},{8,0},{12,4},{16,24},{20,28},{24,16},{28,20},{32,40},... | collective-permute-start | bytes 1572872 | tf_op jit(solution)/shard_map/ppermute | solution.py:12
  33.2 13.4 %collective-permute-start.2 = (bf16[256,1024]{1,0:T(8,128)(2,1)S(1)}, bf16[256,1024]{1,0:T(8,128)(2,1)S(1)}, u32[]{:S(2)}, u32[]{:S(2)}) collective-permute-start(bf16[256,1024]{1,0:T(8,128)(2,1)S(1)} %collective-permute-done.1), channel_id=1, source_target_pairs={{0,16},{4,20},{8,24},{12,28},{16,0},{20,4},{24,8},{28,12},{32,48},... | collective-permute-start | bytes 1572872 | tf_op jit(solution)/shard_map/ppermute | solution.py:12
  46.6 11.1 %collective-permute-start.3 = (bf16[256,1024]{1,0:T(8,128)(2,1)S(1)}, bf16[256,1024]{1,0:T(8,128)(2,1)S(1)}, u32[]{:S(2)}, u32[]{:S(2)}) collective-permute-start(bf16[256,1024]{1,0:T(8,128)(2,1)S(1)} %collective-permute-done.2), channel_id=1, source_target_pairs={{0,32},{4,36},{8,40},{12,44},{16,48},{20,52},{24,56},{28,60},{32,0... | collective-permute-start | bytes 1572872 | tf_op jit(solution)/shard_map/ppermute | solution.py:12
  57.7 14.5 %collective-permute-start.4 = (bf16[256,1024]{1,0:T(8,128)(2,1)S(1)}, bf16[256,1024]{1,0:T(8,128)(2,1)S(1)}, u32[]{:S(2)}, u32[]{:S(2)}) collective-permute-start(bf16[256,1024]{1,0:T(8,128)(2,1)S(1)} %collective-permute-done.3), channel_id=1, source_target_pairs={{0,64},{4,68},{8,72},{12,76},{16,80},{20,84},{24,88},{28,92},{32,9... | collective-permute-start | bytes 1572872 | tf_op jit(solution)/shard_map/ppermute | solution.py:12
  72.2 0.8 copy-start.9
  73.1 58.7 %all-gather.3.cloned.1.call-start = ((), (), s32[]{:S(2)}) async-start(), calls=%async_computation.2 | async-start | bytes 2621440 | tf_op jit(solution)/shard_map/all_gather | solution.py:107
  76.3 17.2 %copy-start.10 = (f32[3,2,1024]{2,1,0:T(2,128)S(1)}, f32[3,2,1024]{2,1,0:T(2,128)}, u32[]{:S(2)}) copy-start(f32[3,2,1024]{2,1,0:T(2,128)} %param.7) | copy-start | bytes 73732
  148.9 12.2 %collective-permute-start.5 = (bf16[2,2,2,1024]{3,2,1,0:T(2,128)(2,1)S(1)}, bf16[2,2,2,1024]{3,2,1,0:T(2,128)(2,1)S(1)}, u32[]{:S(2)}, u32[]{:S(2)}) collective-permute-start(bf16[2,2,2,1024]{3,2,1,0:T(2,128)(2,1)S(1)} %slice.94), channel_id=1, source_target_pairs={{0,4},{4,8},{8,12},{12,16},{16,20},{20,24},{24,28},{28,32},{32,36}... | collective-permute-start | bytes 49160 | tf_op jit(solution)/shard_map/ppermute | solution.py:18
  156.3 3.1 copy-start.5
  161.1 1.6 copy-start.6
  161.7 1.8 copy-start.7
  167.4 2.3 copy-start.2
  167.4 2.3 copy-start.4
  167.4 2.0 copy-start.8
  173.8 67.0 %all-to-all-start = ((f32[256,3,1024]{0,1,2:T(4,128)}), f32[256,3,1024]{0,1,2:T(4,128)}, u32[]{:S(2)}, u32[]{:S(2)}) async-start(f32[256,3,1024]{0,1,2:T(4,128)} %copy.53), calls=%async_computation | async-start | bytes 8388608 | tf_op jit(solution)/shard_map/all_to_all | solution.py:125
  282.1 9.8 %copy-start = (f32[64,3,32,256]{3,2,1,0:T(8,128)S(1)}, f32[64,3,32,256]{3,2,1,0:T(8,128)}, u32[]{:S(2)}) copy-start(f32[64,3,32,256]{3,2,1,0:T(8,128)} %fusion.2) | copy-start | bytes 18874372
  331.1 7.0 %copy-start.1 = (f32[64,256,2,32]{1,3,2,0:T(8,128)S(1)}, f32[64,256,2,32]{1,3,2,0:T(8,128)}, u32[]{:S(2)}) copy-start(f32[64,256,2,32]{1,3,2,0:T(8,128)} %get-tuple-element.7) | copy-start | bytes 12582916
  407.4 11.1 %copy-start.3 = (f32[256,2,1024]{0,2,1:T(8,128)S(1)}, f32[256,2,1024]{0,2,1:T(8,128)}, u32[]{:S(2)}) copy-start(f32[256,2,1024]{0,2,1:T(8,128)} %copy-done.2) | copy-start | bytes 6291460
  407.4 11.1 %copy-start.11 = (f32[1024]{0:T(1024)S(1)}, f32[1024]{0:T(1024)}, u32[]{:S(2)}) copy-start(f32[1024]{0:T(1024)} %param.9) | copy-start | bytes 12292
  419.9 22.0 %collective-permute-start.6 = (f32[256,1024]{0,1:T(8,128)S(1)}, f32[256,1024]{0,1:T(8,128)S(1)}, u32[]{:S(2)}, u32[]{:S(2)}) collective-permute-start(f32[256,1024]{0,1:T(8,128)S(1)} %fusion.42), channel_id=1, source_target_pairs={{0,4},{4,0},{8,12},{12,8},{16,20},{20,16},{24,28},{28,24},{32,36},... | collective-permute-start | bytes 3145736 | tf_op jit(solution)/shard_map/ppermute | solution.py:12
  442.0 21.0 %collective-permute-start.7 = (f32[256,1024]{0,1:T(8,128)S(1)}, f32[256,1024]{0,1:T(8,128)S(1)}, u32[]{:S(2)}, u32[]{:S(2)}) collective-permute-start(f32[256,1024]{0,1:T(8,128)S(1)} %collective-permute-done.6), channel_id=1, source_target_pairs={{0,8},{4,12},{8,0},{12,4},{16,24},{20,28},{24,16},{28,20},{32,40},... | collective-permute-start | bytes 3145736 | tf_op jit(solution)/shard_map/ppermute | solution.py:12
  463.0 28.0 %collective-permute-start.8 = (f32[256,1024]{0,1:T(8,128)S(1)}, f32[256,1024]{0,1:T(8,128)S(1)}, u32[]{:S(2)}, u32[]{:S(2)}) collective-permute-start(f32[256,1024]{0,1:T(8,128)S(1)} %collective-permute-done.7), channel_id=1, source_target_pairs={{0,16},{4,20},{8,24},{12,28},{16,0},{20,4},{24,8},{28,12},{32,48},... | collective-permute-start | bytes 3145736 | tf_op jit(solution)/shard_map/ppermute | solution.py:12
  491.0 24.5 %collective-permute-start.9 = (f32[256,1024]{0,1:T(8,128)S(1)}, f32[256,1024]{0,1:T(8,128)S(1)}, u32[]{:S(2)}, u32[]{:S(2)}) collective-permute-start(f32[256,1024]{0,1:T(8,128)S(1)} %collective-permute-done.8), channel_id=1, source_target_pairs={{0,32},{4,36},{8,40},{12,44},{16,48},{20,52},{24,56},{28,60},{32,0... | collective-permute-start | bytes 3145736 | tf_op jit(solution)/shard_map/ppermute | solution.py:12
  515.5 22.7 %collective-permute-start.10 = (f32[256,1024]{0,1:T(8,128)S(1)}, f32[256,1024]{0,1:T(8,128)S(1)}, u32[]{:S(2)}, u32[]{:S(2)}) collective-permute-start(f32[256,1024]{0,1:T(8,128)S(1)} %collective-permute-done.9), channel_id=1, source_target_pairs={{0,64},{4,68},{8,72},{12,76},{16,80},{20,84},{24,88},{28,92},{32,9... | collective-permute-start | bytes 3145736 | tf_op jit(solution)/shard_map/ppermute | solution.py:12
Sparse Core Ops, SparseCore 0:
  73.2 26.4 all-gather.4
  101.3 26.0 all-gather.2
where the time goes:
time: 559 us; the launch traced here: 550 us
  waiting for transfers between devices  229 us (41%)
  matrix products  115 us (21%)
  local copies, waits for them, and re-layouts  109 us (19%)
  starting transfers between devices  33.3 us (6%)
  blocking collectives  31.9 us (6%)
  other arithmetic  17.9 us (3%)
  between operations  13.9 us (2%)
    ppermute x10, waiting for transfers between devices, from_partner(): lax.ppermute(array, axis, [(i, i ^ 1 << stride) for i in range(lax.axis_s...  164 us
    all_to_all x1, waiting for transfers between devices, shards(): lax.all_to_all(stacked_rows, 'ctx', split_axis=2, concat_axis=0, tiled=True)  58.1 us
    unnamed x28, local copies, waits for them, and re-layouts  42.7 us
    rev x1, local copies, waits for them, and re-layouts, shards(): both_rows = jnp.concatenate([gathered, jnp.flip(mirror_full, (0, 1))], 0)  32.1 us
    all_to_all x1, blocking collectives, shards(): lax.all_to_all(column_result, 'ctx', split_axis=0, concat_axis=2, tiled=T...  31.9 us
    ppermute x10, starting transfers between devices, from_partner(): lax.ppermute(array, axis, [(i, i ^ 1 << stride) for i in range(lax.axis_s...  19.8 us
    dot_general x1, matrix products, shards(): jnp.dot(both_rows, weights, preferred_element_type=jnp.float32)  13.6 us
    all_to_all x2, local copies, waits for them, and re-layouts, shards(): lax.all_to_all(column_result, 'ctx', split_axis=0, concat_axis=2, tiled=T...  11.6 us
  transfers between devices with their start and end apart: 14, of which 12 were waited for; matrix products, arithmetic and copies ran while one was open for 11% of the time, Pallas kernels for 0%

commit v1 on v0

v1 whole, which is shorter than its diff:
```python
import functools
import math

import jax
import jax.numpy as jnp
import numpy as np
from jax import lax
from jax.experimental import pallas as pl
from jax.experimental.pallas import tpu as pltpu
from jax.sharding import PartitionSpec as P

BF16 = jnp.bfloat16
F32 = jnp.float32
GROUP = 16
VMEM_BYTES = 56 * 1024 * 1024


def params():
    return pltpu.CompilerParams(vmem_limit_bytes=VMEM_BYTES)


def tables(blocks, rows):
    length = blocks * rows
    j1 = np.arange(blocks)
    n = np.arange(blocks)
    q = np.arange(rows)
    outer = 2 * math.pi * ((4 * j1[:, None] + 1) * n[None, :] % (4 * blocks)) / (4 * blocks)
    eye = np.eye(GROUP)
    forward = np.concatenate([np.kron(np.cos(outer), eye), np.kron(-np.sin(outer), eye)], 0)
    backward = np.concatenate([np.kron(np.cos(outer).T, eye), np.kron(-np.sin(outer).T, eye)], 1)
    turn = 2 * math.pi * ((4 * j1[:, None] + 1) * q[None, :]) / (4 * length)
    turn = np.repeat(turn, GROUP, 0)
    inner = 2 * math.pi * (q[:, None] * q[None, :] % rows) / rows
    c, s = np.cos(inner), np.sin(inner)
    inner_forward = np.block([[c, -s], [s, c]])
    inner_backward = np.block([[c, s], [-s, c]]) / length
    small = lambda a: jnp.asarray(a.astype(np.float32)).astype(BF16)
    return dict(
        forward=small(forward),
        backward=small(backward),
        turn_cos=jnp.asarray(np.cos(turn), F32),
        turn_sin=jnp.asarray(np.sin(turn), F32),
        inner_forward=small(inner_forward),
        inner_backward=small(inner_backward),
    )


def mm(a, b):
    return jnp.dot(a, b, preferred_element_type=F32)


def spectrum(x, forward, turn_cos, turn_sin, inner):
    half = forward.shape[0] // 2
    mixed = mm(forward, x)
    real, imag = mixed[:half], mixed[half:]
    turned_real = (real * turn_cos + imag * turn_sin).astype(BF16)
    turned_imag = (imag * turn_cos - real * turn_sin).astype(BF16)
    return mm(jnp.concatenate([turned_real, turned_imag], 1), inner)


def filter_prep_kernel(filter_ref, halo_ref, taps_ref, skip_ref, out_ref):
    rows, width = filter_ref.shape
    row = lax.broadcasted_iota(jnp.int32, (rows, width), 0)
    first = filter_ref[...] + jnp.where(row == 0, skip_ref[...], 0.0)
    total = taps_ref[0:1] * first
    for tap in (1, 2):
        moved = pltpu.roll(first, tap, 0)
        for edge in range(tap):
            moved = jnp.where(row == edge, halo_ref[8 - tap + edge : 9 - tap + edge], moved)
        total = total + taps_ref[tap : tap + 1] * moved
    out_ref[...] = total.T.astype(BF16)


def filter_prep(long_filter, halo, taps, skip, block=256):
    rows, width = long_filter.shape
    block = min(block, width)
    return pl.pallas_call(
        filter_prep_kernel,
        grid=(width // block,),
        in_specs=[
            pl.BlockSpec((rows, block), lambda i: (0, i)),
            pl.BlockSpec((8, block), lambda i: (0, i)),
            pl.BlockSpec((3, block), lambda i: (0, i)),
            pl.BlockSpec((1, block), lambda i: (0, i)),
        ],
        out_specs=pl.BlockSpec((block, rows), lambda i: (i, 0)),
        out_shape=jax.ShapeDtypeStruct((width, rows), BF16),
        compiler_params=params(),
        cost_estimate=pl.CostEstimate(flops=10 * rows * width, bytes_accessed=6 * rows * width, transcendentals=0),
        name="filter_prep",
    )(long_filter, halo, taps, skip)


def filter_spectrum_kernel(x_ref, forward_ref, cos_ref, sin_ref, inner_ref, out_ref):
    blocks, width, rows = x_ref.shape
    for g in range(width // GROUP):
        x = x_ref[:, g * GROUP : (g + 1) * GROUP, :].reshape(blocks * GROUP, rows)
        out_ref[g] = spectrum(x, forward_ref[...], cos_ref[...], sin_ref[...], inner_ref[...])


def filter_spectrum(x, t):
    blocks, width, rows = x.shape
    groups = width // GROUP
    return pl.pallas_call(
        filter_spectrum_kernel,
        out_shape=jax.ShapeDtypeStruct((groups, blocks * GROUP, 2 * rows), F32),
        compiler_params=params(),
        cost_estimate=pl.CostEstimate(flops=2 * 10**9, bytes_accessed=6 * 2**20, transcendentals=0),
        name="filter_spectrum",
    )(x, t["forward"], t["turn_cos"], t["turn_sin"], t["inner_forward"])


def convolve_kernel(
    x_ref, spec_ref, forward_ref, backward_ref, cos_ref, sin_ref, inner_ref, inner_back_ref, out_ref
):
    blocks, width, rows = x_ref.shape
    groups = width // GROUP
    turn_cos, turn_sin = cos_ref[...], sin_ref[...]
    for g in range(groups):
        x = x_ref[:, g * GROUP : (g + 1) * GROUP, :].reshape(blocks * GROUP, rows)
        data = spectrum(x, forward_ref[...], turn_cos, turn_sin, inner_ref[...])
        real, imag = data[:, :rows], data[:, rows:]
        filt = spec_ref.at[g % (groups // 2)]
        filter_real, filter_imag = filt[:, :rows], filt[:, rows:]
        if g >= groups // 2:
            filter_imag = -filter_imag
        prod_real = (real * filter_real - imag * filter_imag).astype(BF16)
        prod_imag = (real * filter_imag + imag * filter_real).astype(BF16)
        back = mm(jnp.concatenate([prod_real, prod_imag], 1), inner_back_ref[...])
        real, imag = back[:, :rows], back[:, rows:]
        turned_real = (real * turn_cos - imag * turn_sin).astype(BF16)
        turned_imag = (imag * turn_cos + real * turn_sin).astype(BF16)
        out = mm(backward_ref[...], jnp.concatenate([turned_real, turned_imag], 0))
        out_ref[:, g * GROUP : (g + 1) * GROUP, :] = out.astype(BF16).reshape(blocks, GROUP, rows)


def convolve(x, spec, t):
    return pl.pallas_call(
        convolve_kernel,
        out_shape=jax.ShapeDtypeStruct(x.shape, BF16),
        compiler_params=params(),
        cost_estimate=pl.CostEstimate(flops=8 * 10**9, bytes_accessed=10 * 2**20, transcendentals=0),
        name="convolve",
    )(
        x, spec, t["forward"], t["backward"], t["turn_cos"], t["turn_sin"], t["inner_forward"], t["inner_backward"]
    )


def flipped(x):
    width = x.shape[1]
    block = min(256, width)
    count = width // block
    total = lax.broadcasted_iota(jnp.int32, (block, block), 0) + lax.broadcasted_iota(jnp.int32, (block, block), 1)
    swap = jnp.where(total == block - 1, 1.0, 0.0).astype(BF16)
    parts = [mm(x[:, (count - 1 - b) * block : (count - b) * block], swap).astype(BF16) for b in range(count)]
    return jnp.concatenate(parts, 1)


def project_kernel(transposed, order_ref, own_ref, sib_ref, far_ref, farsib_ref, w_ref, out_ref, left_ref):
    rows, depth = own_ref.shape
    block = w_ref.shape[1]
    refs = (own_ref, sib_ref, far_ref, farsib_ref)

    @pl.when(pl.program_id(0) == 0)
    def _():
        for k in range(4):
            left_ref[k, :rows] = refs[k][...]
            left_ref[k, rows:] = flipped(refs[3 - k][...])

    total = jnp.zeros((2 * rows, block), F32)
    for k in range(4):
        at = pl.multiple_of(order_ref[k] * depth, depth)
        total = total + mm(left_ref[k], w_ref[pl.ds(at, depth), :])
    if transposed:
        turned = total.T.astype(BF16)
        width = out_ref.shape[1] // 2
        for d in range(out_ref.shape[0]):
            out_ref[d, :width] = turned[d * width : (d + 1) * width, :rows]
            out_ref[d, width:] = turned[d * width : (d + 1) * width, rows:]
    else:
        out_ref[...] = total.astype(BF16)


def project(order, parts, w, ctx_count, transposed, block=256):
    rows, depth = parts[0].shape
    model, width = w.shape
    block = min(block, width)
    slice_width = width // ctx_count
    if transposed:
        out_shape = (ctx_count, 2 * slice_width, rows)
        out_spec = pl.BlockSpec((block // slice_width, 2 * slice_width, rows), lambda i, o: (i, 0, 0))
    else:
        out_shape = (2 * rows, width)
        out_spec = pl.BlockSpec((2 * rows, block), lambda i, o: (0, i))
    whole = pl.BlockSpec((rows, depth), lambda i, o: (0, 0))
    return pl.pallas_call(
        functools.partial(project_kernel, transposed),
        grid_spec=pltpu.PrefetchScalarGridSpec(
            num_scalar_prefetch=1,
            grid=(width // block,),
            in_specs=[whole] * 4 + [pl.BlockSpec((model, block), lambda i, o: (0, i))],
            out_specs=out_spec,
            scratch_shapes=[pltpu.VMEM((4, 2 * rows, depth), BF16)],
        ),
        out_shape=jax.ShapeDtypeStruct(out_shape, BF16),
        compiler_params=params(),
        cost_estimate=pl.CostEstimate(
            flops=4 * rows * model * width, bytes_accessed=2 * model * width, transcendentals=0
        ),
        name="project_values" if transposed else "project_gates",
    )(order, *parts, w)


def finish_kernel(gates_ref, below_ref, above_ref, taps_ref, conv_ref, out_ref):
    rows, block = out_ref.shape
    half = conv_ref.shape[1] // 2
    row = lax.broadcasted_iota(jnp.int32, (rows, block), 0)
    forward = gates_ref[:rows].astype(F32)
    reverse = gates_ref[rows:].astype(F32)
    below = below_ref[...].astype(F32)
    above = above_ref[...].astype(F32)
    tail = below.shape[0]
    gate_forward = taps_ref[0:1] * forward
    gate_reverse = taps_ref[0:1] * reverse
    for tap in (1, 2):
        moved = pltpu.roll(forward, tap, 0)
        other = pltpu.roll(reverse, rows - tap, 0)
        for edge in range(tap):
            moved = jnp.where(row == edge, below[tail - tap + edge : tail - tap + edge + 1], moved)
            other = jnp.where(row == rows - tap + edge, above[edge : edge + 1], other)
        gate_forward = gate_forward + taps_ref[tap : tap + 1] * moved
        gate_reverse = gate_reverse + taps_ref[tap : tap + 1] * other
    conv_forward = conv_ref[:, :half].reshape(block, rows).astype(F32).T
    conv_reverse = conv_ref[:, half:].reshape(block, rows).astype(F32).T
    out_ref[...] = (gate_forward * conv_forward + gate_reverse * conv_reverse).astype(BF16)


def finish(gates, below, above, taps, conv, block=256):
    rows, width = gates.shape[0] // 2, gates.shape[1]
    block = min(block, width)
    pair = conv.shape[1]
    return pl.pallas_call(
        finish_kernel,
        grid=(width // block,),
        in_specs=[
            pl.BlockSpec((2 * rows, block), lambda i: (0, i)),
            pl.BlockSpec((below.shape[0], block), lambda i: (0, i)),
            pl.BlockSpec((above.shape[0], block), lambda i: (0, i)),
            pl.BlockSpec((3, block), lambda i: (0, i)),
            pl.BlockSpec((2 * block // pair, pair, rows), lambda i: (i, 0, 0)),
        ],
        out_specs=pl.BlockSpec((rows, block), lambda i: (0, i)),
        out_shape=jax.ShapeDtypeStruct((rows, width), BF16),
        compiler_params=params(),
        cost_estimate=pl.CostEstimate(flops=16 * rows * width, bytes_accessed=12 * rows * width, transcendentals=0),
        name="finish",
    )(gates, below, above, taps, conv)


def shards(tokens, in_weight, short_kernel, long_filter, skip_gain):
    ctx_count = lax.axis_size("ctx")
    tp_count = lax.axis_size("tp")
    ctx = lax.axis_index("ctx")
    tp = lax.axis_index("tp")
    rows, width = tokens.shape
    slice_width = width // ctx_count
    t = tables(ctx_count, rows)

    def to_tp(x, bits):
        return lax.ppermute(x, "tp", [(i, i ^ bits) for i in range(tp_count)])

    def to_next(x):
        return lax.ppermute(x, "ctx", [(i, i + 1) for i in range(ctx_count - 1)])

    def to_previous(x):
        return lax.ppermute(x, "ctx", [(i + 1, i) for i in range(ctx_count - 1)])

    def exchange(x):
        return lax.all_to_all(x, "ctx", split_axis=0, concat_axis=0, tiled=True)

    far = to_tp(tokens, 2)
    sib = to_tp(tokens, 1)
    filter_halo = to_next(long_filter[rows - 8 :])
    farsib = to_tp(far, 1)
    order = jnp.stack([tp, tp ^ 1, tp ^ 2, tp ^ 3]).astype(jnp.int32)
    parts = (tokens, sib, far, farsib)
    gate_weight = in_weight[:, 0]
    value_weight = in_weight[:, 1]
    gate_taps = short_kernel[:, 0]
    value_taps = short_kernel[:, 1]
    skip = jnp.where(ctx == 0, skip_gain, 0.0)[None, :]

    filter_rows = filter_prep(long_filter, filter_halo, value_taps, skip)
    filter_columns = exchange(filter_rows.reshape(ctx_count, slice_width, rows))
    values = project(order, parts, value_weight, ctx_count, True)
    value_columns = exchange(values)
    spec = filter_spectrum(filter_columns, t)
    conv_columns = convolve(value_columns, spec, t)
    conv = exchange(conv_columns)
    gates = project(order, parts, gate_weight, ctx_count, False)
    below = to_next(gates[rows - 16 : rows])
    above = to_previous(gates[rows : rows + 16])
    return finish(gates, below, above, gate_taps, conv)


def solution(mesh):
    placed = (P("ctx", "tp"), P(None, None, "tp"), P(None, None, "tp"), P("ctx", "tp"), P("tp"))
    return jax.shard_map(shards, mesh=mesh, in_specs=placed, out_specs=P("ctx", "tp"), check_vma=False)
```

time: 559 us -> 159 us (0.28)
  the two profiles are of different devices: /device:TPU:10 before, /device:TPU:26 now
where the time goes in v1:
time: 159 us; the launch traced here: 158 us
  local copies, waits for them, and re-layouts  62.7 us (39%)
  Pallas kernels  42 us (26%)
  starting transfers between devices  36.7 us (23%)
  waiting for transfers between devices  15.7 us (10%)
    slice x1, local copies, waits for them, and re-layouts, shards(): value_weight = in_weight[:, 1]  32.1 us
    unnamed x26, local copies, waits for them, and re-layouts  29 us
    all_to_all x3, starting transfers between devices, exchange(): return lax.all_to_all(x, 'ctx', split_axis=0, concat_axis=0, tiled=True)  24 us
    pallas_call x2, Pallas kernels, project(): pl.pallas_call(functools.partial(project_kernel, transposed), grid_spec=p...  20 us
    all_to_all x3, waiting for transfers between devices, exchange(): return lax.all_to_all(x, 'ctx', split_axis=0, concat_axis=0, tiled=True)  9.96 us
    pallas_call x1, Pallas kernels, convolve(): pl.pallas_call(convolve_kernel, out_shape=jax.ShapeDtypeStruct(x.shape, B...  9.45 us
    ppermute x2, starting transfers between devices, to_next(): return lax.ppermute(x, 'ctx', [(i, i + 1) for i in range(ctx_count - 1)])  7.84 us
    ppermute x1, waiting for transfers between devices, to_previous(): return lax.ppermute(x, 'ctx', [(i + 1, i) for i in range(ctx_count - 1)])  5.73 us
  transfers between devices with their start and end apart: 9, of which 2 were waited for; matrix products, arithmetic and copies ran while one was open for 38% of the time, Pallas kernels for 18%

profile of v1, /device:TPU:26, one launch (start us, length us, event | category | flops | bytes accessed | tf_op | source)
XLA Modules:
  0.0 158.4 jit_solution(7802039065063132855)
XLA Ops:
  0.0 2.1 %collective-permute-start.1 = (bf16[256,1024]{1,0:T(8,128)(2,1)}, bf16[256,1024]{1,0:T(8,128)(2,1)S(1)}, u32[]{:S(2)}, u32[]{:S(2)}) collective-permute-start(bf16[256,1024]{1,0:T(8,128)(2,1)} %own_ref.3), channel_id=1, source_target_pairs={{0,2},{1,3},{2,0},{3,1},{4,6},{5,7},{6,4},{7,5},{8,10},{9,11},{10,... | collective-permute-start | bytes 1572872 | tf_op jit(solution)/shard_map/ppermute | solution.py:270
  2.1 0.0 collective-permute-start
  2.1 0.8 slice.26
  2.9 4.5 %collective-permute-start.5 = (f32[8,1024]{1,0:T(8,128)S(1)}, f32[8,1024]{1,0:T(8,128)S(1)}, u32[]{:S(2)}, u32[]{:S(2)}) collective-permute-start(f32[8,1024]{1,0:T(8,128)S(1)} %slice.26), channel_id=1, source_target_pairs={{0,4},{4,8},{8,12},{12,16},{16,20},{20,24},{24,28},{28,32},{32,36}... | collective-permute-start | bytes 98312 | tf_op jit(solution)/shard_map/ppermute | solution.py:273
  7.4 32.1 %fusion = (bf16[4096,1,1024]{2,1,0:T(2,128)(2,1)}, bf16[4096,1,1024]{2,1,0:T(2,128)(2,1)}) fusion(bf16[4096,2,1024]{2,1,0:T(2,128)(2,1)} %param.12), kind=kLoop, calls=%fused_computation.6 | loop fusion | bytes 33554432 | tf_op jit(solution)/shard_map/slice | solution.py:288
  39.5 0.3 collective-permute-start.2
  39.8 0.6 broadcast_select_fusion
  40.4 12.1 %copy.24 = bf16[4096,1,1024]{2,0,1:T(8,128)(2,1)} copy(bf16[4096,1,1024]{2,1,0:T(2,128)(2,1)} %get-tuple-element.5) | data formatting | bytes 16777216
  52.5 0.6 copy.26
  53.2 0.6 copy-done.5
  53.8 3.6 %filter_prep.1 = bf16[1024,256]{1,0:T(8,128)(2,1)} custom-call(f32[256,1024]{1,0:T(8,128)} %filter_ref.1, f32[8,1024]{1,0:T(8,128)} %copy-done.5, f32[3,1024]{1,0:T(4,128)} %bitcast.22, f32[1,1024]{1,0:T(1,128)} %bitcast.23), custom_call_target="tpu_custom_call" | custom-call | flops 2621440 | bytes 1572864 | tf_op jit(solution)/shard_map/filter_prep/pallas_call | solution.py:77
  57.3 8.9 %all-to-all-start.1 = ((bf16[32,32,256]{2,1,0:T(8,128)(2,1)}), bf16[32,32,256]{2,1,0:T(8,128)(2,1)S(1)}, u32[]{:S(2)}, u32[]{:S(2)}) async-start(bf16[32,32,256]{2,1,0:T(8,128)(2,1)} %bitcast.20), calls=%async_computation.1 | async-start | bytes 1048576 | tf_op jit(solution)/shard_map/all_to_all | solution.py:279
  66.3 0.6 pad_add_fusion.order_ref
  66.9 0.8 copy-done.9
  67.7 0.2 copy-done.10
  67.8 10.1 %project_values.1 = bf16[32,64,256]{2,1,0:T(8,128)(2,1)} custom-call(s32[4]{0:T(128)} %pad_add_fusion.order_ref, bf16[256,1024]{1,0:T(8,128)(2,1)} %own_ref.3, bf16[256,1024]{1,0:T(8,128)(2,1)} %copy-done.9, bf16[256,1024]{1,0:T(8,128)(2,1)} %copy-done.8, bf16[256,1024]{1,0:T(8,128)(2,1)} %copy-done.10, bf16[4096,1024]{1,0:T(8,128)(2,1)} %bitcast.18), custom_call_target="tpu_custom_call" | custom-call | flops 4294967296 | bytes 8388608 | tf_op jit(solution)/shard_map/project_values/pallas_call | solution.py:196
  77.9 8.3 %all-to-all-start = ((bf16[32,64,256]{2,1,0:T(8,128)(2,1)}), bf16[32,64,256]{2,1,0:T(8,128)(2,1)S(1)}, u32[]{:S(2)}, u32[]{:S(2)}) async-start(bf16[32,64,256]{2,1,0:T(8,128)(2,1)} %project_values.1), calls=%async_computation | async-start | bytes 2097152 | tf_op jit(solution)/shard_map/all_to_all | solution.py:279
  86.3 4.9 %filter_spectrum.1.spec_ref = f32[2,512,512]{2,1,0:T(8,128)} custom-call(bf16[32,32,256]{2,1,0:T(8,128)(2,1)} %copy-done.2, bf16[1024,512]{1,0:T(8,128)(2,1)} %constant.37.forward_ref, f32[512,256]{1,0:T(8,128)} %constant.33.clone.cos_ref, f32[512,256]{1,0:T(8,128)} %constant.34.clone.sin_ref, bf16[512,512]{1,0:T(8,128)(2,1)} %constant.38.inner_ref), custom_call_target="tpu_custom_call" | custom-call | flops 2000000000 | bytes 6291456 | tf_op jit(solution)/shard_map/filter_spectrum/pallas_call | solution.py:104
  91.2 10.0 %all-to-all-done.x_ref = bf16[32,64,256]{2,1,0:T(8,128)(2,1)S(1)} async-done(((bf16[32,64,256]{2,1,0:T(8,128)(2,1)}), bf16[32,64,256]{2,1,0:T(8,128)(2,1)S(1)}, u32[]{:S(2)}, u32[]{:S(2)}) %all-to-all-start) | async-done | bytes 1048608 | tf_op jit(solution)/shard_map/all_to_all | solution.py:279
  101.1 1.0 copy-done.1
  102.1 9.4 %convolve.1 = bf16[32,64,256]{2,1,0:T(8,128)(2,1)} custom-call(bf16[32,64,256]{2,1,0:T(8,128)(2,1)} %copy-done.1, f32[2,512,512]{2,1,0:T(8,128)} %filter_spectrum.1.spec_ref, bf16[1024,512]{1,0:T(8,128)(2,1)} %constant.37.forward_ref, bf16[512,1024]{1,0:T(8,128)(2,1)} %constant.39.backward_ref, f32[512,256]{1,0:T(8,128)} %constant.33.clone.cos_ref, ...), custom_call_target="tpu_custom_call" | custom-call | flops 8000000000 | bytes 10485760 | tf_op jit(solution)/shard_map/convolve/pallas_call | solution.py:138
  111.6 6.7 %all-to-all-start.2 = ((bf16[32,64,256]{2,1,0:T(8,128)(2,1)}), bf16[32,64,256]{2,1,0:T(8,128)(2,1)S(1)}, u32[]{:S(2)}, u32[]{:S(2)}) async-start(bf16[32,64,256]{2,1,0:T(8,128)(2,1)} %convolve.1), calls=%async_computation.2 | async-start | bytes 2097152 | tf_op jit(solution)/shard_map/all_to_all | solution.py:279
  118.3 12.1 %copy.25 = bf16[4096,1,1024]{2,0,1:T(8,128)(2,1)} copy(bf16[4096,1,1024]{2,1,0:T(2,128)(2,1)} %get-tuple-element.6) | data formatting | bytes 16777216
  130.5 9.9 %project_gates.1.gates_ref = bf16[512,1024]{1,0:T(8,128)(2,1)} custom-call(s32[4]{0:T(128)} %pad_add_fusion.order_ref, bf16[256,1024]{1,0:T(8,128)(2,1)} %own_ref.3, bf16[256,1024]{1,0:T(8,128)(2,1)} %copy-done.9, bf16[256,1024]{1,0:T(8,128)(2,1)} %copy-done.8, bf16[256,1024]{1,0:T(8,128)(2,1)} %copy-done.10, bf16[4096,1024]{1,0:T(8,128)(2,1)} %bitcast.19), custom_call_target="tpu_custom_call" | custom-call | flops 4294967296 | bytes 8388608 | tf_op jit(solution)/shard_map/project_gates/pallas_call | solution.py:196
  140.4 0.8 fusion.1
  141.2 3.4 %collective-permute-start.3 = (bf16[16,1024]{1,0:T(8,128)(2,1)S(1)}, bf16[16,1024]{1,0:T(8,128)(2,1)S(1)}, u32[]{:S(2)}, u32[]{:S(2)}) collective-permute-start(bf16[16,1024]{1,0:T(8,128)(2,1)S(1)} %get-tuple-element.8), channel_id=1, source_target_pairs={{0,4},{4,8},{8,12},{12,16},{16,20},{20,24},{24,28},{28,32},{32,36}... | collective-permute-start | bytes 98312 | tf_op jit(solution)/shard_map/ppermute | solution.py:273
  144.6 2.5 %collective-permute-start.4 = (bf16[16,1024]{1,0:T(8,128)(2,1)S(1)}, bf16[16,1024]{1,0:T(8,128)(2,1)S(1)}, u32[]{:S(2)}, u32[]{:S(2)}) collective-permute-start(bf16[16,1024]{1,0:T(8,128)(2,1)S(1)} %get-tuple-element.7), channel_id=1, source_target_pairs={{4,0},{8,4},{12,8},{16,12},{20,16},{24,20},{28,24},{32,28},{36,32}... | collective-permute-start | bytes 98312 | tf_op jit(solution)/shard_map/ppermute | solution.py:276
  147.0 0.6 copy.27
  147.6 5.7 %collective-permute-done.4.above_ref = bf16[16,1024]{1,0:T(8,128)(2,1)S(1)} collective-permute-done((bf16[16,1024]{1,0:T(8,128)(2,1)S(1)}, bf16[16,1024]{1,0:T(8,128)(2,1)S(1)}, u32[]{:S(2)}, u32[]{:S(2)}) %collective-permute-start.4) | collective-permute-done | bytes 32800 | tf_op jit(solution)/shard_map/ppermute | solution.py:276
  153.4 0.6 copy-done.4
  154.0 0.4 copy-done
  154.4 4.0 %finish.1 = bf16[256,1024]{1,0:T(8,128)(2,1)} custom-call(bf16[512,1024]{1,0:T(8,128)(2,1)} %project_gates.1.gates_ref, bf16[16,1024]{1,0:T(8,128)(2,1)} %copy-done.3, bf16[16,1024]{1,0:T(8,128)(2,1)} %copy-done.4, f32[3,1024]{1,0:T(4,128)} %bitcast.21, bf16[32,64,256]{2,1,0:T(8,128)(2,1)} %copy-done), custom_call_target="tpu_custom_call" | custom-call | flops 4194304 | bytes 3145728 | tf_op jit(solution)/shard_map/finish/pallas_call | solution.py:242
  (24 shorter events, 0.1 us)
Async XLA Ops:
  0.0 39.5 %collective-permute-start.1 = (bf16[256,1024]{1,0:T(8,128)(2,1)}, bf16[256,1024]{1,0:T(8,128)(2,1)S(1)}, u32[]{:S(2)}, u32[]{:S(2)}) collective-permute-start(bf16[256,1024]{1,0:T(8,128)(2,1)} %own_ref.3), channel_id=1, source_target_pairs={{0,2},{1,3},{2,0},{3,1},{4,6},{5,7},{6,4},{7,5},{8,10},{9,11},{10,... | collective-permute-start | bytes 1572872 | tf_op jit(solution)/shard_map/ppermute | solution.py:270
  2.1 64.7 %collective-permute-start = (bf16[256,1024]{1,0:T(8,128)(2,1)}, bf16[256,1024]{1,0:T(8,128)(2,1)S(1)}, u32[]{:S(2)}, u32[]{:S(2)}) collective-permute-start(bf16[256,1024]{1,0:T(8,128)(2,1)} %own_ref.3), channel_id=1, source_target_pairs={{0,1},{1,0},{2,3},{3,2},{4,5},{5,4},{6,7},{7,6},{8,9},{9,8},{10,11... | collective-permute-start | bytes 1572872 | tf_op jit(solution)/shard_map/ppermute | solution.py:270
  2.9 36.9 %copy-start.6 = (f32[3,2,1024]{2,1,0:T(2,128)S(1)}, f32[3,2,1024]{2,1,0:T(2,128)}, u32[]{:S(2)}) copy-start(f32[3,2,1024]{2,1,0:T(2,128)} %param.13) | copy-start | bytes 73732
  2.9 36.9 %copy-start.7 = (f32[1024]{0:T(1024)S(1)}, f32[1024]{0:T(1024)}, u32[]{:S(2)}) copy-start(f32[1024]{0:T(1024)} %param.15) | copy-start | bytes 12292
  2.9 50.3 %collective-permute-start.5 = (f32[8,1024]{1,0:T(8,128)S(1)}, f32[8,1024]{1,0:T(8,128)S(1)}, u32[]{:S(2)}, u32[]{:S(2)}) collective-permute-start(f32[8,1024]{1,0:T(8,128)S(1)} %slice.26), channel_id=1, source_target_pairs={{0,4},{4,8},{8,12},{12,16},{16,20},{20,24},{24,28},{28,32},{32,36}... | collective-permute-start | bytes 98312 | tf_op jit(solution)/shard_map/ppermute | solution.py:273
  39.5 27.4 %copy-start.8 = (bf16[256,1024]{1,0:T(8,128)(2,1)}, bf16[256,1024]{1,0:T(8,128)(2,1)S(1)}, u32[]{:S(2)}) copy-start(bf16[256,1024]{1,0:T(8,128)(2,1)S(1)} %collective-permute-done.1.far_ref) | copy-start | bytes 1572868
  39.5 27.4 %collective-permute-start.2 = (bf16[256,1024]{1,0:T(8,128)(2,1)S(1)}, bf16[256,1024]{1,0:T(8,128)(2,1)S(1)}, u32[]{:S(2)}, u32[]{:S(2)}) collective-permute-start(bf16[256,1024]{1,0:T(8,128)(2,1)S(1)} %collective-permute-done.1.far_ref), channel_id=1, source_target_pairs={{0,1},{1,0},{2,3},{3,2},{4,5},{5,4},{6,7},{7,6},{8,9},{9,8},{10,11... | collective-permute-start | bytes 1572872 | tf_op jit(solution)/shard_map/ppermute | solution.py:270
  53.1 0.6 copy-start.5
  57.3 20.6 %all-to-all-start.1 = ((bf16[32,32,256]{2,1,0:T(8,128)(2,1)}), bf16[32,32,256]{2,1,0:T(8,128)(2,1)S(1)}, u32[]{:S(2)}, u32[]{:S(2)}) async-start(bf16[32,32,256]{2,1,0:T(8,128)(2,1)} %bitcast.20), calls=%async_computation.1 | async-start | bytes 1048576 | tf_op jit(solution)/shard_map/all_to_all | solution.py:279
  66.9 0.8 copy-start.9
  66.9 1.0 copy-start.10
  77.9 8.3 %copy-start.2 = (bf16[32,32,256]{2,1,0:T(8,128)(2,1)}, bf16[32,32,256]{2,1,0:T(8,128)(2,1)S(1)}, u32[]{:S(2)}) copy-start(bf16[32,32,256]{2,1,0:T(8,128)(2,1)S(1)} %all-to-all-done.1.x_ref) | copy-start | bytes 1572868
  77.9 23.2 %all-to-all-start = ((bf16[32,64,256]{2,1,0:T(8,128)(2,1)}), bf16[32,64,256]{2,1,0:T(8,128)(2,1)S(1)}, u32[]{:S(2)}, u32[]{:S(2)}) async-start(bf16[32,64,256]{2,1,0:T(8,128)(2,1)} %project_values.1), calls=%async_computation | async-start | bytes 2097152 | tf_op jit(solution)/shard_map/all_to_all | solution.py:279
  101.1 1.0 copy-start.1
  111.6 41.8 %all-to-all-start.2 = ((bf16[32,64,256]{2,1,0:T(8,128)(2,1)}), bf16[32,64,256]{2,1,0:T(8,128)(2,1)S(1)}, u32[]{:S(2)}, u32[]{:S(2)}) async-start(bf16[32,64,256]{2,1,0:T(8,128)(2,1)} %convolve.1), calls=%async_computation.2 | async-start | bytes 2097152 | tf_op jit(solution)/shard_map/all_to_all | solution.py:279
  141.2 6.5 %collective-permute-start.3 = (bf16[16,1024]{1,0:T(8,128)(2,1)S(1)}, bf16[16,1024]{1,0:T(8,128)(2,1)S(1)}, u32[]{:S(2)}, u32[]{:S(2)}) collective-permute-start(bf16[16,1024]{1,0:T(8,128)(2,1)S(1)} %get-tuple-element.8), channel_id=1, source_target_pairs={{0,4},{4,8},{8,12},{12,16},{16,20},{20,24},{24,28},{28,32},{32,36}... | collective-permute-start | bytes 98312 | tf_op jit(solution)/shard_map/ppermute | solution.py:273
  144.6 8.8 %collective-permute-start.4 = (bf16[16,1024]{1,0:T(8,128)(2,1)S(1)}, bf16[16,1024]{1,0:T(8,128)(2,1)S(1)}, u32[]{:S(2)}, u32[]{:S(2)}) collective-permute-start(bf16[16,1024]{1,0:T(8,128)(2,1)S(1)} %get-tuple-element.7), channel_id=1, source_target_pairs={{4,0},{8,4},{12,8},{16,12},{20,16},{24,20},{28,24},{32,28},{36,32}... | collective-permute-start | bytes 98312 | tf_op jit(solution)/shard_map/ppermute | solution.py:276
  147.6 5.7 %copy-start.3 = (bf16[16,1024]{1,0:T(8,128)(2,1)}, bf16[16,1024]{1,0:T(8,128)(2,1)S(1)}, u32[]{:S(2)}) copy-start(bf16[16,1024]{1,0:T(8,128)(2,1)S(1)} %collective-permute-done.3.below_ref) | copy-start | bytes 98308
  153.4 0.6 copy-start.4
  153.4 1.0 copy-start

commit v2 on v0

v2 whole, which is shorter than its diff:
```python
import math

import jax
import jax.numpy as jnp
import numpy as np
from jax import lax
from jax.experimental import pallas as pl
from jax.experimental.pallas import tpu as pltpu
from jax.sharding import PartitionSpec as P

BF16 = jnp.bfloat16
F32 = jnp.float32
LANES = 128
GROUP = 8
PACK = 16
MIB = 1024 * 1024
PROJECT_BYTES = 50 * MIB
CONVOLVE_BYTES = 16 * MIB
SMALL_BYTES = 10 * MIB


def params(limit):
    return pltpu.CompilerParams(vmem_limit_bytes=limit)


def cost(flops, moved):
    return pl.CostEstimate(flops=flops, bytes_accessed=moved, transcendentals=0)


def mm(a, b):
    return jnp.dot(a, b, preferred_element_type=F32)


def tables(blocks, rows):
    length = blocks * rows
    half = rows // 2
    j1 = np.arange(blocks)
    q = np.arange(rows)
    outer = 2 * math.pi * ((4 * j1[:, None] + 1) * j1[None, :] % (4 * blocks)) / (4 * blocks)
    eye = np.eye(GROUP)
    forward = np.concatenate([np.kron(np.cos(outer), eye), np.kron(-np.sin(outer), eye)], 0)
    turn = 2 * math.pi * ((4 * j1[:, None] + 1) * q[None, :]) / (4 * length)
    turn = turn[:, None, :]
    inner = []
    for odd in (0, 1):
        angle = 2 * math.pi * (q[:half, None] * (2 * q[None, :half] + odd) % rows) / rows
        c, s = np.cos(angle), np.sin(angle)
        inner.append(np.block([[c, -s], [s, c]]))
    inner = np.stack(inner)
    small = lambda a: jnp.asarray(a.astype(np.float32)).astype(BF16)
    return dict(
        forward=small(forward),
        backward=small(forward.T),
        turn_cos=jnp.asarray(np.cos(turn), F32),
        turn_sin=jnp.asarray(np.sin(turn), F32),
        inner=small(inner),
        inner_back=small(inner.transpose(0, 2, 1) / length),
    )


def turns(cos_ref, sin_ref):
    blocks, _, rows = cos_ref.shape
    wide = lambda ref: jnp.broadcast_to(ref[...], (blocks, GROUP, rows)).reshape(blocks * GROUP, rows)
    return wide(cos_ref), wide(sin_ref)


def columns_of(x_ref, pack):
    blocks, _, rows = x_ref.shape
    x = x_ref[:, pack * PACK : (pack + 1) * PACK, :].astype(F32)
    return [x[:, h * GROUP : (h + 1) * GROUP].reshape(blocks * GROUP, rows).astype(BF16) for h in range(2)]


def spectrum(x, forward, turn_cos, turn_sin, inner):
    count = x.shape[0]
    half = x.shape[1] // 2
    mixed = mm(forward, x)
    real, imag = mixed[:count], mixed[count:]
    turned_real = real * turn_cos + imag * turn_sin
    turned_imag = imag * turn_cos - real * turn_sin
    result = []
    for odd in (0, 1):
        sign = -1.0 if odd else 1.0
        parts = [(t[:, :half] + sign * t[:, half:]).astype(BF16) for t in (turned_real, turned_imag)]
        result.append(mm(jnp.concatenate(parts, 1), inner[odd]))
    return result


def filter_prep_kernel(filter_ref, out_ref):
    out_ref[...] = filter_ref[...].T.astype(BF16)


def filter_prep(long_filter, block=512):
    rows, width = long_filter.shape
    block = min(block, width)
    return pl.pallas_call(
        filter_prep_kernel,
        grid=(width // block,),
        in_specs=[pl.BlockSpec((rows, block), lambda i: (0, i))],
        out_specs=pl.BlockSpec((block, rows), lambda i: (i, 0)),
        out_shape=jax.ShapeDtypeStruct((width, rows), BF16),
        compiler_params=params(SMALL_BYTES),
        cost_estimate=cost(10 * rows * width, 6 * rows * width),
        name="filter_prep",
    )(long_filter)


def filter_spectrum(x_ref, at, taps_ref, skip_ref, forward_ref, turn_cos, turn_sin, inner_ref, out_ref):
    blocks, _, rows = x_ref.shape
    width = GROUP * out_ref.shape[0]
    local = taps_ref.shape[2]
    lane = lax.broadcasted_iota(jnp.int32, (width, local), 1)
    mine = lane - lax.broadcasted_iota(jnp.int32, (width, local), 0) == lax.axis_index("ctx") * width
    column = lambda row: jnp.sum(jnp.where(mine, row, 0.0), axis=1, keepdims=True)
    taps = [column(taps_ref[tap, 1:2]) for tap in range(3)]
    skip = column(skip_ref[...])
    position = lax.broadcasted_iota(jnp.int32, (PACK, rows), 1)
    for pack in range(width // PACK):
        these = slice(pack * PACK, (pack + 1) * PACK)
        x = x_ref[:, at + pack * PACK : at + (pack + 1) * PACK, :].astype(F32)
        first = x[:1] + jnp.where(position == 0, skip[these], 0.0)[None]
        x = jnp.concatenate([first, x[1:]], 0)
        total = taps[0][these][None] * x
        for tap in (1, 2):
            moved = pltpu.roll(x, tap, 2)
            before = jnp.concatenate([jnp.zeros((1, PACK, rows), F32), moved[:-1]], 0)
            total = total + taps[tap][these][None] * jnp.where((position < tap)[None], before, moved)
        for h in range(2):
            part = total[:, h * GROUP : (h + 1) * GROUP].reshape(blocks * GROUP, rows).astype(BF16)
            for odd, result in enumerate(spectrum(part, forward_ref[...], turn_cos, turn_sin, inner_ref)):
                out_ref[2 * pack + h, odd] = result


def convolve_kernel(
    x_ref, taps_ref, skip_ref, forward_ref, cos_ref, sin_ref, inner_ref, inner_back_ref, backward_ref, out_ref, spec_ref
):
    blocks, width, rows = out_ref.shape
    half = rows // 2
    packs = width // PACK
    turn_cos, turn_sin = turns(cos_ref, sin_ref)
    filter_spectrum(x_ref, width, taps_ref, skip_ref, forward_ref, turn_cos, turn_sin, inner_ref, spec_ref)
    for pack in range(packs):
        outs = []
        for h, x in enumerate(columns_of(x_ref, pack)):
            data = spectrum(x, forward_ref[...], turn_cos, turn_sin, inner_ref)
            back = []
            for odd in (0, 1):
                filt = spec_ref.at[2 * (pack % (packs // 2)) + h, odd]
                real, imag = data[odd][:, :half], data[odd][:, half:]
                filter_real, filter_imag = filt[:, :half], filt[:, half:]
                if pack >= packs // 2:
                    filter_imag = -filter_imag
                prod_real = (real * filter_real - imag * filter_imag).astype(BF16)
                prod_imag = (real * filter_imag + imag * filter_real).astype(BF16)
                back.append(mm(jnp.concatenate([prod_real, prod_imag], 1), inner_back_ref[odd]))
            near, far = back[0] + back[1], back[0] - back[1]
            real = jnp.concatenate([near[:, :half], far[:, :half]], 1)
            imag = jnp.concatenate([near[:, half:], far[:, half:]], 1)
            turned_real = (real * turn_cos - imag * turn_sin).astype(BF16)
            turned_imag = (imag * turn_cos + real * turn_sin).astype(BF16)
            out = mm(backward_ref[...], jnp.concatenate([turned_real, turned_imag], 0))
            outs.append(out.reshape(blocks, GROUP, rows))
        out_ref[:, pack * PACK : (pack + 1) * PACK, :] = jnp.concatenate(outs, 1).astype(BF16)


def convolve(x, taps, skip, t):
    blocks, width, rows = x.shape
    count = width // 3
    return pl.pallas_call(
        convolve_kernel,
        out_shape=jax.ShapeDtypeStruct((blocks, 2 * count, rows), BF16),
        scratch_shapes=[pltpu.VMEM((count // GROUP, 2, blocks * GROUP, rows), F32)],
        compiler_params=params(CONVOLVE_BYTES),
        cost_estimate=cost(5 * 10**9, 4 * MIB),
        name="convolve",
    )(x, taps, skip, t["forward"], t["turn_cos"], t["turn_sin"], t["inner"], t["inner_back"], t["backward"])


def swap_matrix(block):
    total = lax.broadcasted_iota(jnp.int32, (block, block), 0) + lax.broadcasted_iota(jnp.int32, (block, block), 1)
    return jnp.where(total == block - 1, 1.0, 0.0).astype(BF16)


def project_kernel(
    which, own_hbm, sib_hbm, far_hbm, farsib_hbm, w_hbm, filter_hbm, out_ref, left_ref, raw_ref, total_ref, part_sems, w_sems, filter_sem
):
    _, rows2, depth = left_ref.shape
    rows = rows2 // 2
    width = total_ref.shape[1]
    tiles = width // LANES
    block = min(256, width)
    chunk = raw_ref.shape[1]
    tp = lax.axis_index("tp")
    part_copies = [
        pltpu.make_async_copy(src, left_ref.at[k, :rows], part_sems.at[k])
        for k, src in enumerate((own_hbm, sib_hbm, far_hbm, farsib_hbm))
    ]
    w_copies = [
        pltpu.make_async_copy(
            w_hbm.at[pl.ds(pl.multiple_of((tp ^ k) * chunk, chunk), chunk)], raw_ref.at[k], w_sems.at[k]
        )
        for k in range(4)
    ]
    w_copies[0].start()
    for copy in part_copies:
        copy.start()
    for copy in w_copies[1:]:
        copy.start()
    if filter_hbm is not None:
        slice_width = filter_hbm.shape[1]
        filter_copy = pltpu.make_async_copy(filter_hbm, out_ref.at[:, 2 * slice_width :], filter_sem)
        filter_copy.start()
    for copy in part_copies:
        copy.wait()
    swap = swap_matrix(block)
    count = depth // block
    for k in range(4):
        other = left_ref[3 - k, :rows]
        for b in range(count):
            piece = mm(other[:, (count - 1 - b) * block : (count - b) * block], swap)
            left_ref[k, rows:, b * block : (b + 1) * block] = piece.astype(BF16)
    for k in range(4):
        w_copies[k].wait()
        left = left_ref[k]
        for b in range(width // block):
            cols = slice(b * block, (b + 1) * block)
            weights = [
                raw_ref[k, pl.ds(2 * tile + which, depth, stride=2 * tiles), :]
                for tile in range(b * block // LANES, (b + 1) * block // LANES)
            ]
            term = mm(left, jnp.concatenate(weights, 1))
            if k == 0:
                total_ref[:, cols] = term
            elif k < 3:
                total_ref[:, cols] += term
            else:
                total = total_ref[:, cols] + term
                if filter_hbm is not None:
                    turned = total.T.astype(BF16)
                    per = block // slice_width
                    for d in range(per):
                        part = turned[d * slice_width : (d + 1) * slice_width]
                        out_ref[b * per + d, :slice_width] = part[:, :rows]
                        out_ref[b * per + d, slice_width : 2 * slice_width] = part[:, rows:]
                else:
                    out_ref[:, cols] = total.astype(BF16)
    if filter_hbm is not None:
        filter_copy.wait()


def project(parts, weight_rows, which, width, filter_rows=None):
    rows, depth = parts[0].shape
    tiles = width // LANES
    model = weight_rows.shape[0] // (2 * tiles)
    extra = () if filter_rows is None else (filter_rows,)
    if extra:
        out_shape = (filter_rows.shape[0], 3 * filter_rows.shape[1], rows)
    else:
        out_shape = (2 * rows, width)

    def kernel(*refs):
        filter_hbm = refs[5] if extra else None
        project_kernel(which, *refs[:5], filter_hbm, *refs[5 + len(extra) :])

    return pl.pallas_call(
        kernel,
        in_specs=[pl.BlockSpec(memory_space=pl.ANY)] * (5 + len(extra)),
        out_specs=pl.BlockSpec(memory_space=pltpu.VMEM),
        scratch_shapes=[
            pltpu.VMEM((4, 2 * rows, depth), BF16),
            pltpu.VMEM((4, depth * 2 * tiles, LANES), BF16),
            pltpu.VMEM((2 * rows, width), F32),
            pltpu.SemaphoreType.DMA((4,)),
            pltpu.SemaphoreType.DMA((4,)),
            pltpu.SemaphoreType.DMA,
        ],
        out_shape=jax.ShapeDtypeStruct(out_shape, BF16),
        compiler_params=params(PROJECT_BYTES),
        cost_estimate=cost(4 * rows * model * width, 4 * model * width),
        name="project_values" if extra else "project_gates",
    )(*parts, weight_rows, *extra)


def gate_mix_kernel(gates_ref, below_ref, above_ref, taps_ref, out_ref):
    rows = gates_ref.shape[0] // 2
    block = gates_ref.shape[1]
    row = lax.broadcasted_iota(jnp.int32, (rows, block), 0)
    forward = gates_ref[:rows].astype(F32)
    reverse = gates_ref[rows:].astype(F32)
    below = below_ref[...].astype(F32)
    above = above_ref[...].astype(F32)
    tail = below.shape[0]
    gate_forward = taps_ref[0, 0:1] * forward
    gate_reverse = taps_ref[0, 0:1] * reverse
    for tap in (1, 2):
        moved = pltpu.roll(forward, tap, 0)
        other = pltpu.roll(reverse, rows - tap, 0)
        for edge in range(tap):
            moved = jnp.where(row == edge, below[tail - tap + edge : tail - tap + edge + 1], moved)
            other = jnp.where(row == rows - tap + edge, above[edge : edge + 1], other)
        gate_forward = gate_forward + taps_ref[tap, 0:1] * moved
        gate_reverse = gate_reverse + taps_ref[tap, 0:1] * other
    out_ref[0] = gate_forward.T
    out_ref[1] = gate_reverse.T


def gate_mix(gates, below, above, taps, block=256):
    rows, width = gates.shape[0] // 2, gates.shape[1]
    block = min(block, width)
    return pl.pallas_call(
        gate_mix_kernel,
        grid=(width // block,),
        in_specs=[
            pl.BlockSpec((2 * rows, block), lambda i: (0, i)),
            pl.BlockSpec((below.shape[0], block), lambda i: (0, i)),
            pl.BlockSpec((above.shape[0], block), lambda i: (0, i)),
            pl.BlockSpec((3, 2, block), lambda i: (0, 0, i)),
        ],
        out_specs=pl.BlockSpec((2, block, rows), lambda i: (0, i, 0)),
        out_shape=jax.ShapeDtypeStruct((2, width, rows), F32),
        compiler_params=params(SMALL_BYTES),
        cost_estimate=cost(16 * rows * width, 12 * rows * width),
        name="gate_mix",
    )(gates, below, above, taps)


def finish_kernel(gates_ref, conv_ref, out_ref):
    rows, block = out_ref.shape
    half = conv_ref.shape[1] // 2
    forward = conv_ref[:, :half].reshape(block, rows).astype(F32)
    reverse = conv_ref[:, half:].reshape(block, rows).astype(F32)
    out_ref[...] = (gates_ref[0] * forward + gates_ref[1] * reverse).T.astype(BF16)


def finish(gates, conv, block=256):
    _, width, rows = gates.shape
    block = min(block, width)
    pair = conv.shape[1]
    return pl.pallas_call(
        finish_kernel,
        grid=(width // block,),
        in_specs=[
            pl.BlockSpec((2, block, rows), lambda i: (0, i, 0)),
            pl.BlockSpec((2 * block // pair, pair, rows), lambda i: (i, 0, 0)),
        ],
        out_specs=pl.BlockSpec((rows, block), lambda i: (0, i)),
        out_shape=jax.ShapeDtypeStruct((rows, width), BF16),
        compiler_params=params(SMALL_BYTES),
        cost_estimate=cost(4 * rows * width, 14 * rows * width),
        name="finish",
    )(gates, conv)


def shards(tokens, in_weight, short_kernel, long_filter, skip_gain):
    ctx_count = lax.axis_size("ctx")
    tp_count = lax.axis_size("tp")
    rows, width = tokens.shape
    model = in_weight.shape[0]
    slice_width = width // ctx_count
    tiles = width // LANES
    t = tables(ctx_count, rows)

    def to_tp(x, bits):
        return lax.ppermute(x, "tp", [(i, i ^ bits) for i in range(tp_count)])

    def to_next(x):
        return lax.ppermute(x, "ctx", [(i, i + 1) for i in range(ctx_count - 1)])

    def to_previous(x):
        return lax.ppermute(x, "ctx", [(i + 1, i) for i in range(ctx_count - 1)])

    def exchange(x):
        return lax.all_to_all(x, "ctx", split_axis=0, concat_axis=0, tiled=True)

    weight_rows = in_weight.reshape(model, 2, tiles, LANES).transpose(0, 2, 1, 3).reshape(model * 2 * tiles, LANES)
    far = to_tp(tokens, 2)
    sib = to_tp(tokens, 1)
    filter_rows = filter_prep(long_filter).reshape(ctx_count, slice_width, rows)
    far, filter_rows = lax.optimization_barrier((far, filter_rows))
    farsib = to_tp(far, 1)
    parts = (tokens, sib, far, farsib)
    values = project(parts, weight_rows, 1, width, filter_rows)
    columns = exchange(values)
    parts, _ = lax.optimization_barrier((parts, values))
    gates = project(parts, weight_rows, 0, width)
    below, above = to_next(gates[rows - 16 : rows]), to_previous(gates[rows : rows + 16])
    mixed = gate_mix(gates, below, above, short_kernel)
    columns, mixed = lax.optimization_barrier((columns, mixed))
    conv = exchange(convolve(columns, short_kernel, skip_gain[None], t))
    return finish(mixed, conv)


def solution(mesh):
    placed = (P("ctx", "tp"), P(None, None, "tp"), P(None, None, "tp"), P("ctx", "tp"), P("tp"))
    return jax.shard_map(shards, mesh=mesh, in_specs=placed, out_specs=P("ctx", "tp"), check_vma=False)
```

time: 559 us -> 93 us (0.17)
  the two profiles are of different devices: /device:TPU:10 before, /device:TPU:0 now
where the time goes in v2:
time: 93 us; the launch traced here: 92.6 us
  Pallas kernels  27.8 us (30%)
  blocking collectives  21.8 us (23%)
  waiting for transfers between devices  21.4 us (23%)
  starting transfers between devices  19 us (20%)
  local copies, waits for them, and re-layouts  2.33 us (3%)
    all_to_all x1, blocking collectives, exchange(): return lax.all_to_all(x, 'ctx', split_axis=0, concat_axis=0, tiled=True)  21.8 us
    pallas_call x2, Pallas kernels, project(): pl.pallas_call(kernel, in_specs=[pl.BlockSpec(memory_space=pl.ANY)] * (5...  17.2 us
    ppermute x3, waiting for transfers between devices, to_tp(): return lax.ppermute(x, 'tp', [(i, i ^ bits) for i in range(tp_count)])  12.4 us
    all_to_all x1, starting transfers between devices, exchange(): return lax.all_to_all(x, 'ctx', split_axis=0, concat_axis=0, tiled=True)  9.92 us
    pallas_call x1, Pallas kernels, convolve(): pl.pallas_call(convolve_kernel, out_shape=jax.ShapeDtypeStruct((blocks, 2...  7.12 us
    ppermute x1, waiting for transfers between devices, to_previous(): return lax.ppermute(x, 'ctx', [(i + 1, i) for i in range(ctx_count - 1)])  6.33 us
    ppermute x1, starting transfers between devices, to_next(): return lax.ppermute(x, 'ctx', [(i, i + 1) for i in range(ctx_count - 1)])  4.55 us
    ppermute x3, starting transfers between devices, to_tp(): return lax.ppermute(x, 'tp', [(i, i ^ bits) for i in range(tp_count)])  3.11 us
  transfers between devices with their start and end apart: 6, of which 4 were waited for; matrix products, arithmetic and copies ran while one was open for 0% of the time, Pallas kernels for 10%

profile of v2, /device:TPU:0, one launch (start us, length us, event | category | flops | bytes accessed | tf_op | source)
XLA Modules:
  0.0 92.6 jit_solution(1885235323700474054)
XLA Ops:
  0.0 3.1 %collective-permute-start.1 = (bf16[256,1024]{1,0:T(8,128)(2,1)}, bf16[256,1024]{1,0:T(8,128)(2,1)S(1)}, u32[]{:S(2)}, u32[]{:S(2)}) collective-permute-start(bf16[256,1024]{1,0:T(8,128)(2,1)} %refs_0_.2), channel_id=1, source_target_pairs={{0,2},{1,3},{2,0},{3,1},{4,6},{5,7},{6,4},{7,5},{8,10},{9,11},{10,... | collective-permute-start | bytes 1572872 | tf_op jit(solution)/shard_map/ppermute | solution.py:363
  3.1 0.0 collective-permute-start
  3.1 1.2 %copy-done.2 = f32[256,1024]{1,0:T(8,128)S(1)} copy-done((f32[256,1024]{1,0:T(8,128)S(1)}, f32[256,1024]{1,0:T(8,128)}, u32[]{:S(2)}) %copy-start.2) | copy-done | bytes 1048600
  4.3 0.4 filter_prep.1
  4.7 10.5 %collective-permute-done.1.refs_2_ = bf16[256,1024]{1,0:T(8,128)(2,1)S(1)} collective-permute-done((bf16[256,1024]{1,0:T(8,128)(2,1)}, bf16[256,1024]{1,0:T(8,128)(2,1)S(1)}, u32[]{:S(2)}, u32[]{:S(2)}) %collective-permute-start.1) | collective-permute-done | bytes 524320 | tf_op jit(solution)/shard_map/ppermute | solution.py:363
  15.2 0.0 collective-permute-start.2
  15.2 0.0 collective-permute-done.refs_1_
  15.2 1.9 %collective-permute-done.2.refs_3_ = bf16[256,1024]{1,0:T(8,128)(2,1)S(1)} collective-permute-done((bf16[256,1024]{1,0:T(8,128)(2,1)S(1)}, bf16[256,1024]{1,0:T(8,128)(2,1)S(1)}, u32[]{:S(2)}, u32[]{:S(2)}) %collective-permute-start.2) | collective-permute-done | bytes 524320 | tf_op jit(solution)/shard_map/ppermute | solution.py:363
  17.2 1.0 %copy-done = bf16[256,1024]{1,0:T(8,128)(2,1)S(1)} copy-done((bf16[256,1024]{1,0:T(8,128)(2,1)S(1)}, bf16[256,1024]{1,0:T(8,128)(2,1)}, u32[]{:S(2)}) %copy-start) | copy-done | bytes 524312
  18.2 9.2 %project_values.1 = bf16[32,96,256]{2,1,0:T(8,128)(2,1)} custom-call(bf16[256,1024]{1,0:T(8,128)(2,1)S(1)} %copy-done, bf16[256,1024]{1,0:T(8,128)(2,1)S(1)} %collective-permute-done.refs_1_, bf16[256,1024]{1,0:T(8,128)(2,1)S(1)} %collective-permute-done.1.refs_2_, bf16[256,1024]{1,0:T(8,128)(2,1)S(1)} %collective-permute-done.2.refs_3_, ...), custom_call_target="tpu_custom_call" | custom-call | flops 4294967296 | bytes 16777216 | tf_op jit(solution)/shard_map/project_values/pallas_call | solution.py:264
  27.4 0.0 copy-start.1
  27.4 9.9 %all-to-all-start = ((bf16[32,96,256]{2,1,0:T(8,128)(2,1)}), bf16[32,96,256]{2,1,0:T(8,128)(2,1)}, u32[]{:S(2)}, u32[]{:S(2)}) async-start(bf16[32,96,256]{2,1,0:T(8,128)(2,1)} %project_values.1), calls=%async_computation | async-start | bytes 3145728 | tf_op jit(solution)/shard_map/all_to_all | solution.py:372
  37.4 0.0 copy-done.1
  37.4 0.0 copy-start.3
  37.4 8.0 %project_gates.1.gates_ref = bf16[512,1024]{1,0:T(8,128)(2,1)S(1)} custom-call(bf16[256,1024]{1,0:T(8,128)(2,1)S(1)} %copy-done.1, bf16[256,1024]{1,0:T(8,128)(2,1)S(1)} %collective-permute-done.refs_1_, bf16[256,1024]{1,0:T(8,128)(2,1)S(1)} %collective-permute-done.1.refs_2_, bf16[256,1024]{1,0:T(8,128)(2,1)S(1)} %collective-permute-done.2.refs_3_, ...), custom_call_target="tpu_custom_call" | custom-call | flops 4294967296 | bytes 16777216 | tf_op jit(solution)/shard_map/project_gates/pallas_call | solution.py:264
  45.4 0.0 copy-start.4
  45.4 0.0 copy-start.5
  45.4 0.0 copy-start.6
  45.4 0.0 copy-start.7
  45.4 0.0 copy-start.8
  45.4 0.0 copy-start.9
  45.4 0.0 copy-start.10
  45.5 1.4 %collective-permute-start.4 = (bf16[16,1024]{1,0:T(8,128)(2,1)S(1)}, bf16[16,1024]{1,0:T(8,128)(2,1)S(1)}, u32[]{:S(2)}, u32[]{:S(2)}) collective-permute-start(bf16[16,1024]{1,0:T(8,128)(2,1)S(1)} %get-tuple-element.21), channel_id=1, source_target_pairs={{4,0},{8,4},{12,8},{16,12},{20,16},{24,20},{28,24},{32,28},{36,32}... | collective-permute-start | bytes 98312 | tf_op jit(solution)/shard_map/ppermute | solution.py:369
  46.9 4.5 %collective-permute-start.3 = (bf16[16,1024]{1,0:T(8,128)(2,1)S(1)}, bf16[16,1024]{1,0:T(8,128)(2,1)S(1)}, u32[]{:S(2)}, u32[]{:S(2)}) collective-permute-start(bf16[16,1024]{1,0:T(8,128)(2,1)S(1)} %get-tuple-element.22), channel_id=1, source_target_pairs={{0,4},{4,8},{8,12},{12,16},{16,20},{20,24},{24,28},{28,32},{32,36}... | collective-permute-start | bytes 98312 | tf_op jit(solution)/shard_map/ppermute | solution.py:366
  51.5 6.3 %collective-permute-done.4.above_ref = bf16[16,1024]{1,0:T(8,128)(2,1)S(1)} collective-permute-done((bf16[16,1024]{1,0:T(8,128)(2,1)S(1)}, bf16[16,1024]{1,0:T(8,128)(2,1)S(1)}, u32[]{:S(2)}, u32[]{:S(2)}) %collective-permute-start.4) | collective-permute-done | bytes 32800 | tf_op jit(solution)/shard_map/ppermute | solution.py:369
  57.8 0.0 collective-permute-done.3.below_ref
  57.8 1.3 %gate_mix.1.gates_ref = f32[2,1024,256]{2,1,0:T(8,128)S(1)} custom-call(bf16[512,1024]{1,0:T(8,128)(2,1)S(1)} %project_gates.1.gates_ref, bf16[16,1024]{1,0:T(8,128)(2,1)S(1)} %collective-permute-done.3.below_ref, bf16[16,1024]{1,0:T(8,128)(2,1)S(1)} %collective-permute-done.4.above_ref, f32[3,2,1024]{2,1,0:T(2,128)S(1)} %copy-done.3), custom_call_target="tpu_custom_call" | custom-call | flops 4194304 | bytes 3145728 | tf_op jit(solution)/shard_map/gate_mix/pallas_call | solution.py:309
  59.1 2.6 %all-to-all-done.x_ref = bf16[32,96,256]{2,1,0:T(8,128)(2,1)} async-done(((bf16[32,96,256]{2,1,0:T(8,128)(2,1)}), bf16[32,96,256]{2,1,0:T(8,128)(2,1)}, u32[]{:S(2)}, u32[]{:S(2)}) %all-to-all-start) | async-done | bytes 1572896 | tf_op jit(solution)/shard_map/all_to_all | solution.py:372
  61.8 0.0 copy-done.5
  61.8 7.1 %convolve.1 = bf16[32,64,256]{2,1,0:T(8,128)(2,1)S(1)} custom-call(bf16[32,96,256]{2,1,0:T(8,128)(2,1)} %all-to-all-done.x_ref, f32[3,2,1024]{2,1,0:T(2,128)S(1)} %copy-done.3, f32[1,1024]{1,0:T(1,128)S(1)} %bitcast.8, bf16[512,256]{1,0:T(8,128)(2,1)S(1)} %copy-done.8, f32[32,1,256]{2,1,0:T(1,128)S(1)} %copy-done.10, f32[32,1,256]{2,1,0:T(1,128)S(1)} %copy-done.9, ...), custom_call_target="tpu_custom_call" | custom-call | flops 5000000000 | bytes 4194304 | tf_op jit(solution)/shard_map/convolve/pallas_call | solution.py:168
  68.9 21.8 %all_to_all.10.conv_ref = bf16[32,64,256]{2,1,0:T(8,128)(2,1)S(1)} all-to-all(bf16[32,64,256]{2,1,0:T(8,128)(2,1)S(1)} %convolve.1), channel_id=1, replica_groups=mesh['ctx'=32,'tp'=4] {'ctx'}, dimensions={0} | all-to-all | bytes 2097152 | tf_op jit(solution)/shard_map/all_to_all | solution.py:372
  90.7 1.8 %finish.1 = bf16[256,1024]{1,0:T(8,128)(2,1)} custom-call(f32[2,1024,256]{2,1,0:T(8,128)S(1)} %gate_mix.1.gates_ref, bf16[32,64,256]{2,1,0:T(8,128)(2,1)S(1)} %all_to_all.10.conv_ref), custom_call_target="tpu_custom_call" | custom-call | flops 1048576 | bytes 3670016 | tf_op jit(solution)/shard_map/finish/pallas_call | solution.py:338
  (10 shorter events, 0.0 us)
Async XLA Ops:
  0.0 15.2 %collective-permute-start.1 = (bf16[256,1024]{1,0:T(8,128)(2,1)}, bf16[256,1024]{1,0:T(8,128)(2,1)S(1)}, u32[]{:S(2)}, u32[]{:S(2)}) collective-permute-start(bf16[256,1024]{1,0:T(8,128)(2,1)} %refs_0_.2), channel_id=1, source_target_pairs={{0,2},{1,3},{2,0},{3,1},{4,6},{5,7},{6,4},{7,5},{8,10},{9,11},{10,... | collective-permute-start | bytes 1572872 | tf_op jit(solution)/shard_map/ppermute | solution.py:363
  3.1 12.1 %collective-permute-start = (bf16[256,1024]{1,0:T(8,128)(2,1)}, bf16[256,1024]{1,0:T(8,128)(2,1)S(1)}, u32[]{:S(2)}, u32[]{:S(2)}) collective-permute-start(bf16[256,1024]{1,0:T(8,128)(2,1)} %refs_0_.2), channel_id=1, source_target_pairs={{0,1},{1,0},{2,3},{3,2},{4,5},{5,4},{6,7},{7,6},{8,9},{9,8},{10,11... | collective-permute-start | bytes 1572872 | tf_op jit(solution)/shard_map/ppermute | solution.py:363
  3.1 1.2 %copy-start.2 = (f32[256,1024]{1,0:T(8,128)S(1)}, f32[256,1024]{1,0:T(8,128)}, u32[]{:S(2)}) copy-start(f32[256,1024]{1,0:T(8,128)} %filter_ref.1) | copy-start | bytes 3145732
  15.2 1.9 %collective-permute-start.2 = (bf16[256,1024]{1,0:T(8,128)(2,1)S(1)}, bf16[256,1024]{1,0:T(8,128)(2,1)S(1)}, u32[]{:S(2)}, u32[]{:S(2)}) collective-permute-start(bf16[256,1024]{1,0:T(8,128)(2,1)S(1)} %collective-permute-done.1.refs_2_), channel_id=1, source_target_pairs={{0,1},{1,0},{2,3},{3,2},{4,5},{5,4},{6,7},{7,6},{8,9},{9,8},{10,11... | collective-permute-start | bytes 1572872 | tf_op jit(solution)/shard_map/ppermute | solution.py:363
  17.1 1.0 %copy-start = (bf16[256,1024]{1,0:T(8,128)(2,1)S(1)}, bf16[256,1024]{1,0:T(8,128)(2,1)}, u32[]{:S(2)}) copy-start(bf16[256,1024]{1,0:T(8,128)(2,1)} %refs_0_.2) | copy-start | bytes 1572868
  27.4 9.9 %copy-start.1 = (bf16[256,1024]{1,0:T(8,128)(2,1)S(1)}, bf16[256,1024]{1,0:T(8,128)(2,1)}, u32[]{:S(2)}) copy-start(bf16[256,1024]{1,0:T(8,128)(2,1)} %refs_0_.2) | copy-start | bytes 1572868
  27.4 34.3 %all-to-all-start = ((bf16[32,96,256]{2,1,0:T(8,128)(2,1)}), bf16[32,96,256]{2,1,0:T(8,128)(2,1)}, u32[]{:S(2)}, u32[]{:S(2)}) async-start(bf16[32,96,256]{2,1,0:T(8,128)(2,1)} %project_values.1), calls=%async_computation | async-start | bytes 3145728 | tf_op jit(solution)/shard_map/all_to_all | solution.py:372
  37.4 20.4 %copy-start.3 = (f32[3,2,1024]{2,1,0:T(2,128)S(1)}, f32[3,2,1024]{2,1,0:T(2,128)}, u32[]{:S(2)}) copy-start(f32[3,2,1024]{2,1,0:T(2,128)} %taps_ref.3) | copy-start | bytes 73732
  45.4 16.4 %copy-start.4 = (f32[1024]{0:T(1024)S(1)}, f32[1024]{0:T(1024)}, u32[]{:S(2)}) copy-start(f32[1024]{0:T(1024)} %param.15) | copy-start | bytes 12292
  45.4 16.4 %copy-start.5 = (bf16[256,512]{1,0:T(8,128)(2,1)S(1)}, bf16[256,512]{1,0:T(8,128)(2,1)}, u32[]{:S(2)}) copy-start(bf16[256,512]{1,0:T(8,128)(2,1)} %constant.21.backward_ref) | copy-start | bytes 786436
  45.4 16.4 %copy-start.6 = (bf16[2,256,256]{2,1,0:T(8,128)(2,1)S(1)}, bf16[2,256,256]{2,1,0:T(8,128)(2,1)}, u32[]{:S(2)}) copy-start(bf16[2,256,256]{2,1,0:T(8,128)(2,1)} %constant.20.inner_back_ref) | copy-start | bytes 786436
  45.4 16.4 %copy-start.7 = (bf16[2,256,256]{2,1,0:T(8,128)(2,1)S(1)}, bf16[2,256,256]{2,1,0:T(8,128)(2,1)}, u32[]{:S(2)}) copy-start(bf16[2,256,256]{2,1,0:T(8,128)(2,1)} %constant.19.inner_ref) | copy-start | bytes 786436
  45.4 16.4 %copy-start.8 = (bf16[512,256]{1,0:T(8,128)(2,1)S(1)}, bf16[512,256]{1,0:T(8,128)(2,1)}, u32[]{:S(2)}) copy-start(bf16[512,256]{1,0:T(8,128)(2,1)} %constant.18.forward_ref) | copy-start | bytes 786436
  45.4 16.4 %copy-start.9 = (f32[32,1,256]{2,1,0:T(1,128)S(1)}, f32[32,1,256]{2,1,0:T(1,128)}, u32[]{:S(2)}) copy-start(f32[32,1,256]{2,1,0:T(1,128)} %constant.15.clone.sin_ref) | copy-start | bytes 98308
  45.4 16.3 %copy-start.10 = (f32[32,1,256]{2,1,0:T(1,128)S(1)}, f32[32,1,256]{2,1,0:T(1,128)}, u32[]{:S(2)}) copy-start(f32[32,1,256]{2,1,0:T(1,128)} %constant.14.clone.cos_ref) | copy-start | bytes 98308
  45.5 12.3 %collective-permute-start.4 = (bf16[16,1024]{1,0:T(8,128)(2,1)S(1)}, bf16[16,1024]{1,0:T(8,128)(2,1)S(1)}, u32[]{:S(2)}, u32[]{:S(2)}) collective-permute-start(bf16[16,1024]{1,0:T(8,128)(2,1)S(1)} %get-tuple-element.21), channel_id=1, source_target_pairs={{4,0},{8,4},{12,8},{16,12},{20,16},{24,20},{28,24},{32,28},{36,32}... | collective-permute-start | bytes 98312 | tf_op jit(solution)/shard_map/ppermute | solution.py:369
  46.9 10.9 %collective-permute-start.3 = (bf16[16,1024]{1,0:T(8,128)(2,1)S(1)}, bf16[16,1024]{1,0:T(8,128)(2,1)S(1)}, u32[]{:S(2)}, u32[]{:S(2)}) collective-permute-start(bf16[16,1024]{1,0:T(8,128)(2,1)S(1)} %get-tuple-element.22), channel_id=1, source_target_pairs={{0,4},{4,8},{8,12},{12,16},{16,20},{20,24},{24,28},{28,32},{32,36}... | collective-permute-start | bytes 98312 | tf_op jit(solution)/shard_map/ppermute | solution.py:366

commit v3 on v2

--- a/solution.py
+++ b/solution.py
@@ -15,6 +15,8 @@
 PACK = 16
 MIB = 1024 * 1024
 PROJECT_BYTES = 50 * MIB
+START_BYTES = 36 * MIB
+END_BYTES = 28 * MIB
 CONVOLVE_BYTES = 16 * MIB
 SMALL_BYTES = 10 * MIB
 
@@ -180,90 +182,77 @@
     return jnp.where(total == block - 1, 1.0, 0.0).astype(BF16)
 
 
-def project_kernel(
-    which, own_hbm, sib_hbm, far_hbm, farsib_hbm, w_hbm, filter_hbm, out_ref, left_ref, raw_ref, total_ref, part_sems, w_sems, filter_sem
+def flip_into(dst, src, swap):
+    block = swap.shape[0]
+    count = src.shape[1] // block
+    for b in range(count):
+        piece = mm(src[:, (count - 1 - b) * block : (count - b) * block], swap)
+        dst[:, b * block : (b + 1) * block] = piece.astype(BF16)
+
+
+def picked(raw_ref, k, depth, width, first, count, which):
+    tiles = width // LANES
+    weights = [
+        raw_ref[k, pl.ds(2 * tile + which, depth, stride=2 * tiles), :]
+        for tile in range(first // LANES, (first + count) // LANES)
+    ]
+    return jnp.concatenate(weights, 1)
+
+
+def weight_copies(w_hbm, raw_ref, sems):
+    chunk = raw_ref.shape[1]
+    tp = lax.axis_index("tp")
+    return [
+        pltpu.make_async_copy(
+            w_hbm.at[pl.ds(pl.multiple_of((tp ^ k) * chunk, chunk), chunk)], raw_ref.at[k], sems.at[k]
+        )
+        for k in range(4)
+    ]
+
+
+def project_gates_kernel(
+    own_hbm, sib_hbm, far_hbm, farsib_hbm, w_hbm, out_ref, left_ref, raw_ref, total_ref, part_sems, w_sems
 ):
     _, rows2, depth = left_ref.shape
     rows = rows2 // 2
     width = total_ref.shape[1]
-    tiles = width // LANES
     block = min(256, width)
-    chunk = raw_ref.shape[1]
-    tp = lax.axis_index("tp")
     part_copies = [
         pltpu.make_async_copy(src, left_ref.at[k, :rows], part_sems.at[k])
         for k, src in enumerate((own_hbm, sib_hbm, far_hbm, farsib_hbm))
     ]
-    w_copies = [
-        pltpu.make_async_copy(
-            w_hbm.at[pl.ds(pl.multiple_of((tp ^ k) * chunk, chunk), chunk)], raw_ref.at[k], w_sems.at[k]
-        )
-        for k in range(4)
-    ]
+    w_copies = weight_copies(w_hbm, raw_ref, w_sems)
     w_copies[0].start()
     for copy in part_copies:
         copy.start()
     for copy in w_copies[1:]:
         copy.start()
-    if filter_hbm is not None:
-        slice_width = filter_hbm.shape[1]
-        filter_copy = pltpu.make_async_copy(filter_hbm, out_ref.at[:, 2 * slice_width :], filter_sem)
-        filter_copy.start()
     for copy in part_copies:
         copy.wait()
     swap = swap_matrix(block)
-    count = depth // block
     for k in range(4):
-        other = left_ref[3 - k, :rows]
-        for b in range(count):
-            piece = mm(other[:, (count - 1 - b) * block : (count - b) * block], swap)
-            left_ref[k, rows:, b * block : (b + 1) * block] = piece.astype(BF16)
+        flip_into(left_ref.at[k, rows:], left_ref[3 - k, :rows], swap)
     for k in range(4):
         w_copies[k].wait()
         left = left_ref[k]
-        for b in range(width // block):
-            cols = slice(b * block, (b + 1) * block)
-            weights = [
-                raw_ref[k, pl.ds(2 * tile + which, depth, stride=2 * tiles), :]
-                for tile in range(b * block // LANES, (b + 1) * block // LANES)
-            ]
-            term = mm(left, jnp.concatenate(weights, 1))
+        for first in range(0, width, block):
+            cols = slice(first, first + block)
+            term = mm(left, picked(raw_ref, k, depth, width, first, block, 0))
             if k == 0:
                 total_ref[:, cols] = term
             elif k < 3:
                 total_ref[:, cols] += term
             else:
-                total = total_ref[:, cols] + term
-                if filter_hbm is not None:
-                    turned = total.T.astype(BF16)
-                    per = block // slice_width
-                    for d in range(per):
-                        part = turned[d * slice_width : (d + 1) * slice_width]
-                        out_ref[b * per + d, :slice_width] = part[:, :rows]
-                        out_ref[b * per + d, slice_width : 2 * slice_width] = part[:, rows:]
-                else:
-                    out_ref[:, cols] = total.astype(BF16)
-    if filter_hbm is not None:
-        filter_copy.wait()
-
-
-def project(parts, weight_rows, which, width, filter_rows=None):
+                out_ref[:, cols] = (total_ref[:, cols] + term).astype(BF16)
+
+
+def project_gates(parts, weight_rows, width):
     rows, depth = parts[0].shape
     tiles = width // LANES
     model = weight_rows.shape[0] // (2 * tiles)
-    extra = () if filter_rows is None else (filter_rows,)
-    if extra:
-        out_shape = (filter_rows.shape[0], 3 * filter_rows.shape[1], rows)
-    else:
-        out_shape = (2 * rows, width)
-
-    def kernel(*refs):
-        filter_hbm = refs[5] if extra else None
-        project_kernel(which, *refs[:5], filter_hbm, *refs[5 + len(extra) :])
-
-    return pl.pallas_call(
-        kernel,
-        in_specs=[pl.BlockSpec(memory_space=pl.ANY)] * (5 + len(extra)),
+    return pl.pallas_call(
+        project_gates_kernel,
+        in_specs=[pl.BlockSpec(memory_space=pl.ANY)] * 5,
         out_specs=pl.BlockSpec(memory_space=pltpu.VMEM),
         scratch_shapes=[
             pltpu.VMEM((4, 2 * rows, depth), BF16),
@@ -271,13 +260,132 @@
             pltpu.VMEM((2 * rows, width), F32),
             pltpu.SemaphoreType.DMA((4,)),
             pltpu.SemaphoreType.DMA((4,)),
+        ],
+        out_shape=jax.ShapeDtypeStruct((2 * rows, width), BF16),
+        compiler_params=params(PROJECT_BYTES),
+        cost_estimate=cost(4 * rows * model * width, 4 * model * width),
+        name="project_gates",
+    )(*parts, weight_rows)
+
+
+def start_values_kernel(own_hbm, sib_hbm, w_hbm, total_ref, flat_hbm, left_ref, raw_ref, flat_ref, part_sems, w_sems, flat_sems):
+    _, rows, depth = left_ref.shape
+    width = total_ref.shape[1]
+    block = min(256, width)
+    part_copies = [
+        pltpu.make_async_copy(src, left_ref.at[k], part_sems.at[k]) for k, src in enumerate((own_hbm, sib_hbm))
+    ]
+    w_copies = weight_copies(w_hbm, raw_ref, w_sems)
+    flat_copies = [
+        pltpu.make_async_copy(flat_ref.at[k], flat_hbm.at[k], flat_sems.at[k]) for k in range(4)
+    ]
+    w_copies[0].start()
+    for copy in part_copies:
+        copy.start()
+    for copy in w_copies[1:]:
+        copy.start()
+    for copy in part_copies:
+        copy.wait()
+    swap = swap_matrix(block)
+    for k in range(2):
+        flip_into(left_ref.at[3 - k], left_ref[k], swap)
+    for k in range(4):
+        w_copies[k].wait()
+        left = left_ref[k]
+        here = slice(0, rows) if k < 2 else slice(rows, 2 * rows)
+        for first in range(0, width, block):
+            cols = slice(first, first + block)
+            weights = picked(raw_ref, k, depth, width, first, block, 1)
+            flat_ref[k, :, cols] = weights
+            term = mm(left, weights)
+            if k % 2 == 0:
+                total_ref[here, cols] = term
+            else:
+                total_ref[here, cols] += term
+        flat_copies[k].start()
+    for copy in flat_copies:
+        copy.wait()
+
+
+def start_values(own, sib, weight_rows, width):
+    rows, depth = own.shape
+    tiles = width // LANES
+    any_space = pl.BlockSpec(memory_space=pl.ANY)
+    return pl.pallas_call(
+        start_values_kernel,
+        in_specs=[any_space] * 3,
+        out_specs=[pl.BlockSpec(memory_space=pltpu.VMEM), any_space],
+        scratch_shapes=[
+            pltpu.VMEM((4, rows, depth), BF16),
+            pltpu.VMEM((4, depth * 2 * tiles, LANES), BF16),
+            pltpu.VMEM((4, depth, width), BF16),
+            pltpu.SemaphoreType.DMA((2,)),
+            pltpu.SemaphoreType.DMA((4,)),
+            pltpu.SemaphoreType.DMA((4,)),
+        ],
+        out_shape=[
+            jax.ShapeDtypeStruct((2 * rows, width), F32),
+            jax.ShapeDtypeStruct((4, depth, width), BF16),
+        ],
+        compiler_params=params(START_BYTES),
+        cost_estimate=cost(8 * rows * depth * width, 24 * depth * width),
+        name="start_values",
+    )(own, sib, weight_rows)
+
+
+def end_values_kernel(far_ref, farsib_ref, total_ref, flat_hbm, filter_hbm, out_ref, left_ref, flat_ref, flat_sems, filter_sem):
+    _, rows, depth = left_ref.shape
+    width = total_ref.shape[1]
+    block = min(256, width)
+    slice_width = filter_hbm.shape[1]
+    per = block // slice_width
+    order = (2, 3, 1, 0)
+    flat_copies = {
+        k: pltpu.make_async_copy(flat_hbm.at[k], flat_ref.at[k], flat_sems.at[k]) for k in order
+    }
+    filter_copy = pltpu.make_async_copy(filter_hbm, out_ref.at[:, 2 * slice_width :], filter_sem)
+    for k in order:
+        flat_copies[k].start()
+    filter_copy.start()
+    swap = swap_matrix(block)
+    flip_into(left_ref.at[0], farsib_ref[...], swap)
+    flip_into(left_ref.at[1], far_ref[...], swap)
+    for strand in range(2):
+        here = slice(strand * rows, (strand + 1) * rows)
+        one, two = (2, 3) if strand == 0 else (1, 0)
+        left_one, left_two = (far_ref[...], farsib_ref[...]) if strand == 0 else (left_ref[1], left_ref[0])
+        flat_copies[one].wait()
+        flat_copies[two].wait()
+        for b in range(width // block):
+            cols = slice(b * block, (b + 1) * block)
+            total = total_ref[here, cols] + mm(left_one, flat_ref[one, :, cols]) + mm(left_two, flat_ref[two, :, cols])
+            turned = total.T.astype(BF16)
+            for d in range(per):
+                out_ref[b * per + d, strand * slice_width : (strand + 1) * slice_width] = turned[
+                    d * slice_width : (d + 1) * slice_width
+                ]
+    filter_copy.wait()
+
+
+def end_values(far, farsib, total, flat, filter_rows):
+    rows, depth = far.shape
+    vmem = pl.BlockSpec(memory_space=pltpu.VMEM)
+    any_space = pl.BlockSpec(memory_space=pl.ANY)
+    return pl.pallas_call(
+        end_values_kernel,
+        in_specs=[vmem] * 3 + [any_space] * 2,
+        out_specs=vmem,
+        scratch_shapes=[
+            pltpu.VMEM((2, rows, depth), BF16),
+            pltpu.VMEM(flat.shape, BF16),
+            pltpu.SemaphoreType.DMA((4,)),
             pltpu.SemaphoreType.DMA,
         ],
-        out_shape=jax.ShapeDtypeStruct(out_shape, BF16),
-        compiler_params=params(PROJECT_BYTES),
-        cost_estimate=cost(4 * rows * model * width, 4 * model * width),
-        name="project_values" if extra else "project_gates",
-    )(*parts, weight_rows, *extra)
+        out_shape=jax.ShapeDtypeStruct((filter_rows.shape[0], 3 * filter_rows.shape[1], rows), BF16),
+        compiler_params=params(END_BYTES),
+        cost_estimate=cost(8 * rows * depth * total.shape[1], 8 * depth * total.shape[1]),
+        name="end_values",
+    )(far, farsib, total, flat, filter_rows)
 
 
 def gate_mix_kernel(gates_ref, below_ref, above_ref, taps_ref, out_ref):
@@ -375,13 +483,13 @@
     far = to_tp(tokens, 2)
     sib = to_tp(tokens, 1)
     filter_rows = filter_prep(long_filter).reshape(ctx_count, slice_width, rows)
-    far, filter_rows = lax.optimization_barrier((far, filter_rows))
+    total, flat = start_values(tokens, sib, weight_rows, width)
+    far, filter_rows, total, flat = lax.optimization_barrier((far, filter_rows, total, flat))
     farsib = to_tp(far, 1)
-    parts = (tokens, sib, far, farsib)
-    values = project(parts, weight_rows, 1, width, filter_rows)
+    values = end_values(far, farsib, total, flat, filter_rows)
     columns = exchange(values)
-    parts, _ = lax.optimization_barrier((parts, values))
-    gates = project(parts, weight_rows, 0, width)
+    parts, _ = lax.optimization_barrier(((tokens, sib, far, farsib), values))
+    gates = project_gates(parts, weight_rows, width)
     below, above = to_next(gates[rows - 16 : rows]), to_previous(gates[rows : rows + 16])
     mixed = gate_mix(gates, below, above, short_kernel)
     columns, mixed = lax.optimization_barrier((columns, mixed))

time: 93 us -> 88.4 us (0.951)
  waiting for transfers between devices: 21.4 us -> 12.7 us
  Pallas kernels: 27.8 us -> 32.2 us
    ppermute x3, waiting for transfers between devices: 12.4 us -> 3.68 us  [to_tp(): return lax.ppermute(x, 'tp', [(i, i ^ bits) for i in range(tp_count)])]
    pallas_call x2 -> x3, Pallas kernels: 17.2 us -> 21.4 us  [the longest x1 8.49 us: start_values(): pl.pallas_call(start_values_kernel, in_specs=[any_space] * 3, out_specs=[...]
  transfers between devices with their start and end apart: 6 -> 6, of which waited for: 4 -> 4; matrix products, arithmetic and copies ran while one was open for 0% -> 0% of each run, Pallas kernels for 10% -> 21%
where the time goes in v3:
time: 88.4 us; the launch traced here: 88 us
  Pallas kernels  32.2 us (36%)
  blocking collectives  21.8 us (25%)
  starting transfers between devices  18.9 us (21%)
  waiting for transfers between devices  12.7 us (14%)
  local copies, waits for them, and re-layouts  2.33 us (3%)
    all_to_all x1, blocking collectives, exchange(): return lax.all_to_all(x, 'ctx', split_axis=0, concat_axis=0, tiled=True)  21.8 us
    all_to_all x1, starting transfers between devices, exchange(): return lax.all_to_all(x, 'ctx', split_axis=0, concat_axis=0, tiled=True)  9.78 us
    pallas_call x1, Pallas kernels, start_values(): pl.pallas_call(start_values_kernel, in_specs=[any_space] * 3, out_specs=[...  8.49 us
    pallas_call x1, Pallas kernels, project_gates(): pl.pallas_call(project_gates_kernel, in_specs=[pl.BlockSpec(memory_space=...  7.96 us
    pallas_call x1, Pallas kernels, convolve(): pl.pallas_call(convolve_kernel, out_shape=jax.ShapeDtypeStruct((blocks, 2...  7.27 us
    ppermute x1, waiting for transfers between devices, to_previous(): return lax.ppermute(x, 'ctx', [(i + 1, i) for i in range(ctx_count - 1)])  6.32 us
    pallas_call x1, Pallas kernels, end_values(): pl.pallas_call(end_values_kernel, in_specs=[vmem] * 3 + [any_space] * 2,...  4.94 us
    ppermute x1, starting transfers between devices, to_next(): return lax.ppermute(x, 'ctx', [(i, i + 1) for i in range(ctx_count - 1)])  4.55 us
  transfers between devices with their start and end apart: 6, of which 4 were waited for; matrix products, arithmetic and copies ran while one was open for 0% of the time, Pallas kernels for 21%

profile of v3, /device:TPU:0, one launch (start us, length us, event | category | flops | bytes accessed | tf_op | source)
XLA Modules:
  0.0 88.0 jit_solution(15607929559460473693)
XLA Ops:
  0.0 0.0 collective-permute-start.1
  0.0 3.1 %collective-permute-start = (bf16[256,1024]{1,0:T(8,128)(2,1)}, bf16[256,1024]{1,0:T(8,128)(2,1)S(1)}, u32[]{:S(2)}, u32[]{:S(2)}) collective-permute-start(bf16[256,1024]{1,0:T(8,128)(2,1)} %own_hbm.2), channel_id=1, source_target_pairs={{0,2},{1,3},{2,0},{3,1},{4,6},{5,7},{6,4},{7,5},{8,10},{9,11},{10,... | collective-permute-start | bytes 1572872 | tf_op jit(solution)/shard_map/ppermute | solution.py:471
  3.1 1.2 %copy-done.2 = f32[256,1024]{1,0:T(8,128)S(1)} copy-done((f32[256,1024]{1,0:T(8,128)S(1)}, f32[256,1024]{1,0:T(8,128)}, u32[]{:S(2)}) %copy-start.2) | copy-done | bytes 1048600
  4.3 0.4 filter_prep.1
  4.7 0.0 collective-permute-done.1.sib_hbm
  4.7 0.0 copy-start
  4.8 1.0 %copy-done = bf16[256,1024]{1,0:T(8,128)(2,1)S(1)} copy-done((bf16[256,1024]{1,0:T(8,128)(2,1)S(1)}, bf16[256,1024]{1,0:T(8,128)(2,1)}, u32[]{:S(2)}) %copy-start) | copy-done | bytes 524312
  5.8 8.5 %start_values.1 = (f32[512,1024]{1,0:T(8,128)S(1)}, bf16[4,1024,1024]{2,1,0:T(8,128)(2,1)S(1)}) custom-call(bf16[256,1024]{1,0:T(8,128)(2,1)S(1)} %copy-done, bf16[256,1024]{1,0:T(8,128)(2,1)S(1)} %collective-permute-done.1.sib_hbm, bf16[65536,128]{1,0:T(8,128)(2,1)} %bitcast.9), custom_call_target="tpu_custom_call" | custom-call | flops 2147483648 | bytes 25165824 | tf_op jit(solution)/shard_map/start_values/pallas_call | solution.py:314
  14.3 1.8 %collective-permute-done.far_ref.far_hbm = bf16[256,1024]{1,0:T(8,128)(2,1)S(1)} collective-permute-done((bf16[256,1024]{1,0:T(8,128)(2,1)}, bf16[256,1024]{1,0:T(8,128)(2,1)S(1)}, u32[]{:S(2)}, u32[]{:S(2)}) %collective-permute-start) | collective-permute-done | bytes 524320 | tf_op jit(solution)/shard_map/ppermute | solution.py:471
  16.1 0.0 collective-permute-start.2
  16.1 1.9 %collective-permute-done.2.farsib_ref.farsib_hbm = bf16[256,1024]{1,0:T(8,128)(2,1)S(1)} collective-permute-done((bf16[256,1024]{1,0:T(8,128)(2,1)S(1)}, bf16[256,1024]{1,0:T(8,128)(2,1)S(1)}, u32[]{:S(2)}, u32[]{:S(2)}) %collective-permute-start.2) | collective-permute-done | bytes 524320 | tf_op jit(solution)/shard_map/ppermute | solution.py:471
  18.0 4.9 %end_values.1 = bf16[32,96,256]{2,1,0:T(8,128)(2,1)} custom-call(bf16[256,1024]{1,0:T(8,128)(2,1)S(1)} %collective-permute-done.far_ref.far_hbm, bf16[256,1024]{1,0:T(8,128)(2,1)S(1)} %collective-permute-done.2.farsib_ref.farsib_hbm, f32[512,1024]{1,0:T(8,128)S(1)} %get-tuple-element.20.total_ref, bf16[4,1024,1024]{2,1,0:T(8,128)(2,1)S(1)} %get-tuple-element.21.flat_hbm, ...), custom_call_target="tpu_custom_call" | custom-call | flops 2147483648 | bytes 8388608 | tf_op jit(solution)/shard_map/end_values/pallas_call | solution.py:374
  22.9 0.0 copy-start.1
  22.9 9.8 %all-to-all-start = ((bf16[32,96,256]{2,1,0:T(8,128)(2,1)}), bf16[32,96,256]{2,1,0:T(8,128)(2,1)}, u32[]{:S(2)}, u32[]{:S(2)}) async-start(bf16[32,96,256]{2,1,0:T(8,128)(2,1)} %end_values.1), calls=%async_computation | async-start | bytes 3145728 | tf_op jit(solution)/shard_map/all_to_all | solution.py:480
  32.7 0.0 copy-start.3
  32.7 8.0 %project_gates.1.gates_ref = bf16[512,1024]{1,0:T(8,128)(2,1)S(1)} custom-call(bf16[256,1024]{1,0:T(8,128)(2,1)S(1)} %copy-done.1, bf16[256,1024]{1,0:T(8,128)(2,1)S(1)} %collective-permute-done.1.sib_hbm, bf16[256,1024]{1,0:T(8,128)(2,1)S(1)} %collective-permute-done.far_ref.far_hbm, bf16[256,1024]{1,0:T(8,128)(2,1)S(1)} %collective-permute-done.2.farsib_ref.farsib_hbm, ...), custom_call_target="tpu_custom_call" | custom-call | flops 4294967296 | bytes 16777216 | tf_op jit(solution)/shard_map/project_gates/pallas_call | solution.py:253
  40.7 0.0 copy-start.4
  40.7 0.0 copy-start.5
  40.7 0.0 copy-start.6
  40.7 0.0 copy-start.7
  40.8 0.0 copy-start.8
  40.8 0.0 copy-start.9
  40.8 0.0 copy-start.10
  40.8 1.4 %collective-permute-start.4 = (bf16[16,1024]{1,0:T(8,128)(2,1)S(1)}, bf16[16,1024]{1,0:T(8,128)(2,1)S(1)}, u32[]{:S(2)}, u32[]{:S(2)}) collective-permute-start(bf16[16,1024]{1,0:T(8,128)(2,1)S(1)} %get-tuple-element.29), channel_id=1, source_target_pairs={{4,0},{8,4},{12,8},{16,12},{20,16},{24,20},{28,24},{32,28},{36,32}... | collective-permute-start | bytes 98312 | tf_op jit(solution)/shard_map/ppermute | solution.py:477
  42.2 4.5 %collective-permute-start.3 = (bf16[16,1024]{1,0:T(8,128)(2,1)S(1)}, bf16[16,1024]{1,0:T(8,128)(2,1)S(1)}, u32[]{:S(2)}, u32[]{:S(2)}) collective-permute-start(bf16[16,1024]{1,0:T(8,128)(2,1)S(1)} %get-tuple-element.30), channel_id=1, source_target_pairs={{0,4},{4,8},{8,12},{12,16},{16,20},{20,24},{24,28},{28,32},{32,36}... | collective-permute-start | bytes 98312 | tf_op jit(solution)/shard_map/ppermute | solution.py:474
  46.8 6.3 %collective-permute-done.4.above_ref = bf16[16,1024]{1,0:T(8,128)(2,1)S(1)} collective-permute-done((bf16[16,1024]{1,0:T(8,128)(2,1)S(1)}, bf16[16,1024]{1,0:T(8,128)(2,1)S(1)}, u32[]{:S(2)}, u32[]{:S(2)}) %collective-permute-start.4) | collective-permute-done | bytes 32800 | tf_op jit(solution)/shard_map/ppermute | solution.py:477
  53.1 0.0 collective-permute-done.3.below_ref
  53.1 1.3 %gate_mix.1.gates_ref = f32[2,1024,256]{2,1,0:T(8,128)S(1)} custom-call(bf16[512,1024]{1,0:T(8,128)(2,1)S(1)} %project_gates.1.gates_ref, bf16[16,1024]{1,0:T(8,128)(2,1)S(1)} %collective-permute-done.3.below_ref, bf16[16,1024]{1,0:T(8,128)(2,1)S(1)} %collective-permute-done.4.above_ref, f32[3,2,1024]{2,1,0:T(2,128)S(1)} %copy-done.3), custom_call_target="tpu_custom_call" | custom-call | flops 4194304 | bytes 3145728 | tf_op jit(solution)/shard_map/gate_mix/pallas_call | solution.py:417
  54.4 2.7 %all-to-all-done.x_ref = bf16[32,96,256]{2,1,0:T(8,128)(2,1)} async-done(((bf16[32,96,256]{2,1,0:T(8,128)(2,1)}), bf16[32,96,256]{2,1,0:T(8,128)(2,1)}, u32[]{:S(2)}, u32[]{:S(2)}) %all-to-all-start) | async-done | bytes 1572896 | tf_op jit(solution)/shard_map/all_to_all | solution.py:480
  57.2 7.3 %convolve.1 = bf16[32,64,256]{2,1,0:T(8,128)(2,1)S(1)} custom-call(bf16[32,96,256]{2,1,0:T(8,128)(2,1)} %all-to-all-done.x_ref, f32[3,2,1024]{2,1,0:T(2,128)S(1)} %copy-done.3, f32[1,1024]{1,0:T(1,128)S(1)} %bitcast.8, bf16[512,256]{1,0:T(8,128)(2,1)S(1)} %copy-done.8, f32[32,1,256]{2,1,0:T(1,128)S(1)} %copy-done.10, f32[32,1,256]{2,1,0:T(1,128)S(1)} %copy-done.9, ...), custom_call_target="tpu_custom_call" | custom-call | flops 5000000000 | bytes 4194304 | tf_op jit(solution)/shard_map/convolve/pallas_call | solution.py:170
  64.4 21.8 %all_to_all.10.conv_ref = bf16[32,64,256]{2,1,0:T(8,128)(2,1)S(1)} all-to-all(bf16[32,64,256]{2,1,0:T(8,128)(2,1)S(1)} %convolve.1), channel_id=1, replica_groups=mesh['ctx'=32,'tp'=4] {'ctx'}, dimensions={0} | all-to-all | bytes 2097152 | tf_op jit(solution)/shard_map/all_to_all | solution.py:480
  86.2 1.8 %finish.1 = bf16[256,1024]{1,0:T(8,128)(2,1)} custom-call(f32[2,1024,256]{2,1,0:T(8,128)S(1)} %gate_mix.1.gates_ref, bf16[32,64,256]{2,1,0:T(8,128)(2,1)S(1)} %all_to_all.10.conv_ref), custom_call_target="tpu_custom_call" | custom-call | flops 1048576 | bytes 3670016 | tf_op jit(solution)/shard_map/finish/pallas_call | solution.py:446
  (11 shorter events, 0.0 us)
Async XLA Ops:
  0.0 4.7 %collective-permute-start.1 = (bf16[256,1024]{1,0:T(8,128)(2,1)}, bf16[256,1024]{1,0:T(8,128)(2,1)S(1)}, u32[]{:S(2)}, u32[]{:S(2)}) collective-permute-start(bf16[256,1024]{1,0:T(8,128)(2,1)} %own_hbm.2), channel_id=1, source_target_pairs={{0,1},{1,0},{2,3},{3,2},{4,5},{5,4},{6,7},{7,6},{8,9},{9,8},{10,11... | collective-permute-start | bytes 1572872 | tf_op jit(solution)/shard_map/ppermute | solution.py:471
  0.0 16.1 %collective-permute-start = (bf16[256,1024]{1,0:T(8,128)(2,1)}, bf16[256,1024]{1,0:T(8,128)(2,1)S(1)}, u32[]{:S(2)}, u32[]{:S(2)}) collective-permute-start(bf16[256,1024]{1,0:T(8,128)(2,1)} %own_hbm.2), channel_id=1, source_target_pairs={{0,2},{1,3},{2,0},{3,1},{4,6},{5,7},{6,4},{7,5},{8,10},{9,11},{10,... | collective-permute-start | bytes 1572872 | tf_op jit(solution)/shard_map/ppermute | solution.py:471
  3.1 1.2 %copy-start.2 = (f32[256,1024]{1,0:T(8,128)S(1)}, f32[256,1024]{1,0:T(8,128)}, u32[]{:S(2)}) copy-start(f32[256,1024]{1,0:T(8,128)} %filter_ref.1) | copy-start | bytes 3145732
  4.7 1.0 %copy-start = (bf16[256,1024]{1,0:T(8,128)(2,1)S(1)}, bf16[256,1024]{1,0:T(8,128)(2,1)}, u32[]{:S(2)}) copy-start(bf16[256,1024]{1,0:T(8,128)(2,1)} %own_hbm.2) | copy-start | bytes 1572868
  16.1 1.9 %collective-permute-start.2 = (bf16[256,1024]{1,0:T(8,128)(2,1)S(1)}, bf16[256,1024]{1,0:T(8,128)(2,1)S(1)}, u32[]{:S(2)}, u32[]{:S(2)}) collective-permute-start(bf16[256,1024]{1,0:T(8,128)(2,1)S(1)} %collective-permute-done.far_ref.far_hbm), channel_id=1, source_target_pairs={{0,1},{1,0},{2,3},{3,2},{4,5},{5,4},{6,7},{7,6},{8,9},{9,8},{10,11... | collective-permute-start | bytes 1572872 | tf_op jit(solution)/shard_map/ppermute | solution.py:471
  22.9 9.8 %copy-start.1 = (bf16[256,1024]{1,0:T(8,128)(2,1)S(1)}, bf16[256,1024]{1,0:T(8,128)(2,1)}, u32[]{:S(2)}) copy-start(bf16[256,1024]{1,0:T(8,128)(2,1)} %own_hbm.2) | copy-start | bytes 1572868
  22.9 34.2 %all-to-all-start = ((bf16[32,96,256]{2,1,0:T(8,128)(2,1)}), bf16[32,96,256]{2,1,0:T(8,128)(2,1)}, u32[]{:S(2)}, u32[]{:S(2)}) async-start(bf16[32,96,256]{2,1,0:T(8,128)(2,1)} %end_values.1), calls=%async_computation | async-start | bytes 3145728 | tf_op jit(solution)/shard_map/all_to_all | solution.py:480
  32.7 20.4 %copy-start.3 = (f32[3,2,1024]{2,1,0:T(2,128)S(1)}, f32[3,2,1024]{2,1,0:T(2,128)}, u32[]{:S(2)}) copy-start(f32[3,2,1024]{2,1,0:T(2,128)} %taps_ref.3) | copy-start | bytes 73732
  40.7 16.4 %copy-start.4 = (f32[1024]{0:T(1024)S(1)}, f32[1024]{0:T(1024)}, u32[]{:S(2)}) copy-start(f32[1024]{0:T(1024)} %param.15) | copy-start | bytes 12292
  40.7 16.4 %copy-start.5 = (bf16[256,512]{1,0:T(8,128)(2,1)S(1)}, bf16[256,512]{1,0:T(8,128)(2,1)}, u32[]{:S(2)}) copy-start(bf16[256,512]{1,0:T(8,128)(2,1)} %constant.21.backward_ref) | copy-start | bytes 786436
  40.7 16.4 %copy-start.6 = (bf16[2,256,256]{2,1,0:T(8,128)(2,1)S(1)}, bf16[2,256,256]{2,1,0:T(8,128)(2,1)}, u32[]{:S(2)}) copy-start(bf16[2,256,256]{2,1,0:T(8,128)(2,1)} %constant.20.inner_back_ref) | copy-start | bytes 786436
  40.7 16.4 %copy-start.7 = (bf16[2,256,256]{2,1,0:T(8,128)(2,1)S(1)}, bf16[2,256,256]{2,1,0:T(8,128)(2,1)}, u32[]{:S(2)}) copy-start(bf16[2,256,256]{2,1,0:T(8,128)(2,1)} %constant.19.inner_ref) | copy-start | bytes 786436
  40.8 16.4 %copy-start.8 = (bf16[512,256]{1,0:T(8,128)(2,1)S(1)}, bf16[512,256]{1,0:T(8,128)(2,1)}, u32[]{:S(2)}) copy-start(bf16[512,256]{1,0:T(8,128)(2,1)} %constant.18.forward_ref) | copy-start | bytes 786436
  40.8 16.4 %copy-start.9 = (f32[32,1,256]{2,1,0:T(1,128)S(1)}, f32[32,1,256]{2,1,0:T(1,128)}, u32[]{:S(2)}) copy-start(f32[32,1,256]{2,1,0:T(1,128)} %constant.15.clone.sin_ref) | copy-start | bytes 98308
  40.8 16.4 %copy-start.10 = (f32[32,1,256]{2,1,0:T(1,128)S(1)}, f32[32,1,256]{2,1,0:T(1,128)}, u32[]{:S(2)}) copy-start(f32[32,1,256]{2,1,0:T(1,128)} %constant.14.clone.cos_ref) | copy-start | bytes 98308
  40.8 12.3 %collective-permute-start.4 = (bf16[16,1024]{1,0:T(8,128)(2,1)S(1)}, bf16[16,1024]{1,0:T(8,128)(2,1)S(1)}, u32[]{:S(2)}, u32[]{:S(2)}) collective-permute-start(bf16[16,1024]{1,0:T(8,128)(2,1)S(1)} %get-tuple-element.29), channel_id=1, source_target_pairs={{4,0},{8,4},{12,8},{16,12},{20,16},{24,20},{28,24},{32,28},{36,32}... | collective-permute-start | bytes 98312 | tf_op jit(solution)/shard_map/ppermute | solution.py:477
  42.2 10.9 %collective-permute-start.3 = (bf16[16,1024]{1,0:T(8,128)(2,1)S(1)}, bf16[16,1024]{1,0:T(8,128)(2,1)S(1)}, u32[]{:S(2)}, u32[]{:S(2)}) collective-permute-start(bf16[16,1024]{1,0:T(8,128)(2,1)S(1)} %get-tuple-element.30), channel_id=1, source_target_pairs={{0,4},{4,8},{8,12},{12,16},{16,20},{20,24},{24,28},{28,32},{32,36}... | collective-permute-start | bytes 98312 | tf_op jit(solution)/shard_map/ppermute | solution.py:474

commit v4 on v3

--- a/solution.py
+++ b/solution.py
@@ -16,7 +16,7 @@
 MIB = 1024 * 1024
 PROJECT_BYTES = 50 * MIB
 START_BYTES = 36 * MIB
-END_BYTES = 28 * MIB
+END_BYTES = 20 * MIB
 CONVOLVE_BYTES = 16 * MIB
 SMALL_BYTES = 10 * MIB
 
@@ -66,25 +66,22 @@
     return wide(cos_ref), wide(sin_ref)
 
 
-def columns_of(x_ref, pack):
-    blocks, _, rows = x_ref.shape
-    x = x_ref[:, pack * PACK : (pack + 1) * PACK, :].astype(F32)
+def columns_of(x):
+    blocks, _, rows = x.shape
     return [x[:, h * GROUP : (h + 1) * GROUP].reshape(blocks * GROUP, rows).astype(BF16) for h in range(2)]
 
 
-def spectrum(x, forward, turn_cos, turn_sin, inner):
-    count = x.shape[0]
-    half = x.shape[1] // 2
-    mixed = mm(forward, x)
-    real, imag = mixed[:count], mixed[count:]
-    turned_real = real * turn_cos + imag * turn_sin
-    turned_imag = imag * turn_cos - real * turn_sin
-    result = []
-    for odd in (0, 1):
-        sign = -1.0 if odd else 1.0
-        parts = [(t[:, :half] + sign * t[:, half:]).astype(BF16) for t in (turned_real, turned_imag)]
-        result.append(mm(jnp.concatenate(parts, 1), inner[odd]))
-    return result
+def spectrum(xs, forward, turn_cos, turn_sin, inner):
+    count, rows = xs[0].shape
+    half = rows // 2
+    near, far = [], []
+    for x in xs:
+        mixed = mm(forward, x)
+        real, imag = mixed[:count], mixed[count:]
+        turned = (real * turn_cos + imag * turn_sin, imag * turn_cos - real * turn_sin)
+        near.append(jnp.concatenate([(t[:, :half] + t[:, half:]).astype(BF16) for t in turned], 1))
+        far.append(jnp.concatenate([(t[:, :half] - t[:, half:]).astype(BF16) for t in turned], 1))
+    return [mm(jnp.concatenate(parts, 0), inner[odd]) for odd, parts in enumerate((near, far))]
 
 
 def filter_prep_kernel(filter_ref, out_ref):
@@ -106,55 +103,68 @@
     )(long_filter)
 
 
-def filter_spectrum(x_ref, at, taps_ref, skip_ref, forward_ref, turn_cos, turn_sin, inner_ref, out_ref):
-    blocks, _, rows = x_ref.shape
-    width = GROUP * out_ref.shape[0]
+def filter_spectrum(x, taps, skip, forward, turn_cos, turn_sin, inner):
+    rows = x.shape[2]
+    position = lax.broadcasted_iota(jnp.int32, (PACK, rows), 1)
+    first = x[:1] + jnp.where(position == 0, skip, 0.0)[None]
+    x = jnp.concatenate([first, x[1:]], 0)
+    total = taps[0][None] * x
+    for tap in (1, 2):
+        moved = pltpu.roll(x, tap, 2)
+        before = jnp.concatenate([jnp.zeros((1, PACK, rows), F32), moved[:-1]], 0)
+        total = total + taps[tap][None] * jnp.where((position < tap)[None], before, moved)
+    return spectrum(columns_of(total), forward, turn_cos, turn_sin, inner)
+
+
+def convolve_kernel(
+    taps_ref, skip_ref, forward_ref, cos_ref, sin_ref, inner_ref, inner_back_ref, backward_ref, x_hbm,
+    out_ref, x_ref, spec_ref, sems
+):
+    blocks, width, rows = out_ref.shape
+    half = rows // 2
+    count = blocks * GROUP
+    packs = width // PACK
+    filter_packs = spec_ref.shape[0]
+    order = [packs + p for p in range(filter_packs)] + list(range(packs))
+    copies = {
+        p: pltpu.make_async_copy(x_hbm.at[:, p * PACK : (p + 1) * PACK], x_ref.at[p], sems.at[p]) for p in order
+    }
+    for p in order:
+        copies[p].start()
+    turn_cos, turn_sin = turns(cos_ref, sin_ref)
     local = taps_ref.shape[2]
-    lane = lax.broadcasted_iota(jnp.int32, (width, local), 1)
-    mine = lane - lax.broadcasted_iota(jnp.int32, (width, local), 0) == lax.axis_index("ctx") * width
+    columns = PACK * filter_packs
+    lane = lax.broadcasted_iota(jnp.int32, (columns, local), 1)
+    mine = lane - lax.broadcasted_iota(jnp.int32, (columns, local), 0) == lax.axis_index("ctx") * columns
     column = lambda row: jnp.sum(jnp.where(mine, row, 0.0), axis=1, keepdims=True)
     taps = [column(taps_ref[tap, 1:2]) for tap in range(3)]
     skip = column(skip_ref[...])
-    position = lax.broadcasted_iota(jnp.int32, (PACK, rows), 1)
-    for pack in range(width // PACK):
+    for pack in range(filter_packs):
         these = slice(pack * PACK, (pack + 1) * PACK)
-        x = x_ref[:, at + pack * PACK : at + (pack + 1) * PACK, :].astype(F32)
-        first = x[:1] + jnp.where(position == 0, skip[these], 0.0)[None]
-        x = jnp.concatenate([first, x[1:]], 0)
-        total = taps[0][these][None] * x
-        for tap in (1, 2):
-            moved = pltpu.roll(x, tap, 2)
-            before = jnp.concatenate([jnp.zeros((1, PACK, rows), F32), moved[:-1]], 0)
-            total = total + taps[tap][these][None] * jnp.where((position < tap)[None], before, moved)
+        copies[packs + pack].wait()
+        x = x_ref[packs + pack].astype(F32)
+        result = filter_spectrum(
+            x, [t[these] for t in taps], skip[these], forward_ref[...], turn_cos, turn_sin, inner_ref
+        )
+        for odd in (0, 1):
+            spec_ref[pack, odd] = result[odd]
+    for pack in range(packs):
+        copies[pack].wait()
+        data = spectrum(columns_of(x_ref[pack].astype(F32)), forward_ref[...], turn_cos, turn_sin, inner_ref)
+        back = []
+        for odd in (0, 1):
+            filt = spec_ref.at[pack % filter_packs, odd]
+            real, imag = data[odd][:, :half], data[odd][:, half:]
+            filter_real, filter_imag = filt[:, :half], filt[:, half:]
+            if pack >= filter_packs:
+                filter_imag = -filter_imag
+            prod_real = (real * filter_real - imag * filter_imag).astype(BF16)
+            prod_imag = (real * filter_imag + imag * filter_real).astype(BF16)
+            back.append(mm(jnp.concatenate([prod_real, prod_imag], 1), inner_back_ref[odd]))
+        outs = []
         for h in range(2):
-            part = total[:, h * GROUP : (h + 1) * GROUP].reshape(blocks * GROUP, rows).astype(BF16)
-            for odd, result in enumerate(spectrum(part, forward_ref[...], turn_cos, turn_sin, inner_ref)):
-                out_ref[2 * pack + h, odd] = result
-
-
-def convolve_kernel(
-    x_ref, taps_ref, skip_ref, forward_ref, cos_ref, sin_ref, inner_ref, inner_back_ref, backward_ref, out_ref, spec_ref
-):
-    blocks, width, rows = out_ref.shape
-    half = rows // 2
-    packs = width // PACK
-    turn_cos, turn_sin = turns(cos_ref, sin_ref)
-    filter_spectrum(x_ref, width, taps_ref, skip_ref, forward_ref, turn_cos, turn_sin, inner_ref, spec_ref)
-    for pack in range(packs):
-        outs = []
-        for h, x in enumerate(columns_of(x_ref, pack)):
-            data = spectrum(x, forward_ref[...], turn_cos, turn_sin, inner_ref)
-            back = []
-            for odd in (0, 1):
-                filt = spec_ref.at[2 * (pack % (packs // 2)) + h, odd]
-                real, imag = data[odd][:, :half], data[odd][:, half:]
-                filter_real, filter_imag = filt[:, :half], filt[:, half:]
-                if pack >= packs // 2:
-                    filter_imag = -filter_imag
-                prod_real = (real * filter_real - imag * filter_imag).astype(BF16)
-                prod_imag = (real * filter_imag + imag * filter_real).astype(BF16)
-                back.append(mm(jnp.concatenate([prod_real, prod_imag], 1), inner_back_ref[odd]))
-            near, far = back[0] + back[1], back[0] - back[1]
+            even, uneven = (part[h * count : (h + 1) * count] for part in back)
+            near, far = even + uneven, even - uneven
             real = jnp.concatenate([near[:, :half], far[:, :half]], 1)
             imag = jnp.concatenate([near[:, half:], far[:, half:]], 1)
             turned_real = (real * turn_cos - imag * turn_sin).astype(BF16)
@@ -167,14 +177,21 @@
 def convolve(x, taps, skip, t):
     blocks, width, rows = x.shape
     count = width // 3
+    vmem = pl.BlockSpec(memory_space=pltpu.VMEM)
     return pl.pallas_call(
         convolve_kernel,
+        in_specs=[vmem] * 8 + [pl.BlockSpec(memory_space=pl.ANY)],
+        out_specs=vmem,
         out_shape=jax.ShapeDtypeStruct((blocks, 2 * count, rows), BF16),
-        scratch_shapes=[pltpu.VMEM((count // GROUP, 2, blocks * GROUP, rows), F32)],
+        scratch_shapes=[
+            pltpu.VMEM((width // PACK, blocks, PACK, rows), BF16),
+            pltpu.VMEM((count // PACK, 2, 2 * blocks * GROUP, rows), F32),
+            pltpu.SemaphoreType.DMA((width // PACK,)),
+        ],
         compiler_params=params(CONVOLVE_BYTES),
         cost_estimate=cost(5 * 10**9, 4 * MIB),
         name="convolve",
-    )(x, taps, skip, t["forward"], t["turn_cos"], t["turn_sin"], t["inner"], t["inner_back"], t["backward"])
+    )(taps, skip, t["forward"], t["turn_cos"], t["turn_sin"], t["inner"], t["inner_back"], t["backward"], x)
 
 
 def swap_matrix(block):
@@ -333,59 +350,76 @@
     )(own, sib, weight_rows)
 
 
-def end_values_kernel(far_ref, farsib_ref, total_ref, flat_hbm, filter_hbm, out_ref, left_ref, flat_ref, flat_sems, filter_sem):
-    _, rows, depth = left_ref.shape
+def add_values_kernel(last, part_ref, total_ref, flat_hbm, *refs):
+    if last:
+        filter_hbm, out_ref, left_ref, flat_ref, flat_sems, filter_sem = refs
+        slice_width = filter_hbm.shape[1]
+        filter_copy = pltpu.make_async_copy(filter_hbm, out_ref.at[:, 2 * slice_width :], filter_sem)
+    else:
+        out_ref, left_ref, flat_ref, flat_sems = refs
+    rows, depth = left_ref.shape
     width = total_ref.shape[1]
     block = min(256, width)
-    slice_width = filter_hbm.shape[1]
-    per = block // slice_width
-    order = (2, 3, 1, 0)
-    flat_copies = {
-        k: pltpu.make_async_copy(flat_hbm.at[k], flat_ref.at[k], flat_sems.at[k]) for k in order
-    }
-    filter_copy = pltpu.make_async_copy(filter_hbm, out_ref.at[:, 2 * slice_width :], filter_sem)
-    for k in order:
-        flat_copies[k].start()
-    filter_copy.start()
-    swap = swap_matrix(block)
-    flip_into(left_ref.at[0], farsib_ref[...], swap)
-    flip_into(left_ref.at[1], far_ref[...], swap)
+    chunks = (3, 0) if last else (2, 1)
+    copies = [
+        pltpu.make_async_copy(flat_hbm.at[k], flat_ref.at[strand], flat_sems.at[strand])
+        for strand, k in enumerate(chunks)
+    ]
+    for copy in copies:
+        copy.start()
+    if last:
+        filter_copy.start()
+    flip_into(left_ref, part_ref[...], swap_matrix(block))
     for strand in range(2):
         here = slice(strand * rows, (strand + 1) * rows)
-        one, two = (2, 3) if strand == 0 else (1, 0)
-        left_one, left_two = (far_ref[...], farsib_ref[...]) if strand == 0 else (left_ref[1], left_ref[0])
-        flat_copies[one].wait()
-        flat_copies[two].wait()
+        left = part_ref[...] if strand == 0 else left_ref[...]
+        copies[strand].wait()
         for b in range(width // block):
             cols = slice(b * block, (b + 1) * block)
-            total = total_ref[here, cols] + mm(left_one, flat_ref[one, :, cols]) + mm(left_two, flat_ref[two, :, cols])
-            turned = total.T.astype(BF16)
-            for d in range(per):
-                out_ref[b * per + d, strand * slice_width : (strand + 1) * slice_width] = turned[
-                    d * slice_width : (d + 1) * slice_width
-                ]
-    filter_copy.wait()
-
-
-def end_values(far, farsib, total, flat, filter_rows):
-    rows, depth = far.shape
+            total = total_ref[here, cols] + mm(left, flat_ref[strand, :, cols])
+            if last:
+                turned = total.T.astype(BF16)
+                per = block // slice_width
+                for d in range(per):
+                    out_ref[b * per + d, strand * slice_width : (strand + 1) * slice_width] = turned[
+                        d * slice_width : (d + 1) * slice_width
+                    ]
+            else:
+                out_ref[here, cols] = total
+    if last:
+        filter_copy.wait()
+
+
+def add_values(part, total, flat, filter_rows=None):
+    rows, depth = part.shape
+    width = total.shape[1]
     vmem = pl.BlockSpec(memory_space=pltpu.VMEM)
     any_space = pl.BlockSpec(memory_space=pl.ANY)
-    return pl.pallas_call(
-        end_values_kernel,
-        in_specs=[vmem] * 3 + [any_space] * 2,
+    last = filter_rows is not None
+    extra = (filter_rows,) if last else ()
+    if last:
+        out_shape = jax.ShapeDtypeStruct((filter_rows.shape[0], 3 * filter_rows.shape[1], rows), BF16)
+    else:
+        out_shape = jax.ShapeDtypeStruct(total.shape, F32)
+
+    def kernel(*refs):
+        add_values_kernel(last, *refs)
+
+    return pl.pallas_call(
+        kernel,
+        in_specs=[vmem] * 2 + [any_space] * (1 + len(extra)),
         out_specs=vmem,
         scratch_shapes=[
-            pltpu.VMEM((2, rows, depth), BF16),
-            pltpu.VMEM(flat.shape, BF16),
-            pltpu.SemaphoreType.DMA((4,)),
-            pltpu.SemaphoreType.DMA,
-        ],
-        out_shape=jax.ShapeDtypeStruct((filter_rows.shape[0], 3 * filter_rows.shape[1], rows), BF16),
+            pltpu.VMEM((rows, depth), BF16),
+            pltpu.VMEM((2, depth, width), BF16),
+            pltpu.SemaphoreType.DMA((2,)),
+        ]
+        + [pltpu.SemaphoreType.DMA] * len(extra),
+        out_shape=out_shape,
         compiler_params=params(END_BYTES),
-        cost_estimate=cost(8 * rows * depth * total.shape[1], 8 * depth * total.shape[1]),
-        name="end_values",
-    )(far, farsib, total, flat, filter_rows)
+        cost_estimate=cost(4 * rows * depth * width, 4 * depth * width),
+        name="last_values" if last else "far_values",
+    )(part, total, flat, *extra)
 
 
 def gate_mix_kernel(gates_ref, below_ref, above_ref, taps_ref, out_ref):
@@ -486,7 +520,8 @@
     total, flat = start_values(tokens, sib, weight_rows, width)
     far, filter_rows, total, flat = lax.optimization_barrier((far, filter_rows, total, flat))
     farsib = to_tp(far, 1)
-    values = end_values(far, farsib, total, flat, filter_rows)
+    total = add_values(far, total, flat)
+    values = add_values(farsib, total, flat, filter_rows)
     columns = exchange(values)
     parts, _ = lax.optimization_barrier(((tokens, sib, far, farsib), values))
     gates = project_gates(parts, weight_rows, width)

time: 88.4 us -> 87 us (0.984)
  waiting for transfers between devices: 12.7 us -> 11.1 us
    ppermute x3, waiting for transfers between devices: 3.68 us -> 1.78 us  [to_tp(): return lax.ppermute(x, 'tp', [(i, i ^ bits) for i in range(tp_count)])]
    pallas_call x2 -> x3, Pallas kernels: 12.2 us -> 11.9 us  [the longest x1 6.42 us: convolve(): pl.pallas_call(convolve_kernel, in_specs=[vmem] * 8 + [pl.BlockSpec(memor...]
  transfers between devices with their start and end apart: 6 -> 6, of which waited for: 4 -> 3; matrix products, arithmetic and copies ran while one was open for 0% -> 0% of each run, Pallas kernels for 21% -> 23%
where the time goes in v4:
time: 87 us; the launch traced here: 86.6 us
  Pallas kernels  31.8 us (37%)
  blocking collectives  22.2 us (26%)
  starting transfers between devices  18.9 us (22%)
  waiting for transfers between devices  11.1 us (13%)
  local copies, waits for them, and re-layouts  2.33 us (3%)
    all_to_all x1, blocking collectives, exchange(): return lax.all_to_all(x, 'ctx', split_axis=0, concat_axis=0, tiled=True)  22.2 us
    all_to_all x1, starting transfers between devices, exchange(): return lax.all_to_all(x, 'ctx', split_axis=0, concat_axis=0, tiled=True)  9.78 us
    pallas_call x1, Pallas kernels, start_values(): pl.pallas_call(start_values_kernel, in_specs=[any_space] * 3, out_specs=[...  8.49 us
    pallas_call x1, Pallas kernels, project_gates(): pl.pallas_call(project_gates_kernel, in_specs=[pl.BlockSpec(memory_space=...  7.94 us
    pallas_call x1, Pallas kernels, convolve(): pl.pallas_call(convolve_kernel, in_specs=[vmem] * 8 + [pl.BlockSpec(memor...  6.42 us
    ppermute x1, waiting for transfers between devices, to_previous(): return lax.ppermute(x, 'ctx', [(i + 1, i) for i in range(ctx_count - 1)])  6.38 us
    pallas_call x2, Pallas kernels, add_values(): pl.pallas_call(kernel, in_specs=[vmem] * 2 + [any_space] * (1 + len(extra...  5.45 us
    ppermute x1, starting transfers between devices, to_next(): return lax.ppermute(x, 'ctx', [(i, i + 1) for i in range(ctx_count - 1)])  4.55 us
  transfers between devices with their start and end apart: 6, of which 3 were waited for; matrix products, arithmetic and copies ran while one was open for 0% of the time, Pallas kernels for 23%

profile of v4, /device:TPU:0, one launch (start us, length us, event | category | flops | bytes accessed | tf_op | source)
XLA Modules:
  0.0 86.6 jit_solution(14060289922452513105)
XLA Ops:
  0.0 0.0 collective-permute-start.1
  0.0 3.1 %collective-permute-start = (bf16[256,1024]{1,0:T(8,128)(2,1)}, bf16[256,1024]{1,0:T(8,128)(2,1)S(1)}, u32[]{:S(2)}, u32[]{:S(2)}) collective-permute-start(bf16[256,1024]{1,0:T(8,128)(2,1)} %own_hbm.2), channel_id=1, source_target_pairs={{0,2},{1,3},{2,0},{3,1},{4,6},{5,7},{6,4},{7,5},{8,10},{9,11},{10,... | collective-permute-start | bytes 1572872 | tf_op jit(solution)/shard_map/ppermute | solution.py:505
  3.1 1.2 %copy-done.2 = f32[256,1024]{1,0:T(8,128)S(1)} copy-done((f32[256,1024]{1,0:T(8,128)S(1)}, f32[256,1024]{1,0:T(8,128)}, u32[]{:S(2)}) %copy-start.2) | copy-done | bytes 1048600
  4.3 0.4 filter_prep.1
  4.7 0.0 copy-start
  4.8 1.0 %copy-done = bf16[256,1024]{1,0:T(8,128)(2,1)S(1)} copy-done((bf16[256,1024]{1,0:T(8,128)(2,1)S(1)}, bf16[256,1024]{1,0:T(8,128)(2,1)}, u32[]{:S(2)}) %copy-start) | copy-done | bytes 524312
  5.8 8.5 %start_values.1 = (f32[512,1024]{1,0:T(8,128)S(1)}, bf16[4,1024,1024]{2,1,0:T(8,128)(2,1)S(1)}) custom-call(bf16[256,1024]{1,0:T(8,128)(2,1)S(1)} %copy-done, bf16[256,1024]{1,0:T(8,128)(2,1)S(1)} %collective-permute-done.1.sib_hbm, bf16[65536,128]{1,0:T(8,128)(2,1)} %bitcast.9), custom_call_target="tpu_custom_call" | custom-call | flops 2147483648 | bytes 25165824 | tf_op jit(solution)/shard_map/start_values/pallas_call | solution.py:331
  14.3 1.8 %collective-permute-done.refs_0_.far_hbm = bf16[256,1024]{1,0:T(8,128)(2,1)S(1)} collective-permute-done((bf16[256,1024]{1,0:T(8,128)(2,1)}, bf16[256,1024]{1,0:T(8,128)(2,1)S(1)}, u32[]{:S(2)}, u32[]{:S(2)}) %collective-permute-start) | collective-permute-done | bytes 524320 | tf_op jit(solution)/shard_map/ppermute | solution.py:505
  16.1 0.0 collective-permute-start.2
  16.1 2.0 %far_values.1.refs_1_ = f32[512,1024]{1,0:T(8,128)S(1)} custom-call(bf16[256,1024]{1,0:T(8,128)(2,1)S(1)} %collective-permute-done.refs_0_.far_hbm, f32[512,1024]{1,0:T(8,128)S(1)} %get-tuple-element.20.refs_1_, bf16[4,1024,1024]{2,1,0:T(8,128)(2,1)S(1)} %get-tuple-element.21.refs_2_), custom_call_target="tpu_custom_call" | custom-call | flops 1073741824 | bytes 4194304 | tf_op jit(solution)/shard_map/far_values/pallas_call | solution.py:408
  18.1 0.0 collective-permute-done.2.refs_0_.farsib_hbm
  18.1 3.4 %last_values.1 = bf16[32,96,256]{2,1,0:T(8,128)(2,1)} custom-call(bf16[256,1024]{1,0:T(8,128)(2,1)S(1)} %collective-permute-done.2.refs_0_.farsib_hbm, f32[512,1024]{1,0:T(8,128)S(1)} %far_values.1.refs_1_, bf16[4,1024,1024]{2,1,0:T(8,128)(2,1)S(1)} %get-tuple-element.21.refs_2_, bf16[32,32,256]{2,1,0:T(8,128)(2,1)S(1)} %bitcast.7), custom_call_target="tpu_custom_call" | custom-call | flops 1073741824 | bytes 4194304 | tf_op jit(solution)/shard_map/last_values/pallas_call | solution.py:408
  21.5 0.0 copy-start.1
  21.5 9.8 %all-to-all-start = ((bf16[32,96,256]{2,1,0:T(8,128)(2,1)}), bf16[32,96,256]{2,1,0:T(8,128)(2,1)}, u32[]{:S(2)}, u32[]{:S(2)}) async-start(bf16[32,96,256]{2,1,0:T(8,128)(2,1)} %last_values.1), calls=%async_computation | async-start | bytes 3145728 | tf_op jit(solution)/shard_map/all_to_all | solution.py:514
  31.3 0.0 copy-start.3
  31.4 7.9 %project_gates.1.gates_ref = bf16[512,1024]{1,0:T(8,128)(2,1)S(1)} custom-call(bf16[256,1024]{1,0:T(8,128)(2,1)S(1)} %copy-done.1, bf16[256,1024]{1,0:T(8,128)(2,1)S(1)} %collective-permute-done.1.sib_hbm, bf16[256,1024]{1,0:T(8,128)(2,1)S(1)} %collective-permute-done.refs_0_.far_hbm, bf16[256,1024]{1,0:T(8,128)(2,1)S(1)} %collective-permute-done.2.refs_0_.farsib_hbm, ...), custom_call_target="tpu_custom_call" | custom-call | flops 4294967296 | bytes 16777216 | tf_op jit(solution)/shard_map/project_gates/pallas_call | solution.py:270
  39.3 0.0 copy-start.4
  39.3 0.0 copy-start.5
  39.3 0.0 copy-start.6
  39.3 0.0 copy-start.7
  39.4 0.0 copy-start.8
  39.4 0.0 copy-start.9
  39.4 0.0 copy-start.10
  39.4 1.4 %collective-permute-start.4 = (bf16[16,1024]{1,0:T(8,128)(2,1)S(1)}, bf16[16,1024]{1,0:T(8,128)(2,1)S(1)}, u32[]{:S(2)}, u32[]{:S(2)}) collective-permute-start(bf16[16,1024]{1,0:T(8,128)(2,1)S(1)} %get-tuple-element.29), channel_id=1, source_target_pairs={{4,0},{8,4},{12,8},{16,12},{20,16},{24,20},{28,24},{32,28},{36,32}... | collective-permute-start | bytes 98312 | tf_op jit(solution)/shard_map/ppermute | solution.py:511
  40.8 4.5 %collective-permute-start.3 = (bf16[16,1024]{1,0:T(8,128)(2,1)S(1)}, bf16[16,1024]{1,0:T(8,128)(2,1)S(1)}, u32[]{:S(2)}, u32[]{:S(2)}) collective-permute-start(bf16[16,1024]{1,0:T(8,128)(2,1)S(1)} %get-tuple-element.30), channel_id=1, source_target_pairs={{0,4},{4,8},{8,12},{12,16},{16,20},{20,24},{24,28},{28,32},{32,36}... | collective-permute-start | bytes 98312 | tf_op jit(solution)/shard_map/ppermute | solution.py:508
  45.4 6.4 %collective-permute-done.4.above_ref = bf16[16,1024]{1,0:T(8,128)(2,1)S(1)} collective-permute-done((bf16[16,1024]{1,0:T(8,128)(2,1)S(1)}, bf16[16,1024]{1,0:T(8,128)(2,1)S(1)}, u32[]{:S(2)}, u32[]{:S(2)}) %collective-permute-start.4) | collective-permute-done | bytes 32800 | tf_op jit(solution)/shard_map/ppermute | solution.py:511
  51.8 0.0 collective-permute-done.3.below_ref
  51.8 1.3 %gate_mix.1.gates_ref = f32[2,1024,256]{2,1,0:T(8,128)S(1)} custom-call(bf16[512,1024]{1,0:T(8,128)(2,1)S(1)} %project_gates.1.gates_ref, bf16[16,1024]{1,0:T(8,128)(2,1)S(1)} %collective-permute-done.3.below_ref, bf16[16,1024]{1,0:T(8,128)(2,1)S(1)} %collective-permute-done.4.above_ref, f32[3,2,1024]{2,1,0:T(2,128)S(1)} %copy-done.3), custom_call_target="tpu_custom_call" | custom-call | flops 4194304 | bytes 3145728 | tf_op jit(solution)/shard_map/gate_mix/pallas_call | solution.py:451
  53.1 3.0 %all-to-all-done.x_hbm = bf16[32,96,256]{2,1,0:T(8,128)(2,1)} async-done(((bf16[32,96,256]{2,1,0:T(8,128)(2,1)}), bf16[32,96,256]{2,1,0:T(8,128)(2,1)}, u32[]{:S(2)}, u32[]{:S(2)}) %all-to-all-start) | async-done | bytes 1572896 | tf_op jit(solution)/shard_map/all_to_all | solution.py:514
  56.1 6.4 %convolve.1 = bf16[32,64,256]{2,1,0:T(8,128)(2,1)S(1)} custom-call(f32[3,2,1024]{2,1,0:T(2,128)S(1)} %copy-done.3, f32[1,1024]{1,0:T(1,128)S(1)} %bitcast.8, bf16[512,256]{1,0:T(8,128)(2,1)S(1)} %copy-done.8, f32[32,1,256]{2,1,0:T(1,128)S(1)} %copy-done.10, f32[32,1,256]{2,1,0:T(1,128)S(1)} %copy-done.9, bf16[2,256,256]{2,1,0:T(8,128)(2,1)S(1)} %copy-done.7, ...), custom_call_target="tpu_custom_call" | custom-call | flops 5000000000 | bytes 4194304 | tf_op jit(solution)/shard_map/convolve/pallas_call | solution.py:181
  62.5 22.2 %all_to_all.10.conv_ref = bf16[32,64,256]{2,1,0:T(8,128)(2,1)S(1)} all-to-all(bf16[32,64,256]{2,1,0:T(8,128)(2,1)S(1)} %convolve.1), channel_id=1, replica_groups=mesh['ctx'=32,'tp'=4] {'ctx'}, dimensions={0} | all-to-all | bytes 2097152 | tf_op jit(solution)/shard_map/all_to_all | solution.py:514
  84.8 1.8 %finish.1 = bf16[256,1024]{1,0:T(8,128)(2,1)} custom-call(f32[2,1024,256]{2,1,0:T(8,128)S(1)} %gate_mix.1.gates_ref, bf16[32,64,256]{2,1,0:T(8,128)(2,1)S(1)} %all_to_all.10.conv_ref), custom_call_target="tpu_custom_call" | custom-call | flops 1048576 | bytes 3670016 | tf_op jit(solution)/shard_map/finish/pallas_call | solution.py:480
  (12 shorter events, 0.0 us)
Async XLA Ops:
  0.0 4.7 %collective-permute-start.1 = (bf16[256,1024]{1,0:T(8,128)(2,1)}, bf16[256,1024]{1,0:T(8,128)(2,1)S(1)}, u32[]{:S(2)}, u32[]{:S(2)}) collective-permute-start(bf16[256,1024]{1,0:T(8,128)(2,1)} %own_hbm.2), channel_id=1, source_target_pairs={{0,1},{1,0},{2,3},{3,2},{4,5},{5,4},{6,7},{7,6},{8,9},{9,8},{10,11... | collective-permute-start | bytes 1572872 | tf_op jit(solution)/shard_map/ppermute | solution.py:505
  0.0 16.1 %collective-permute-start = (bf16[256,1024]{1,0:T(8,128)(2,1)}, bf16[256,1024]{1,0:T(8,128)(2,1)S(1)}, u32[]{:S(2)}, u32[]{:S(2)}) collective-permute-start(bf16[256,1024]{1,0:T(8,128)(2,1)} %own_hbm.2), channel_id=1, source_target_pairs={{0,2},{1,3},{2,0},{3,1},{4,6},{5,7},{6,4},{7,5},{8,10},{9,11},{10,... | collective-permute-start | bytes 1572872 | tf_op jit(solution)/shard_map/ppermute | solution.py:505
  3.1 1.2 %copy-start.2 = (f32[256,1024]{1,0:T(8,128)S(1)}, f32[256,1024]{1,0:T(8,128)}, u32[]{:S(2)}) copy-start(f32[256,1024]{1,0:T(8,128)} %filter_ref.1) | copy-start | bytes 3145732
  4.7 1.0 %copy-start = (bf16[256,1024]{1,0:T(8,128)(2,1)S(1)}, bf16[256,1024]{1,0:T(8,128)(2,1)}, u32[]{:S(2)}) copy-start(bf16[256,1024]{1,0:T(8,128)(2,1)} %own_hbm.2) | copy-start | bytes 1572868
  16.1 2.0 %collective-permute-start.2 = (bf16[256,1024]{1,0:T(8,128)(2,1)S(1)}, bf16[256,1024]{1,0:T(8,128)(2,1)S(1)}, u32[]{:S(2)}, u32[]{:S(2)}) collective-permute-start(bf16[256,1024]{1,0:T(8,128)(2,1)S(1)} %collective-permute-done.refs_0_.far_hbm), channel_id=1, source_target_pairs={{0,1},{1,0},{2,3},{3,2},{4,5},{5,4},{6,7},{7,6},{8,9},{9,8},{10,11... | collective-permute-start | bytes 1572872 | tf_op jit(solution)/shard_map/ppermute | solution.py:505
  21.5 9.8 %copy-start.1 = (bf16[256,1024]{1,0:T(8,128)(2,1)S(1)}, bf16[256,1024]{1,0:T(8,128)(2,1)}, u32[]{:S(2)}) copy-start(bf16[256,1024]{1,0:T(8,128)(2,1)} %own_hbm.2) | copy-start | bytes 1572868
  21.5 34.5 %all-to-all-start = ((bf16[32,96,256]{2,1,0:T(8,128)(2,1)}), bf16[32,96,256]{2,1,0:T(8,128)(2,1)}, u32[]{:S(2)}, u32[]{:S(2)}) async-start(bf16[32,96,256]{2,1,0:T(8,128)(2,1)} %last_values.1), calls=%async_computation | async-start | bytes 3145728 | tf_op jit(solution)/shard_map/all_to_all | solution.py:514
  31.3 20.4 %copy-start.3 = (f32[3,2,1024]{2,1,0:T(2,128)S(1)}, f32[3,2,1024]{2,1,0:T(2,128)}, u32[]{:S(2)}) copy-start(f32[3,2,1024]{2,1,0:T(2,128)} %taps_ref.3) | copy-start | bytes 73732
  39.3 16.7 %copy-start.4 = (f32[1024]{0:T(1024)S(1)}, f32[1024]{0:T(1024)}, u32[]{:S(2)}) copy-start(f32[1024]{0:T(1024)} %param.15) | copy-start | bytes 12292
  39.3 16.7 %copy-start.5 = (bf16[256,512]{1,0:T(8,128)(2,1)S(1)}, bf16[256,512]{1,0:T(8,128)(2,1)}, u32[]{:S(2)}) copy-start(bf16[256,512]{1,0:T(8,128)(2,1)} %constant.21.backward_ref) | copy-start | bytes 786436
  39.3 16.7 %copy-start.6 = (bf16[2,256,256]{2,1,0:T(8,128)(2,1)S(1)}, bf16[2,256,256]{2,1,0:T(8,128)(2,1)}, u32[]{:S(2)}) copy-start(bf16[2,256,256]{2,1,0:T(8,128)(2,1)} %constant.20.inner_back_ref) | copy-start | bytes 786436
  39.3 16.7 %copy-start.7 = (bf16[2,256,256]{2,1,0:T(8,128)(2,1)S(1)}, bf16[2,256,256]{2,1,0:T(8,128)(2,1)}, u32[]{:S(2)}) copy-start(bf16[2,256,256]{2,1,0:T(8,128)(2,1)} %constant.19.inner_ref) | copy-start | bytes 786436
  39.4 16.7 %copy-start.8 = (bf16[512,256]{1,0:T(8,128)(2,1)S(1)}, bf16[512,256]{1,0:T(8,128)(2,1)}, u32[]{:S(2)}) copy-start(bf16[512,256]{1,0:T(8,128)(2,1)} %constant.18.forward_ref) | copy-start | bytes 786436
  39.4 16.7 %copy-start.9 = (f32[32,1,256]{2,1,0:T(1,128)S(1)}, f32[32,1,256]{2,1,0:T(1,128)}, u32[]{:S(2)}) copy-start(f32[32,1,256]{2,1,0:T(1,128)} %constant.15.clone.sin_ref) | copy-start | bytes 98308
  39.4 16.7 %copy-start.10 = (f32[32,1,256]{2,1,0:T(1,128)S(1)}, f32[32,1,256]{2,1,0:T(1,128)}, u32[]{:S(2)}) copy-start(f32[32,1,256]{2,1,0:T(1,128)} %constant.14.clone.cos_ref) | copy-start | bytes 98308
  39.4 12.4 %collective-permute-start.4 = (bf16[16,1024]{1,0:T(8,128)(2,1)S(1)}, bf16[16,1024]{1,0:T(8,128)(2,1)S(1)}, u32[]{:S(2)}, u32[]{:S(2)}) collective-permute-start(bf16[16,1024]{1,0:T(8,128)(2,1)S(1)} %get-tuple-element.29), channel_id=1, source_target_pairs={{4,0},{8,4},{12,8},{16,12},{20,16},{24,20},{28,24},{32,28},{36,32}... | collective-permute-start | bytes 98312 | tf_op jit(solution)/shard_map/ppermute | solution.py:511
  40.8 10.9 %collective-permute-start.3 = (bf16[16,1024]{1,0:T(8,128)(2,1)S(1)}, bf16[16,1024]{1,0:T(8,128)(2,1)S(1)}, u32[]{:S(2)}, u32[]{:S(2)}) collective-permute-start(bf16[16,1024]{1,0:T(8,128)(2,1)S(1)} %get-tuple-element.30), channel_id=1, source_target_pairs={{0,4},{4,8},{8,12},{12,16},{16,20},{20,24},{24,28},{28,32},{32,36}... | collective-permute-start | bytes 98312 | tf_op jit(solution)/shard_map/ppermute | solution.py:508

commit v5 on v4

--- a/solution.py
+++ b/solution.py
@@ -285,7 +285,9 @@
     )(*parts, weight_rows)
 
 
-def start_values_kernel(own_hbm, sib_hbm, w_hbm, total_ref, flat_hbm, left_ref, raw_ref, flat_ref, part_sems, w_sems, flat_sems):
+def start_values_kernel(
+    own_hbm, sib_hbm, w_hbm, total_ref, flat_far_hbm, flat_last_hbm, left_ref, raw_ref, flat_ref, part_sems, w_sems, flat_sems
+):
     _, rows, depth = left_ref.shape
     width = total_ref.shape[1]
     block = min(256, width)
@@ -294,7 +296,8 @@
     ]
     w_copies = weight_copies(w_hbm, raw_ref, w_sems)
     flat_copies = [
-        pltpu.make_async_copy(flat_ref.at[k], flat_hbm.at[k], flat_sems.at[k]) for k in range(4)
+        pltpu.make_async_copy(flat_ref.at[k], dst, flat_sems.at[k])
+        for k, dst in enumerate((flat_last_hbm.at[1], flat_far_hbm.at[1], flat_far_hbm.at[0], flat_last_hbm.at[0]))
     ]
     w_copies[0].start()
     for copy in part_copies:
@@ -331,7 +334,7 @@
     return pl.pallas_call(
         start_values_kernel,
         in_specs=[any_space] * 3,
-        out_specs=[pl.BlockSpec(memory_space=pltpu.VMEM), any_space],
+        out_specs=[pl.BlockSpec(memory_space=pltpu.VMEM), any_space, any_space],
         scratch_shapes=[
             pltpu.VMEM((4, rows, depth), BF16),
             pltpu.VMEM((4, depth * 2 * tiles, LANES), BF16),
@@ -342,7 +345,8 @@
         ],
         out_shape=[
             jax.ShapeDtypeStruct((2 * rows, width), F32),
-            jax.ShapeDtypeStruct((4, depth, width), BF16),
+            jax.ShapeDtypeStruct((2, depth, width), BF16),
+            jax.ShapeDtypeStruct((2, depth, width), BF16),
         ],
         compiler_params=params(START_BYTES),
         cost_estimate=cost(8 * rows * depth * width, 24 * depth * width),
@@ -350,30 +354,22 @@
     )(own, sib, weight_rows)
 
 
-def add_values_kernel(last, part_ref, total_ref, flat_hbm, *refs):
+def add_values_kernel(last, part_ref, total_ref, flat_ref, *refs):
     if last:
-        filter_hbm, out_ref, left_ref, flat_ref, flat_sems, filter_sem = refs
+        filter_hbm, out_ref, left_ref, filter_sem = refs
         slice_width = filter_hbm.shape[1]
         filter_copy = pltpu.make_async_copy(filter_hbm, out_ref.at[:, 2 * slice_width :], filter_sem)
     else:
-        out_ref, left_ref, flat_ref, flat_sems = refs
+        out_ref, left_ref = refs
     rows, depth = left_ref.shape
     width = total_ref.shape[1]
     block = min(256, width)
-    chunks = (3, 0) if last else (2, 1)
-    copies = [
-        pltpu.make_async_copy(flat_hbm.at[k], flat_ref.at[strand], flat_sems.at[strand])
-        for strand, k in enumerate(chunks)
-    ]
-    for copy in copies:
-        copy.start()
     if last:
         filter_copy.start()
     flip_into(left_ref, part_ref[...], swap_matrix(block))
     for strand in range(2):
         here = slice(strand * rows, (strand + 1) * rows)
         left = part_ref[...] if strand == 0 else left_ref[...]
-        copies[strand].wait()
         for b in range(width // block):
             cols = slice(b * block, (b + 1) * block)
             total = total_ref[here, cols] + mm(left, flat_ref[strand, :, cols])
@@ -407,14 +403,9 @@
 
     return pl.pallas_call(
         kernel,
-        in_specs=[vmem] * 2 + [any_space] * (1 + len(extra)),
+        in_specs=[vmem] * 3 + [any_space] * len(extra),
         out_specs=vmem,
-        scratch_shapes=[
-            pltpu.VMEM((rows, depth), BF16),
-            pltpu.VMEM((2, depth, width), BF16),
-            pltpu.SemaphoreType.DMA((2,)),
-        ]
-        + [pltpu.SemaphoreType.DMA] * len(extra),
+        scratch_shapes=[pltpu.VMEM((rows, depth), BF16)] + [pltpu.SemaphoreType.DMA] * len(extra),
         out_shape=out_shape,
         compiler_params=params(END_BYTES),
         cost_estimate=cost(4 * rows * depth * width, 4 * depth * width),
@@ -517,11 +508,13 @@
     far = to_tp(tokens, 2)
     sib = to_tp(tokens, 1)
     filter_rows = filter_prep(long_filter).reshape(ctx_count, slice_width, rows)
-    total, flat = start_values(tokens, sib, weight_rows, width)
-    far, filter_rows, total, flat = lax.optimization_barrier((far, filter_rows, total, flat))
+    total, flat_far, flat_last = start_values(tokens, sib, weight_rows, width)
+    far, filter_rows, total, flat_far, flat_last = lax.optimization_barrier(
+        (far, filter_rows, total, flat_far, flat_last)
+    )
     farsib = to_tp(far, 1)
-    total = add_values(far, total, flat)
-    values = add_values(farsib, total, flat, filter_rows)
+    total = add_values(far, total, flat_far)
+    values = add_values(farsib, total, flat_last, filter_rows)
     columns = exchange(values)
     parts, _ = lax.optimization_barrier(((tokens, sib, far, farsib), values))
     gates = project_gates(parts, weight_rows, width)

time: 87 us -> 85.3 us (0.980)
  Pallas kernels: 31.8 us -> 30.4 us
    pallas_call x2, Pallas kernels: 5.45 us -> 4.06 us  [add_values(): pl.pallas_call(kernel, in_specs=[vmem] * 3 + [any_space] * len(extra), ou...]
  transfers between devices with their start and end apart: 6 -> 6, of which waited for: 3 -> 4; matrix products, arithmetic and copies ran while one was open for 0% -> 0% of each run, Pallas kernels for 23% -> 23%
where the time goes in v5:
time: 85.3 us; the launch traced here: 84.9 us
  Pallas kernels  30.4 us (36%)
  blocking collectives  21.8 us (26%)
  starting transfers between devices  18.9 us (22%)
  waiting for transfers between devices  11.3 us (13%)
  local copies, waits for them, and re-layouts  2.33 us (3%)
    all_to_all x1, blocking collectives, exchange(): return lax.all_to_all(x, 'ctx', split_axis=0, concat_axis=0, tiled=True)  21.8 us
    all_to_all x1, starting transfers between devices, exchange(): return lax.all_to_all(x, 'ctx', split_axis=0, concat_axis=0, tiled=True)  9.78 us
    pallas_call x1, Pallas kernels, start_values(): pl.pallas_call(start_values_kernel, in_specs=[any_space] * 3, out_specs=[...  8.49 us
    pallas_call x1, Pallas kernels, project_gates(): pl.pallas_call(project_gates_kernel, in_specs=[pl.BlockSpec(memory_space=...  7.95 us
    pallas_call x1, Pallas kernels, convolve(): pl.pallas_call(convolve_kernel, in_specs=[vmem] * 8 + [pl.BlockSpec(memor...  6.42 us
    ppermute x1, waiting for transfers between devices, to_previous(): return lax.ppermute(x, 'ctx', [(i + 1, i) for i in range(ctx_count - 1)])  6.32 us
    ppermute x1, starting transfers between devices, to_next(): return lax.ppermute(x, 'ctx', [(i, i + 1) for i in range(ctx_count - 1)])  4.55 us
    pallas_call x2, Pallas kernels, add_values(): pl.pallas_call(kernel, in_specs=[vmem] * 3 + [any_space] * len(extra), ou...  4.06 us
  transfers between devices with their start and end apart: 6, of which 4 were waited for; matrix products, arithmetic and copies ran while one was open for 0% of the time, Pallas kernels for 23%

profile of v5, /device:TPU:0, one launch (start us, length us, event | category | flops | bytes accessed | tf_op | source)
XLA Modules:
  0.0 84.9 jit_solution(979507914813704941)
XLA Ops:
  0.0 0.0 collective-permute-start.1
  0.0 3.1 %collective-permute-start = (bf16[256,1024]{1,0:T(8,128)(2,1)}, bf16[256,1024]{1,0:T(8,128)(2,1)S(1)}, u32[]{:S(2)}, u32[]{:S(2)}) collective-permute-start(bf16[256,1024]{1,0:T(8,128)(2,1)} %own_hbm.2), channel_id=1, source_target_pairs={{0,2},{1,3},{2,0},{3,1},{4,6},{5,7},{6,4},{7,5},{8,10},{9,11},{10,... | collective-permute-start | bytes 1572872 | tf_op jit(solution)/shard_map/ppermute | solution.py:496
  3.1 1.2 %copy-done.2 = f32[256,1024]{1,0:T(8,128)S(1)} copy-done((f32[256,1024]{1,0:T(8,128)S(1)}, f32[256,1024]{1,0:T(8,128)}, u32[]{:S(2)}) %copy-start.2) | copy-done | bytes 1048600
  4.3 0.4 filter_prep.1
  4.7 0.0 collective-permute-done.1.sib_hbm
  4.7 0.0 copy-start
  4.8 1.0 %copy-done = bf16[256,1024]{1,0:T(8,128)(2,1)S(1)} copy-done((bf16[256,1024]{1,0:T(8,128)(2,1)S(1)}, bf16[256,1024]{1,0:T(8,128)(2,1)}, u32[]{:S(2)}) %copy-start) | copy-done | bytes 524312
  5.8 8.5 %start_values.1 = (f32[512,1024]{1,0:T(8,128)S(1)}, bf16[2,1024,1024]{2,1,0:T(8,128)(2,1)S(1)}, bf16[2,1024,1024]{2,1,0:T(8,128)(2,1)S(1)}) custom-call(bf16[256,1024]{1,0:T(8,128)(2,1)S(1)} %copy-done, bf16[256,1024]{1,0:T(8,128)(2,1)S(1)} %collective-permute-done.1.sib_hbm, bf16[65536,128]{1,0:T(8,128)(2,1)} %bitcast.9), custom_call_target="tpu_custom_call" | custom-call | flops 2147483648 | bytes 25165824 | tf_op jit(solution)/shard_map/start_values/pallas_call | solution.py:334
  14.3 1.8 %collective-permute-done.refs_0_.far_hbm = bf16[256,1024]{1,0:T(8,128)(2,1)S(1)} collective-permute-done((bf16[256,1024]{1,0:T(8,128)(2,1)}, bf16[256,1024]{1,0:T(8,128)(2,1)S(1)}, u32[]{:S(2)}, u32[]{:S(2)}) %collective-permute-start) | collective-permute-done | bytes 524320 | tf_op jit(solution)/shard_map/ppermute | solution.py:496
  16.1 0.0 collective-permute-start.2
  16.1 1.4 %far_values.1.refs_1_ = f32[512,1024]{1,0:T(8,128)S(1)} custom-call(bf16[256,1024]{1,0:T(8,128)(2,1)S(1)} %collective-permute-done.refs_0_.far_hbm, f32[512,1024]{1,0:T(8,128)S(1)} %get-tuple-element.23.refs_1_, bf16[2,1024,1024]{2,1,0:T(8,128)(2,1)S(1)} %get-tuple-element.24.refs_2_), custom_call_target="tpu_custom_call" | custom-call | flops 1073741824 | bytes 4194304 | tf_op jit(solution)/shard_map/far_values/pallas_call | solution.py:404
  17.5 0.5 collective-permute-done.2.refs_0_.farsib_hbm
  18.0 2.7 %last_values.1 = bf16[32,96,256]{2,1,0:T(8,128)(2,1)} custom-call(bf16[256,1024]{1,0:T(8,128)(2,1)S(1)} %collective-permute-done.2.refs_0_.farsib_hbm, f32[512,1024]{1,0:T(8,128)S(1)} %far_values.1.refs_1_, bf16[2,1024,1024]{2,1,0:T(8,128)(2,1)S(1)} %get-tuple-element.25.refs_2_, bf16[32,32,256]{2,1,0:T(8,128)(2,1)S(1)} %bitcast.7), custom_call_target="tpu_custom_call" | custom-call | flops 1073741824 | bytes 4194304 | tf_op jit(solution)/shard_map/last_values/pallas_call | solution.py:404
  20.6 0.0 copy-start.1
  20.7 9.8 %all-to-all-start = ((bf16[32,96,256]{2,1,0:T(8,128)(2,1)}), bf16[32,96,256]{2,1,0:T(8,128)(2,1)}, u32[]{:S(2)}, u32[]{:S(2)}) async-start(bf16[32,96,256]{2,1,0:T(8,128)(2,1)} %last_values.1), calls=%async_computation | async-start | bytes 3145728 | tf_op jit(solution)/shard_map/all_to_all | solution.py:505
  30.5 0.0 copy-start.3
  30.5 8.0 %project_gates.1.gates_ref = bf16[512,1024]{1,0:T(8,128)(2,1)S(1)} custom-call(bf16[256,1024]{1,0:T(8,128)(2,1)S(1)} %copy-done.1, bf16[256,1024]{1,0:T(8,128)(2,1)S(1)} %collective-permute-done.1.sib_hbm, bf16[256,1024]{1,0:T(8,128)(2,1)S(1)} %collective-permute-done.refs_0_.far_hbm, bf16[256,1024]{1,0:T(8,128)(2,1)S(1)} %collective-permute-done.2.refs_0_.farsib_hbm, ...), custom_call_target="tpu_custom_call" | custom-call | flops 4294967296 | bytes 16777216 | tf_op jit(solution)/shard_map/project_gates/pallas_call | solution.py:270
  38.4 0.0 copy-start.4
  38.4 0.0 copy-start.5
  38.5 0.0 copy-start.6
  38.5 0.0 copy-start.7
  38.5 0.0 copy-start.8
  38.5 0.0 copy-start.9
  38.5 0.0 copy-start.10
  38.5 1.4 %collective-permute-start.4 = (bf16[16,1024]{1,0:T(8,128)(2,1)S(1)}, bf16[16,1024]{1,0:T(8,128)(2,1)S(1)}, u32[]{:S(2)}, u32[]{:S(2)}) collective-permute-start(bf16[16,1024]{1,0:T(8,128)(2,1)S(1)} %get-tuple-element.33), channel_id=1, source_target_pairs={{4,0},{8,4},{12,8},{16,12},{20,16},{24,20},{28,24},{32,28},{36,32}... | collective-permute-start | bytes 98312 | tf_op jit(solution)/shard_map/ppermute | solution.py:502
  40.0 4.5 %collective-permute-start.3 = (bf16[16,1024]{1,0:T(8,128)(2,1)S(1)}, bf16[16,1024]{1,0:T(8,128)(2,1)S(1)}, u32[]{:S(2)}, u32[]{:S(2)}) collective-permute-start(bf16[16,1024]{1,0:T(8,128)(2,1)S(1)} %get-tuple-element.34), channel_id=1, source_target_pairs={{0,4},{4,8},{8,12},{12,16},{16,20},{20,24},{24,28},{28,32},{32,36}... | collective-permute-start | bytes 98312 | tf_op jit(solution)/shard_map/ppermute | solution.py:499
  44.5 6.3 %collective-permute-done.4.above_ref = bf16[16,1024]{1,0:T(8,128)(2,1)S(1)} collective-permute-done((bf16[16,1024]{1,0:T(8,128)(2,1)S(1)}, bf16[16,1024]{1,0:T(8,128)(2,1)S(1)}, u32[]{:S(2)}, u32[]{:S(2)}) %collective-permute-start.4) | collective-permute-done | bytes 32800 | tf_op jit(solution)/shard_map/ppermute | solution.py:502
  50.9 1.3 %gate_mix.1.gates_ref = f32[2,1024,256]{2,1,0:T(8,128)S(1)} custom-call(bf16[512,1024]{1,0:T(8,128)(2,1)S(1)} %project_gates.1.gates_ref, bf16[16,1024]{1,0:T(8,128)(2,1)S(1)} %collective-permute-done.3.below_ref, bf16[16,1024]{1,0:T(8,128)(2,1)S(1)} %collective-permute-done.4.above_ref, f32[3,2,1024]{2,1,0:T(2,128)S(1)} %copy-done.3), custom_call_target="tpu_custom_call" | custom-call | flops 4194304 | bytes 3145728 | tf_op jit(solution)/shard_map/gate_mix/pallas_call | solution.py:442
  52.2 2.7 %all-to-all-done.x_hbm = bf16[32,96,256]{2,1,0:T(8,128)(2,1)} async-done(((bf16[32,96,256]{2,1,0:T(8,128)(2,1)}), bf16[32,96,256]{2,1,0:T(8,128)(2,1)}, u32[]{:S(2)}, u32[]{:S(2)}) %all-to-all-start) | async-done | bytes 1572896 | tf_op jit(solution)/shard_map/all_to_all | solution.py:505
  54.9 6.4 %convolve.1 = bf16[32,64,256]{2,1,0:T(8,128)(2,1)S(1)} custom-call(f32[3,2,1024]{2,1,0:T(2,128)S(1)} %copy-done.3, f32[1,1024]{1,0:T(1,128)S(1)} %bitcast.8, bf16[512,256]{1,0:T(8,128)(2,1)S(1)} %copy-done.8, f32[32,1,256]{2,1,0:T(1,128)S(1)} %copy-done.10, f32[32,1,256]{2,1,0:T(1,128)S(1)} %copy-done.9, bf16[2,256,256]{2,1,0:T(8,128)(2,1)S(1)} %copy-done.7, ...), custom_call_target="tpu_custom_call" | custom-call | flops 5000000000 | bytes 4194304 | tf_op jit(solution)/shard_map/convolve/pallas_call | solution.py:181
  61.3 21.8 %all_to_all.10.conv_ref = bf16[32,64,256]{2,1,0:T(8,128)(2,1)S(1)} all-to-all(bf16[32,64,256]{2,1,0:T(8,128)(2,1)S(1)} %convolve.1), channel_id=1, replica_groups=mesh['ctx'=32,'tp'=4] {'ctx'}, dimensions={0} | all-to-all | bytes 2097152 | tf_op jit(solution)/shard_map/all_to_all | solution.py:505
  83.1 1.8 %finish.1 = bf16[256,1024]{1,0:T(8,128)(2,1)} custom-call(f32[2,1024,256]{2,1,0:T(8,128)S(1)} %gate_mix.1.gates_ref, bf16[32,64,256]{2,1,0:T(8,128)(2,1)S(1)} %all_to_all.10.conv_ref), custom_call_target="tpu_custom_call" | custom-call | flops 1048576 | bytes 3670016 | tf_op jit(solution)/shard_map/finish/pallas_call | solution.py:471
  (12 shorter events, 0.0 us)
Async XLA Ops:
  0.0 4.7 %collective-permute-start.1 = (bf16[256,1024]{1,0:T(8,128)(2,1)}, bf16[256,1024]{1,0:T(8,128)(2,1)S(1)}, u32[]{:S(2)}, u32[]{:S(2)}) collective-permute-start(bf16[256,1024]{1,0:T(8,128)(2,1)} %own_hbm.2), channel_id=1, source_target_pairs={{0,1},{1,0},{2,3},{3,2},{4,5},{5,4},{6,7},{7,6},{8,9},{9,8},{10,11... | collective-permute-start | bytes 1572872 | tf_op jit(solution)/shard_map/ppermute | solution.py:496
  0.0 16.1 %collective-permute-start = (bf16[256,1024]{1,0:T(8,128)(2,1)}, bf16[256,1024]{1,0:T(8,128)(2,1)S(1)}, u32[]{:S(2)}, u32[]{:S(2)}) collective-permute-start(bf16[256,1024]{1,0:T(8,128)(2,1)} %own_hbm.2), channel_id=1, source_target_pairs={{0,2},{1,3},{2,0},{3,1},{4,6},{5,7},{6,4},{7,5},{8,10},{9,11},{10,... | collective-permute-start | bytes 1572872 | tf_op jit(solution)/shard_map/ppermute | solution.py:496
  3.1 1.2 %copy-start.2 = (f32[256,1024]{1,0:T(8,128)S(1)}, f32[256,1024]{1,0:T(8,128)}, u32[]{:S(2)}) copy-start(f32[256,1024]{1,0:T(8,128)} %filter_ref.1) | copy-start | bytes 3145732
  4.7 1.0 %copy-start = (bf16[256,1024]{1,0:T(8,128)(2,1)S(1)}, bf16[256,1024]{1,0:T(8,128)(2,1)}, u32[]{:S(2)}) copy-start(bf16[256,1024]{1,0:T(8,128)(2,1)} %own_hbm.2) | copy-start | bytes 1572868
  16.1 1.9 %collective-permute-start.2 = (bf16[256,1024]{1,0:T(8,128)(2,1)S(1)}, bf16[256,1024]{1,0:T(8,128)(2,1)S(1)}, u32[]{:S(2)}, u32[]{:S(2)}) collective-permute-start(bf16[256,1024]{1,0:T(8,128)(2,1)S(1)} %collective-permute-done.refs_0_.far_hbm), channel_id=1, source_target_pairs={{0,1},{1,0},{2,3},{3,2},{4,5},{5,4},{6,7},{7,6},{8,9},{9,8},{10,11... | collective-permute-start | bytes 1572872 | tf_op jit(solution)/shard_map/ppermute | solution.py:496
  20.6 9.8 %copy-start.1 = (bf16[256,1024]{1,0:T(8,128)(2,1)S(1)}, bf16[256,1024]{1,0:T(8,128)(2,1)}, u32[]{:S(2)}) copy-start(bf16[256,1024]{1,0:T(8,128)(2,1)} %own_hbm.2) | copy-start | bytes 1572868
  20.7 34.2 %all-to-all-start = ((bf16[32,96,256]{2,1,0:T(8,128)(2,1)}), bf16[32,96,256]{2,1,0:T(8,128)(2,1)}, u32[]{:S(2)}, u32[]{:S(2)}) async-start(bf16[32,96,256]{2,1,0:T(8,128)(2,1)} %last_values.1), calls=%async_computation | async-start | bytes 3145728 | tf_op jit(solution)/shard_map/all_to_all | solution.py:505
  30.5 20.4 %copy-start.3 = (f32[3,2,1024]{2,1,0:T(2,128)S(1)}, f32[3,2,1024]{2,1,0:T(2,128)}, u32[]{:S(2)}) copy-start(f32[3,2,1024]{2,1,0:T(2,128)} %taps_ref.3) | copy-start | bytes 73732
  38.4 16.4 %copy-start.4 = (f32[1024]{0:T(1024)S(1)}, f32[1024]{0:T(1024)}, u32[]{:S(2)}) copy-start(f32[1024]{0:T(1024)} %param.15) | copy-start | bytes 12292
  38.4 16.4 %copy-start.5 = (bf16[256,512]{1,0:T(8,128)(2,1)S(1)}, bf16[256,512]{1,0:T(8,128)(2,1)}, u32[]{:S(2)}) copy-start(bf16[256,512]{1,0:T(8,128)(2,1)} %constant.21.backward_ref) | copy-start | bytes 786436
  38.5 16.4 %copy-start.6 = (bf16[2,256,256]{2,1,0:T(8,128)(2,1)S(1)}, bf16[2,256,256]{2,1,0:T(8,128)(2,1)}, u32[]{:S(2)}) copy-start(bf16[2,256,256]{2,1,0:T(8,128)(2,1)} %constant.20.inner_back_ref) | copy-start | bytes 786436
  38.5 16.4 %copy-start.7 = (bf16[2,256,256]{2,1,0:T(8,128)(2,1)S(1)}, bf16[2,256,256]{2,1,0:T(8,128)(2,1)}, u32[]{:S(2)}) copy-start(bf16[2,256,256]{2,1,0:T(8,128)(2,1)} %constant.19.inner_ref) | copy-start | bytes 786436
  38.5 16.4 %copy-start.8 = (bf16[512,256]{1,0:T(8,128)(2,1)S(1)}, bf16[512,256]{1,0:T(8,128)(2,1)}, u32[]{:S(2)}) copy-start(bf16[512,256]{1,0:T(8,128)(2,1)} %constant.18.forward_ref) | copy-start | bytes 786436
  38.5 16.4 %copy-start.9 = (f32[32,1,256]{2,1,0:T(1,128)S(1)}, f32[32,1,256]{2,1,0:T(1,128)}, u32[]{:S(2)}) copy-start(f32[32,1,256]{2,1,0:T(1,128)} %constant.15.clone.sin_ref) | copy-start | bytes 98308
  38.5 16.4 %copy-start.10 = (f32[32,1,256]{2,1,0:T(1,128)S(1)}, f32[32,1,256]{2,1,0:T(1,128)}, u32[]{:S(2)}) copy-start(f32[32,1,256]{2,1,0:T(1,128)} %constant.14.clone.cos_ref) | copy-start | bytes 98308
  38.5 12.3 %collective-permute-start.4 = (bf16[16,1024]{1,0:T(8,128)(2,1)S(1)}, bf16[16,1024]{1,0:T(8,128)(2,1)S(1)}, u32[]{:S(2)}, u32[]{:S(2)}) collective-permute-start(bf16[16,1024]{1,0:T(8,128)(2,1)S(1)} %get-tuple-element.33), channel_id=1, source_target_pairs={{4,0},{8,4},{12,8},{16,12},{20,16},{24,20},{28,24},{32,28},{36,32}... | collective-permute-start | bytes 98312 | tf_op jit(solution)/shard_map/ppermute | solution.py:502
  40.0 10.9 %collective-permute-start.3 = (bf16[16,1024]{1,0:T(8,128)(2,1)S(1)}, bf16[16,1024]{1,0:T(8,128)(2,1)S(1)}, u32[]{:S(2)}, u32[]{:S(2)}) collective-permute-start(bf16[16,1024]{1,0:T(8,128)(2,1)S(1)} %get-tuple-element.34), channel_id=1, source_target_pairs={{0,4},{4,8},{8,12},{12,16},{16,20},{20,24},{24,28},{28,32},{32,36}... | collective-permute-start | bytes 98312 | tf_op jit(solution)/shard_map/ppermute | solution.py:499

commit v6 on v5

--- a/solution.py
+++ b/solution.py
@@ -356,9 +356,10 @@
 
 def add_values_kernel(last, part_ref, total_ref, flat_ref, *refs):
     if last:
-        filter_hbm, out_ref, left_ref, filter_sem = refs
+        filter_hbm, out_hbm, left_ref, filter_sem, out_ref, out_sems = refs
         slice_width = filter_hbm.shape[1]
-        filter_copy = pltpu.make_async_copy(filter_hbm, out_ref.at[:, 2 * slice_width :], filter_sem)
+        filter_copy = pltpu.make_async_copy(filter_hbm, out_hbm.at[:, 2 * slice_width :], filter_sem)
+        out_copies = []
     else:
         out_ref, left_ref = refs
     rows, depth = left_ref.shape
@@ -380,9 +381,16 @@
                     out_ref[b * per + d, strand * slice_width : (strand + 1) * slice_width] = turned[
                         d * slice_width : (d + 1) * slice_width
                     ]
+                where = (slice(b * per, (b + 1) * per), slice(strand * slice_width, (strand + 1) * slice_width))
+                out_copies.append(
+                    pltpu.make_async_copy(out_ref.at[where], out_hbm.at[where], out_sems.at[len(out_copies)])
+                )
+                out_copies[-1].start()
             else:
                 out_ref[here, cols] = total
     if last:
+        for copy in out_copies:
+            copy.wait()
         filter_copy.wait()
 
 
@@ -394,9 +402,16 @@
     last = filter_rows is not None
     extra = (filter_rows,) if last else ()
     if last:
-        out_shape = jax.ShapeDtypeStruct((filter_rows.shape[0], 3 * filter_rows.shape[1], rows), BF16)
+        ctx_count, slice_width, _ = filter_rows.shape
+        out_shape = jax.ShapeDtypeStruct((ctx_count, 3 * slice_width, rows), BF16)
+        staging = [
+            pltpu.SemaphoreType.DMA,
+            pltpu.VMEM((ctx_count, 2 * slice_width, rows), BF16),
+            pltpu.SemaphoreType.DMA((2 * width // min(256, width),)),
+        ]
     else:
         out_shape = jax.ShapeDtypeStruct(total.shape, F32)
+        staging = []
 
     def kernel(*refs):
         add_values_kernel(last, *refs)
@@ -404,8 +419,8 @@
     return pl.pallas_call(
         kernel,
         in_specs=[vmem] * 3 + [any_space] * len(extra),
-        out_specs=vmem,
-        scratch_shapes=[pltpu.VMEM((rows, depth), BF16)] + [pltpu.SemaphoreType.DMA] * len(extra),
+        out_specs=any_space if last else vmem,
+        scratch_shapes=[pltpu.VMEM((rows, depth), BF16)] + staging,
         out_shape=out_shape,
         compiler_params=params(END_BYTES),
         cost_estimate=cost(4 * rows * depth * width, 4 * depth * width),

time: 85.3 us -> 84.9 us (level)
  no operation moved by 1% of the time
where the time goes in v6:
time: 84.9 us; the launch traced here: 84.5 us
  Pallas kernels  30 us (35%)
  blocking collectives  21.8 us (26%)
  starting transfers between devices  18.9 us (22%)
  waiting for transfers between devices  11.3 us (13%)
  local copies, waits for them, and re-layouts  2.33 us (3%)
    all_to_all x1, blocking collectives, exchange(): return lax.all_to_all(x, 'ctx', split_axis=0, concat_axis=0, tiled=True)  21.8 us
    all_to_all x1, starting transfers between devices, exchange(): return lax.all_to_all(x, 'ctx', split_axis=0, concat_axis=0, tiled=True)  9.78 us
    pallas_call x1, Pallas kernels, start_values(): pl.pallas_call(start_values_kernel, in_specs=[any_space] * 3, out_specs=[...  8.49 us
    pallas_call x1, Pallas kernels, project_gates(): pl.pallas_call(project_gates_kernel, in_specs=[pl.BlockSpec(memory_space=...  7.95 us
    pallas_call x1, Pallas kernels, convolve(): pl.pallas_call(convolve_kernel, in_specs=[vmem] * 8 + [pl.BlockSpec(memor...  6.43 us
    ppermute x1, waiting for transfers between devices, to_previous(): return lax.ppermute(x, 'ctx', [(i + 1, i) for i in range(ctx_count - 1)])  6.33 us
    ppermute x1, starting transfers between devices, to_next(): return lax.ppermute(x, 'ctx', [(i, i + 1) for i in range(ctx_count - 1)])  4.55 us
    pallas_call x2, Pallas kernels, add_values(): pl.pallas_call(kernel, in_specs=[vmem] * 3 + [any_space] * len(extra), ou...  3.67 us
  transfers between devices with their start and end apart: 6, of which 4 were waited for; matrix products, arithmetic and copies ran while one was open for 0% of the time, Pallas kernels for 23%

profile of v6, /device:TPU:0, one launch (start us, length us, event | category | flops | bytes accessed | tf_op | source)
XLA Modules:
  0.0 84.5 jit_solution(8188260666092804141)
XLA Ops:
  0.0 0.0 collective-permute-start.1
  0.0 3.1 %collective-permute-start = (bf16[256,1024]{1,0:T(8,128)(2,1)}, bf16[256,1024]{1,0:T(8,128)(2,1)S(1)}, u32[]{:S(2)}, u32[]{:S(2)}) collective-permute-start(bf16[256,1024]{1,0:T(8,128)(2,1)} %own_hbm.2), channel_id=1, source_target_pairs={{0,2},{1,3},{2,0},{3,1},{4,6},{5,7},{6,4},{7,5},{8,10},{9,11},{10,... | collective-permute-start | bytes 1572872 | tf_op jit(solution)/shard_map/ppermute | solution.py:511
  3.1 1.2 %copy-done.2 = f32[256,1024]{1,0:T(8,128)S(1)} copy-done((f32[256,1024]{1,0:T(8,128)S(1)}, f32[256,1024]{1,0:T(8,128)}, u32[]{:S(2)}) %copy-start.2) | copy-done | bytes 1048600
  4.3 0.4 filter_prep.1
  4.7 0.0 collective-permute-done.1.sib_hbm
  4.7 0.0 copy-start
  4.8 1.0 %copy-done = bf16[256,1024]{1,0:T(8,128)(2,1)S(1)} copy-done((bf16[256,1024]{1,0:T(8,128)(2,1)S(1)}, bf16[256,1024]{1,0:T(8,128)(2,1)}, u32[]{:S(2)}) %copy-start) | copy-done | bytes 524312
  5.8 8.5 %start_values.1 = (f32[512,1024]{1,0:T(8,128)S(1)}, bf16[2,1024,1024]{2,1,0:T(8,128)(2,1)S(1)}, bf16[2,1024,1024]{2,1,0:T(8,128)(2,1)S(1)}) custom-call(bf16[256,1024]{1,0:T(8,128)(2,1)S(1)} %copy-done, bf16[256,1024]{1,0:T(8,128)(2,1)S(1)} %collective-permute-done.1.sib_hbm, bf16[65536,128]{1,0:T(8,128)(2,1)} %bitcast.9), custom_call_target="tpu_custom_call" | custom-call | flops 2147483648 | bytes 25165824 | tf_op jit(solution)/shard_map/start_values/pallas_call | solution.py:334
  14.3 1.8 %collective-permute-done.refs_0_.far_hbm = bf16[256,1024]{1,0:T(8,128)(2,1)S(1)} collective-permute-done((bf16[256,1024]{1,0:T(8,128)(2,1)}, bf16[256,1024]{1,0:T(8,128)(2,1)S(1)}, u32[]{:S(2)}, u32[]{:S(2)}) %collective-permute-start) | collective-permute-done | bytes 524320 | tf_op jit(solution)/shard_map/ppermute | solution.py:511
  16.1 0.0 collective-permute-start.2
  16.1 1.4 %far_values.1.refs_1_ = f32[512,1024]{1,0:T(8,128)S(1)} custom-call(bf16[256,1024]{1,0:T(8,128)(2,1)S(1)} %collective-permute-done.refs_0_.far_hbm, f32[512,1024]{1,0:T(8,128)S(1)} %get-tuple-element.23.refs_1_, bf16[2,1024,1024]{2,1,0:T(8,128)(2,1)S(1)} %get-tuple-element.24.refs_2_), custom_call_target="tpu_custom_call" | custom-call | flops 1073741824 | bytes 4194304 | tf_op jit(solution)/shard_map/far_values/pallas_call | solution.py:419
  17.5 0.5 collective-permute-done.2.refs_0_.farsib_hbm
  18.0 2.3 %last_values.1 = bf16[32,96,256]{2,1,0:T(8,128)(2,1)} custom-call(bf16[256,1024]{1,0:T(8,128)(2,1)S(1)} %collective-permute-done.2.refs_0_.farsib_hbm, f32[512,1024]{1,0:T(8,128)S(1)} %far_values.1.refs_1_, bf16[2,1024,1024]{2,1,0:T(8,128)(2,1)S(1)} %get-tuple-element.25.refs_2_, bf16[32,32,256]{2,1,0:T(8,128)(2,1)S(1)} %bitcast.7), custom_call_target="tpu_custom_call" | custom-call | flops 1073741824 | bytes 4194304 | tf_op jit(solution)/shard_map/last_values/pallas_call | solution.py:419
  20.3 0.0 copy-start.1
  20.3 9.8 %all-to-all-start = ((bf16[32,96,256]{2,1,0:T(8,128)(2,1)}), bf16[32,96,256]{2,1,0:T(8,128)(2,1)}, u32[]{:S(2)}, u32[]{:S(2)}) async-start(bf16[32,96,256]{2,1,0:T(8,128)(2,1)} %last_values.1), calls=%async_computation | async-start | bytes 3145728 | tf_op jit(solution)/shard_map/all_to_all | solution.py:520
  30.1 0.0 copy-start.3
  30.1 7.9 %project_gates.1.gates_ref = bf16[512,1024]{1,0:T(8,128)(2,1)S(1)} custom-call(bf16[256,1024]{1,0:T(8,128)(2,1)S(1)} %copy-done.1, bf16[256,1024]{1,0:T(8,128)(2,1)S(1)} %collective-permute-done.1.sib_hbm, bf16[256,1024]{1,0:T(8,128)(2,1)S(1)} %collective-permute-done.refs_0_.far_hbm, bf16[256,1024]{1,0:T(8,128)(2,1)S(1)} %collective-permute-done.2.refs_0_.farsib_hbm, ...), custom_call_target="tpu_custom_call" | custom-call | flops 4294967296 | bytes 16777216 | tf_op jit(solution)/shard_map/project_gates/pallas_call | solution.py:270
  38.0 0.0 copy-start.4
  38.0 0.0 copy-start.5
  38.1 0.0 copy-start.6
  38.1 0.0 copy-start.7
  38.1 0.0 copy-start.8
  38.1 0.0 copy-start.9
  38.1 0.0 copy-start.10
  38.1 1.4 %collective-permute-start.4 = (bf16[16,1024]{1,0:T(8,128)(2,1)S(1)}, bf16[16,1024]{1,0:T(8,128)(2,1)S(1)}, u32[]{:S(2)}, u32[]{:S(2)}) collective-permute-start(bf16[16,1024]{1,0:T(8,128)(2,1)S(1)} %get-tuple-element.33), channel_id=1, source_target_pairs={{4,0},{8,4},{12,8},{16,12},{20,16},{24,20},{28,24},{32,28},{36,32}... | collective-permute-start | bytes 98312 | tf_op jit(solution)/shard_map/ppermute | solution.py:517
  39.6 4.5 %collective-permute-start.3 = (bf16[16,1024]{1,0:T(8,128)(2,1)S(1)}, bf16[16,1024]{1,0:T(8,128)(2,1)S(1)}, u32[]{:S(2)}, u32[]{:S(2)}) collective-permute-start(bf16[16,1024]{1,0:T(8,128)(2,1)S(1)} %get-tuple-element.34), channel_id=1, source_target_pairs={{0,4},{4,8},{8,12},{12,16},{16,20},{20,24},{24,28},{28,32},{32,36}... | collective-permute-start | bytes 98312 | tf_op jit(solution)/shard_map/ppermute | solution.py:514
  44.1 6.3 %collective-permute-done.4.above_ref = bf16[16,1024]{1,0:T(8,128)(2,1)S(1)} collective-permute-done((bf16[16,1024]{1,0:T(8,128)(2,1)S(1)}, bf16[16,1024]{1,0:T(8,128)(2,1)S(1)}, u32[]{:S(2)}, u32[]{:S(2)}) %collective-permute-start.4) | collective-permute-done | bytes 32800 | tf_op jit(solution)/shard_map/ppermute | solution.py:517
  50.5 1.3 %gate_mix.1.gates_ref = f32[2,1024,256]{2,1,0:T(8,128)S(1)} custom-call(bf16[512,1024]{1,0:T(8,128)(2,1)S(1)} %project_gates.1.gates_ref, bf16[16,1024]{1,0:T(8,128)(2,1)S(1)} %collective-permute-done.3.below_ref, bf16[16,1024]{1,0:T(8,128)(2,1)S(1)} %collective-permute-done.4.above_ref, f32[3,2,1024]{2,1,0:T(2,128)S(1)} %copy-done.3), custom_call_target="tpu_custom_call" | custom-call | flops 4194304 | bytes 3145728 | tf_op jit(solution)/shard_map/gate_mix/pallas_call | solution.py:457
  51.8 2.7 %all-to-all-done.x_hbm = bf16[32,96,256]{2,1,0:T(8,128)(2,1)} async-done(((bf16[32,96,256]{2,1,0:T(8,128)(2,1)}), bf16[32,96,256]{2,1,0:T(8,128)(2,1)}, u32[]{:S(2)}, u32[]{:S(2)}) %all-to-all-start) | async-done | bytes 1572896 | tf_op jit(solution)/shard_map/all_to_all | solution.py:520
  54.5 6.4 %convolve.1 = bf16[32,64,256]{2,1,0:T(8,128)(2,1)S(1)} custom-call(f32[3,2,1024]{2,1,0:T(2,128)S(1)} %copy-done.3, f32[1,1024]{1,0:T(1,128)S(1)} %bitcast.8, bf16[512,256]{1,0:T(8,128)(2,1)S(1)} %copy-done.8, f32[32,1,256]{2,1,0:T(1,128)S(1)} %copy-done.10, f32[32,1,256]{2,1,0:T(1,128)S(1)} %copy-done.9, bf16[2,256,256]{2,1,0:T(8,128)(2,1)S(1)} %copy-done.7, ...), custom_call_target="tpu_custom_call" | custom-call | flops 5000000000 | bytes 4194304 | tf_op jit(solution)/shard_map/convolve/pallas_call | solution.py:181
  60.9 21.8 %all_to_all.10.conv_ref = bf16[32,64,256]{2,1,0:T(8,128)(2,1)S(1)} all-to-all(bf16[32,64,256]{2,1,0:T(8,128)(2,1)S(1)} %convolve.1), channel_id=1, replica_groups=mesh['ctx'=32,'tp'=4] {'ctx'}, dimensions={0} | all-to-all | bytes 2097152 | tf_op jit(solution)/shard_map/all_to_all | solution.py:520
  82.7 1.8 %finish.1 = bf16[256,1024]{1,0:T(8,128)(2,1)} custom-call(f32[2,1024,256]{2,1,0:T(8,128)S(1)} %gate_mix.1.gates_ref, bf16[32,64,256]{2,1,0:T(8,128)(2,1)S(1)} %all_to_all.10.conv_ref), custom_call_target="tpu_custom_call" | custom-call | flops 1048576 | bytes 3670016 | tf_op jit(solution)/shard_map/finish/pallas_call | solution.py:486
  (12 shorter events, 0.0 us)
Async XLA Ops:
  0.0 4.7 %collective-permute-start.1 = (bf16[256,1024]{1,0:T(8,128)(2,1)}, bf16[256,1024]{1,0:T(8,128)(2,1)S(1)}, u32[]{:S(2)}, u32[]{:S(2)}) collective-permute-start(bf16[256,1024]{1,0:T(8,128)(2,1)} %own_hbm.2), channel_id=1, source_target_pairs={{0,1},{1,0},{2,3},{3,2},{4,5},{5,4},{6,7},{7,6},{8,9},{9,8},{10,11... | collective-permute-start | bytes 1572872 | tf_op jit(solution)/shard_map/ppermute | solution.py:511
  0.0 16.1 %collective-permute-start = (bf16[256,1024]{1,0:T(8,128)(2,1)}, bf16[256,1024]{1,0:T(8,128)(2,1)S(1)}, u32[]{:S(2)}, u32[]{:S(2)}) collective-permute-start(bf16[256,1024]{1,0:T(8,128)(2,1)} %own_hbm.2), channel_id=1, source_target_pairs={{0,2},{1,3},{2,0},{3,1},{4,6},{5,7},{6,4},{7,5},{8,10},{9,11},{10,... | collective-permute-start | bytes 1572872 | tf_op jit(solution)/shard_map/ppermute | solution.py:511
  3.1 1.2 %copy-start.2 = (f32[256,1024]{1,0:T(8,128)S(1)}, f32[256,1024]{1,0:T(8,128)}, u32[]{:S(2)}) copy-start(f32[256,1024]{1,0:T(8,128)} %filter_ref.1) | copy-start | bytes 3145732
  4.7 1.0 %copy-start = (bf16[256,1024]{1,0:T(8,128)(2,1)S(1)}, bf16[256,1024]{1,0:T(8,128)(2,1)}, u32[]{:S(2)}) copy-start(bf16[256,1024]{1,0:T(8,128)(2,1)} %own_hbm.2) | copy-start | bytes 1572868
  16.1 1.9 %collective-permute-start.2 = (bf16[256,1024]{1,0:T(8,128)(2,1)S(1)}, bf16[256,1024]{1,0:T(8,128)(2,1)S(1)}, u32[]{:S(2)}, u32[]{:S(2)}) collective-permute-start(bf16[256,1024]{1,0:T(8,128)(2,1)S(1)} %collective-permute-done.refs_0_.far_hbm), channel_id=1, source_target_pairs={{0,1},{1,0},{2,3},{3,2},{4,5},{5,4},{6,7},{7,6},{8,9},{9,8},{10,11... | collective-permute-start | bytes 1572872 | tf_op jit(solution)/shard_map/ppermute | solution.py:511
  20.3 9.8 %copy-start.1 = (bf16[256,1024]{1,0:T(8,128)(2,1)S(1)}, bf16[256,1024]{1,0:T(8,128)(2,1)}, u32[]{:S(2)}) copy-start(bf16[256,1024]{1,0:T(8,128)(2,1)} %own_hbm.2) | copy-start | bytes 1572868
  20.3 34.2 %all-to-all-start = ((bf16[32,96,256]{2,1,0:T(8,128)(2,1)}), bf16[32,96,256]{2,1,0:T(8,128)(2,1)}, u32[]{:S(2)}, u32[]{:S(2)}) async-start(bf16[32,96,256]{2,1,0:T(8,128)(2,1)} %last_values.1), calls=%async_computation | async-start | bytes 3145728 | tf_op jit(solution)/shard_map/all_to_all | solution.py:520
  30.1 20.4 %copy-start.3 = (f32[3,2,1024]{2,1,0:T(2,128)S(1)}, f32[3,2,1024]{2,1,0:T(2,128)}, u32[]{:S(2)}) copy-start(f32[3,2,1024]{2,1,0:T(2,128)} %taps_ref.3) | copy-start | bytes 73732
  38.0 16.4 %copy-start.4 = (f32[1024]{0:T(1024)S(1)}, f32[1024]{0:T(1024)}, u32[]{:S(2)}) copy-start(f32[1024]{0:T(1024)} %param.15) | copy-start | bytes 12292
  38.0 16.4 %copy-start.5 = (bf16[256,512]{1,0:T(8,128)(2,1)S(1)}, bf16[256,512]{1,0:T(8,128)(2,1)}, u32[]{:S(2)}) copy-start(bf16[256,512]{1,0:T(8,128)(2,1)} %constant.21.backward_ref) | copy-start | bytes 786436
  38.1 16.4 %copy-start.6 = (bf16[2,256,256]{2,1,0:T(8,128)(2,1)S(1)}, bf16[2,256,256]{2,1,0:T(8,128)(2,1)}, u32[]{:S(2)}) copy-start(bf16[2,256,256]{2,1,0:T(8,128)(2,1)} %constant.20.inner_back_ref) | copy-start | bytes 786436
  38.1 16.4 %copy-start.7 = (bf16[2,256,256]{2,1,0:T(8,128)(2,1)S(1)}, bf16[2,256,256]{2,1,0:T(8,128)(2,1)}, u32[]{:S(2)}) copy-start(bf16[2,256,256]{2,1,0:T(8,128)(2,1)} %constant.19.inner_ref) | copy-start | bytes 786436
  38.1 16.4 %copy-start.8 = (bf16[512,256]{1,0:T(8,128)(2,1)S(1)}, bf16[512,256]{1,0:T(8,128)(2,1)}, u32[]{:S(2)}) copy-start(bf16[512,256]{1,0:T(8,128)(2,1)} %constant.18.forward_ref) | copy-start | bytes 786436
  38.1 16.4 %copy-start.9 = (f32[32,1,256]{2,1,0:T(1,128)S(1)}, f32[32,1,256]{2,1,0:T(1,128)}, u32[]{:S(2)}) copy-start(f32[32,1,256]{2,1,0:T(1,128)} %constant.15.clone.sin_ref) | copy-start | bytes 98308
  38.1 16.4 %copy-start.10 = (f32[32,1,256]{2,1,0:T(1,128)S(1)}, f32[32,1,256]{2,1,0:T(1,128)}, u32[]{:S(2)}) copy-start(f32[32,1,256]{2,1,0:T(1,128)} %constant.14.clone.cos_ref) | copy-start | bytes 98308
  38.1 12.3 %collective-permute-start.4 = (bf16[16,1024]{1,0:T(8,128)(2,1)S(1)}, bf16[16,1024]{1,0:T(8,128)(2,1)S(1)}, u32[]{:S(2)}, u32[]{:S(2)}) collective-permute-start(bf16[16,1024]{1,0:T(8,128)(2,1)S(1)} %get-tuple-element.33), channel_id=1, source_target_pairs={{4,0},{8,4},{12,8},{16,12},{20,16},{24,20},{28,24},{32,28},{36,32}... | collective-permute-start | bytes 98312 | tf_op jit(solution)/shard_map/ppermute | solution.py:517
  39.6 10.9 %collective-permute-start.3 = (bf16[16,1024]{1,0:T(8,128)(2,1)S(1)}, bf16[16,1024]{1,0:T(8,128)(2,1)S(1)}, u32[]{:S(2)}, u32[]{:S(2)}) collective-permute-start(bf16[16,1024]{1,0:T(8,128)(2,1)S(1)} %get-tuple-element.34), channel_id=1, source_target_pairs={{0,4},{4,8},{8,12},{12,16},{16,20},{20,24},{24,28},{28,32},{32,36}... | collective-permute-start | bytes 98312 | tf_op jit(solution)/shard_map/ppermute | solution.py:514
